TPU v7x, 32 devices: a whole 2x2x4 slice. The times are simulated.
32 devices in a mesh: subj: 2 (over x), vox: 16 (over z, y, core).
Axes of the slice: x: 2, y: 2, z: 4, core: 2. Of those that a mesh axis runs over, the one named last changes fastest.
Arguments:
- data: bfloat16 [2, 450, 16384], P('subj', None, 'vox'), may hold values from -6 to 6
- maps: bfloat16 [2, 256, 16384], P('subj', None, 'vox'), may hold values from -0.046875 to 0.046875
Outputs:
- response: float32 [450, 256], replicated
- new_maps: bfloat16 [2, 256, 16384], P('subj', None, 'vox')
All inputs are finite; a program needn't handle non-finite values.
Results may differ from a plain program's by a relative error of at most 0.0043.
The roundings to bfloat16 on the way count: a program that leaves them out, or rounds other values in their place, can miss the bound.
Values sent between devices are 32-bit elements; how exact they have to be, the bound alone decides.
No kernel may reach another device: no remote copies, remote signals or barrier semaphores. Data moves between devices by JAX's collectives and lax.ppermute only.
A program may use at most 64 MiB of HBM per device.

v0:
```python
import jax
import jax.numpy as jnp
from jax import lax
from jax.sharding import PartitionSpec as P

NS_STEPS = 5


def whiten(gram):
    scale = jnp.sqrt(jnp.sum(gram * gram, axis=(1, 2)) + 1e-06)[:, None, None]
    present_estimate = gram / scale
    eye = jnp.broadcast_to(jnp.eye(gram.shape[1], dtype=jnp.float32), gram.shape)
    inverse = eye
    for step in range(NS_STEPS):
        middle = 1.5 * eye - 0.5 * jnp.einsum(
            "sij,sjk->sik", inverse, present_estimate, precision=lax.Precision.HIGHEST
        )
        present_estimate = jnp.einsum(
            "sij,sjk->sik", present_estimate, middle, precision=lax.Precision.HIGHEST
        )
        inverse = jnp.einsum("sij,sjk->sik", middle, inverse, precision=lax.Precision.HIGHEST)
    return inverse / jnp.sqrt(scale)


def shards(data, maps):
    participant_count = lax.axis_size("subj") * data.shape[0]
    present_estimate = maps
    running_partial = jnp.einsum(
        "gqf,gmf->qm", data, present_estimate, preferred_element_type=jnp.float32
    )
    share = lax.psum_scatter(running_partial, "vox", scatter_dimension=1, tiled=True)
    share = lax.psum(share, "subj")
    total = lax.all_gather(share, "vox", axis=1, tiled=True)
    response = total / participant_count
    common_signal = response.astype(jnp.bfloat16)
    projected_signal = jnp.einsum(
        "go,zgj->zoj", common_signal, data, preferred_element_type=jnp.float32
    )
    local_gram = jnp.einsum(
        "dtc,drc->dtr", projected_signal, projected_signal, precision=lax.Precision.HIGHEST
    )
    gram = lax.psum(local_gram, "vox")
    subject_factor = whiten(gram)
    present_estimate = jnp.einsum(
        "czm,cmj->czj", subject_factor, projected_signal, precision=lax.Precision.HIGHEST
    ).astype(jnp.bfloat16)
    return (response, present_estimate)


def solution(mesh):
    in_specs = (P("subj", None, "vox"), P("subj", None, "vox"))
    out_specs = (P(), P("subj", None, "vox"))
    return jax.shard_map(shards, mesh=mesh, in_specs=in_specs, out_specs=out_specs, check_vma=False)
```

profile of v0, /device:TPU:0, one launch (start us, length us, event | category | flops | bytes accessed | tf_op | source)
XLA Modules:
  0.0 204.3 jit_solution(10254550541701556656)
XLA Ops:
  7.2 0.0 copy-start
  7.2 0.0 reduce-scatter.2.cloned.1.call-start
  7.2 1.1 copy-done
  8.4 2.3 %fusion.8 = f32[450,256]{0,1:T(8,128)} fusion(bf16[1,450,1024]{2,1,0:T(8,128)(2,1)S(1)} %copy-done, bf16[1,256,1024]{2,1,0:T(8,128)(2,1)} %param.3), kind=kOutput, calls=%fused_computation.16 | convolution fusion | flops 235929600 | bytes 1906688 | tf_op jit(solution)/shard_map/gqf,gmf->qm/dot_general | solution.py:28
  10.7 0.0 reduce-scatter.2.cloned.1.call-update
  10.7 0.0 all-reduce.2.cloned.1.call-start
  10.7 59.9 %reduce-scatter.2.cloned.1.call-done = f32[450,16]{0,1:T(8,128)} async-done(((f32[450,256]{0,1:T(8,128)}), f32[450,16]{0,1:T(8,128)}) %reduce-scatter.2.cloned.1.call-update) | async-done | bytes 28816 | tf_op jit(solution)/shard_map/reduce_scatter | solution.py:31
  70.6 9.0 %psum.14 = f32[450,16]{0,1:T(8,128)S(1)} all-reduce(f32[450,16]{0,1:T(8,128)} %reduce-scatter.2.cloned.1.call-done), channel_id=1, replica_groups=mesh['subj'=2,'vox'=16] {'subj'}, use_global_device_ids=true, to_apply=%region_1.0 | all-reduce | flops 7200 | bytes 57600 | tf_op jit(solution)/shard_map/psum | solution.py:32
  79.6 20.8 %all_gather.3 = f32[450,256]{0,1:T(8,128)S(1)} all-gather(f32[450,16]{0,1:T(8,128)S(1)} %psum.14), channel_id=1, replica_groups=mesh['subj'=2,'vox'=16] {'vox'}, dimensions={1}, use_global_device_ids=true | all-gather | bytes 489600 | tf_op jit(solution)/shard_map/all_gather | solution.py:33
  100.5 0.4 fusion.6
  100.9 1.7 convolution_bitcast_fusion
  102.6 0.0 all-reduce.2.cloned.1.call-update
  102.7 1.0 copy.4
  103.7 84.2 %all-reduce.2.cloned.1.call-done = f32[1,256,256]{2,1,0:T(8,128)} async-done(((f32[1,256,256]{2,1,0:T(8,128)}), f32[1,256,256]{2,1,0:T(8,128)}) %all-reduce.2.cloned.1.call-update) | async-done | bytes 262160 | tf_op jit(solution)/shard_map/psum | solution.py:42
  187.9 0.0 copy-start.1
  187.9 1.7 multiply_reduce_fusion
  190.3 0.0 copy-done.1
  190.4 0.3 fusion.5
  190.7 0.3 fusion.15
  191.0 0.4 fusion.11
  191.3 0.4 fusion.4
  191.7 0.4 fusion.17
  192.1 0.4 fusion.16
  192.5 0.4 fusion.3
  192.9 0.4 fusion.19
  193.3 0.4 fusion.18
  193.7 0.4 fusion.2
  194.1 0.4 fusion.20
  194.4 0.4 fusion.21
  194.8 0.4 fusion.1
  195.2 0.4 convolution_divide_fusion
  195.6 1.8 fusion
  (1 shorter events, 0.0 us)
Async XLA Ops:
  7.2 1.2 copy-start
  7.2 63.5 %reduce-scatter.2.cloned.1.call-start = ((), (), s32[]{:S(2)}) async-start(), calls=%async_computation.1 | async-start | bytes 557056 | tf_op jit(solution)/shard_map/reduce_scatter | solution.py:31
  10.7 177.2 %all-reduce.2.cloned.1.call-start = ((), (), s32[]{:S(2)}) async-start(), calls=%async_computation.2 | async-start | bytes 524288 | tf_op jit(solution)/shard_map/psum | solution.py:42
  187.9 2.4 %copy-start.1 = (f32[1,256,256]{2,1,0:T(8,128)S(1)}, f32[1,256,256]{2,1,0:T(8,128)}, u32[]{:S(2)}) copy-start(f32[1,256,256]{2,1,0:T(8,128)} %all-reduce.2.cloned.1.call-done) | copy-start | bytes 786436
Sparse Core Ops, SparseCore 0:
  12.1 58.4 reduce-scatter.1
  102.8 85.0 all-reduce.1
where the time goes:
time: 205 us; the launch traced here: 204 us
  waiting for transfers between devices  144 us (70%)
  blocking collectives  29.8 us (15%)
  between operations  14.9 us (7%)
  matrix products  11.5 us (6%)
  local copies, waits for them, and re-layouts  2.1 us (1%)
    psum x1, waiting for transfers between devices, shards(): gram = lax.psum(local_gram, 'vox')  84.2 us
    reduce_scatter x1, waiting for transfers between devices, shards(): lax.psum_scatter(running_partial, 'vox', scatter_dimension=1, tiled=True)  59.9 us
    all_gather x1, blocking collectives, shards(): total = lax.all_gather(share, 'vox', axis=1, tiled=True)  20.8 us
    psum x1, blocking collectives, shards(): share = lax.psum(share, 'subj')  9 us
  transfers between devices with their start and end apart: 2, of which 2 were waited for; matrix products, arithmetic and copies ran while one was open for 0% of the time, Pallas kernels for 0%

commit v1 on v0

v1 whole, which is shorter than its diff:
```python
import functools

import jax
import jax.numpy as jnp
from jax import lax
from jax.experimental import pallas as pl
from jax.experimental.pallas import tpu as pltpu
from jax.sharding import PartitionSpec as P

NS_STEPS = 5
VMEM_LIMIT = 40 * 1024 * 1024
AXES = ("subj", "vox")
NT = (((1,), (1,)), ((), ()))


def dot(a, b):
    return jnp.dot(a, b, preferred_element_type=jnp.float32)


def dot_nt(a, b):
    return lax.dot_general(a, b, NT, preferred_element_type=jnp.float32)


def split(a):
    high = a.astype(jnp.bfloat16)
    return high, (a - high.astype(jnp.float32)).astype(jnp.bfloat16)


def dot3(a, b):
    (ah, al), (bh, bl) = split(a), split(b)
    return dot(ah, bh) + (dot(ah, bl) + dot(al, bh))


def grid_of(rows, cols):
    return (
        lax.broadcasted_iota(jnp.int32, (rows, cols), 0),
        lax.broadcasted_iota(jnp.int32, (rows, cols), 1),
    )


def partials_kernel(times, place_ref, data_ref, maps_ref, send_ref, keep_ref, padded):
    full, comps = padded.shape[0], maps_ref.shape[0]
    half, block = comps // 2, full // 2
    tail = times // 16 * 16
    padded[tail:, :] = jnp.zeros((full - tail, padded.shape[1]), padded.dtype)
    padded[0:times, :] = data_ref[...]
    core = place_ref[0]
    every = padded[...]
    for which, out_ref in ((1 - core, send_ref), (core, keep_ref)):
        start = pl.multiple_of(which * half, half)
        out_ref[0:half, :] = dot_nt(maps_ref[pl.ds(start, half), :], every)
        upper = dot_nt(padded[pl.ds(start, half), :], every)
        lower = dot_nt(padded[pl.ds(block + start, half), :], padded[block:, :])
        row, col = grid_of(half, block)
        row = row + start
        diagonal = jnp.sum(jnp.where(row == col, lower, 0.0), axis=1, keepdims=True)
        out_ref[half:, 0:block] = jnp.where(col >= row, upper[:, 0:block], lower)
        out_ref[half:, block:] = jnp.where(col == times - block, diagonal, upper[:, block:])


def finish_kernel(times, people, chunk, pieces, place_ref, data_ref, *refs):
    own, other = refs[:pieces], refs[pieces : 2 * pieces]
    response_ref, maps_ref, total, packed, padded, sem = refs[2 * pieces :]
    load = pltpu.make_async_copy(data_ref, padded, sem)
    load.start()
    comps, full = total.shape
    half, block = comps // 2, full // 2
    core, spot, side = place_ref[0], place_ref[1], place_ref[2]
    for which, parts in ((core, own), (1 - core, other)):
        for d in range(pieces):
            at = pl.multiple_of(which * half + (spot ^ d) * chunk, 8)
            total[pl.ds(at, chunk), :] = parts[d][0:chunk, :]
        for d in range(2):
            at = pl.multiple_of(which * half + (side ^ d) * (half // 2), 8)
            packed[pl.ds(at, half // 2), :] = parts[d][chunk:, :]
    response = total[...] / people
    response_ref[...] = response.T[0:times, :]
    signal = response.astype(jnp.bfloat16)
    first, second = signal[:, 0:block], signal[:, block:]
    row, col = grid_of(comps, block)
    corner = packed[:, 0:block]
    beside = packed[:, block:]
    last = jnp.sum(jnp.where(col == times - block, beside, 0.0), axis=1, keepdims=True)
    u11 = jnp.where(col > row, corner, jnp.where(col == row, 0.5 * corner, 0.0))
    u22 = jnp.where(col < row, corner, jnp.where(col == row, 0.5 * last, 0.0))
    u12 = jnp.where(col < times - block, beside, 0.0)

    def dot2(a, b):
        high, low = split(b)
        return dot(a, high) + dot(a, low)

    left = dot2(first, u11)
    right = dot2(first, u12) + dot2(second, u22)
    lh, ll = split(left)
    rh, rl = split(right)
    product = (dot_nt(lh, first) + dot_nt(ll, first)) + (dot_nt(rh, second) + dot_nt(rl, second))
    gram = product + product.T
    scale = jnp.sqrt(jnp.sum(gram * gram) + 1e-06)
    row, col = grid_of(comps, comps)
    identity = jnp.where(row == col, 1.5, 0.0)
    estimate = gram / scale
    inverse = identity - 0.5 * estimate
    estimate = dot3(estimate, inverse)
    for step in range(1, NS_STEPS):
        middle = identity - 0.5 * dot3(inverse, estimate)
        if step < NS_STEPS - 1:
            estimate = dot3(estimate, middle)
        inverse = dot3(middle, inverse)
    factor = inverse / jnp.sqrt(scale)
    fh, fl = split(factor)
    weights = dot(fh, signal) + dot(fl, signal)
    wh, wl = split(weights[:, 0:times])
    load.wait()
    data = padded[...]
    maps_ref[...] = (dot(wh, data) + dot(wl, data)).astype(jnp.bfloat16)


def exchange(value, subjects, voxels, subj_step, vox_step):
    pairs = [
        (s * voxels + v, (s ^ subj_step) * voxels + (v ^ vox_step))
        for s in range(subjects)
        for v in range(voxels)
    ]
    return lax.ppermute(value, AXES, pairs)


def shards(data, maps):
    subjects, voxels = lax.axis_size("subj"), lax.axis_size("vox")
    _, times, wide = data.shape
    comps = maps.shape[1]
    people = subjects * data.shape[0]
    full, half = 2 * comps, comps // 2
    spots = 2 * subjects
    chunk = half // spots
    swap = functools.partial(exchange, subjects=subjects, voxels=voxels)
    s, v = lax.axis_index("subj"), lax.axis_index("vox")
    core, side = v % 2, v // 2 % 2
    spot = s * 2 + side
    place = jnp.stack([core, spot, side]).astype(jnp.int32)
    smem = pl.BlockSpec(memory_space=pltpu.SMEM)
    vmem = pl.BlockSpec(memory_space=pltpu.VMEM)
    params = pltpu.CompilerParams(vmem_limit_bytes=VMEM_LIMIT)

    send, keep = pl.pallas_call(
        functools.partial(partials_kernel, times),
        out_shape=[jax.ShapeDtypeStruct((comps, full), jnp.float32)] * 2,
        in_specs=[smem, vmem, vmem],
        out_specs=[vmem, vmem],
        scratch_shapes=[pltpu.VMEM((full, wide), jnp.bfloat16)],
        compiler_params=params,
        name="partials",
    )(place, data[0], maps[0])
    halves = keep + swap(send, subj_step=0, vox_step=1)

    def of_response(at):
        return lax.dynamic_slice_in_dim(halves, at * chunk, chunk, 0)

    def of_both(spot_at, side_at):
        square = lax.dynamic_slice_in_dim(halves, half + side_at * (half // 2), half // 2, 0)
        return jnp.concatenate([of_response(spot_at), square], 0)

    def step_of(d):
        return dict(subj_step=d >> 1, vox_step=2 * (d & 1))

    got = [swap(of_both(spot ^ 1, side ^ 1), **step_of(1))]
    got += [swap(of_response(spot ^ d), **step_of(d)) for d in range(2, spots)]
    sums = of_both(spot, side) + got[0]
    sums = jnp.concatenate([sums[:chunk] + sum(got[1:]), sums[chunk:]], 0)
    step = 4
    while step < voxels:
        sums = sums + swap(sums, subj_step=0, vox_step=step)
        step *= 2
    own = [sums, swap(sums, **step_of(1))]
    own += [swap(sums[:chunk], **step_of(d)) for d in range(2, spots)]
    other = [swap(piece, subj_step=0, vox_step=1) for piece in own]

    response, new_maps = pl.pallas_call(
        functools.partial(finish_kernel, times, people, chunk, spots),
        out_shape=[
            jax.ShapeDtypeStruct((times, comps), jnp.float32),
            jax.ShapeDtypeStruct((comps, wide), jnp.bfloat16),
        ],
        in_specs=[smem, pl.BlockSpec(memory_space=pl.ANY)] + [vmem] * (2 * spots),
        out_specs=[vmem, vmem],
        scratch_shapes=[
            pltpu.VMEM((comps, full), jnp.float32),
            pltpu.VMEM((comps, full), jnp.float32),
            pltpu.VMEM((times, wide), jnp.bfloat16),
            pltpu.SemaphoreType.DMA,
        ],
        compiler_params=params,
        name="finish",
    )(place, data[0], *own, *other)
    return response, new_maps[None]


def solution(mesh):
    in_specs = (P("subj", None, "vox"), P("subj", None, "vox"))
    out_specs = (P(), P("subj", None, "vox"))
    return jax.shard_map(shards, mesh=mesh, in_specs=in_specs, out_specs=out_specs, check_vma=False)
```

time: 205 us -> 55.3 us (0.27)
  waiting for transfers between devices: 144 us -> 29.2 us
  blocking collectives: 29.8 us -> 0 us
  between operations: 14.9 us -> 0.77 us
  starting transfers between devices: 0.08 us -> 13.1 us
  matrix products: 11.5 us -> 0 us
  Pallas kernels: 0 us -> 9.35 us
    psum x1 -> x0, waiting for transfers between devices: 84.2 us -> none  [shards(): gram = lax.psum(local_gram, 'vox')]
    reduce_scatter x1 -> x0, waiting for transfers between devices: 59.9 us -> none  [shards(): lax.psum_scatter(running_partial, 'vox', scatter_dimension=1, tiled=True)]
    ppermute x0 -> x13, waiting for transfers between devices: none -> 29.2 us  [exchange(): return lax.ppermute(value, AXES, pairs)]
    all_gather x1 -> x0, blocking collectives: 20.8 us -> none  [shards(): total = lax.all_gather(share, 'vox', axis=1, tiled=True)]
    ppermute x0 -> x13, starting transfers between devices: none -> 13.1 us  [exchange(): return lax.ppermute(value, AXES, pairs)]
    dot_general x18 -> x0, matrix products: 11.5 us -> none  [the longest x1 2.31 us: shards(): jnp.einsum('gqf,gmf->qm', data, present_estimate, preferred_element_type=...]
    pallas_call x0 -> x2, Pallas kernels: none -> 9.35 us  [the longest x1 6.86 us: shards(): pl.pallas_call(functools.partial(finish_kernel, times, people, chunk, spo...]
    psum x1 -> x0, blocking collectives: 9 us -> none  [shards(): share = lax.psum(share, 'subj')]
  transfers between devices with their start and end apart: 2 -> 13, of which waited for: 2 -> 9; matrix products, arithmetic and copies ran while one was open for 0% -> 0% of each run, Pallas kernels for 0% -> 0%
where the time goes in v1:
time: 55.3 us; the launch traced here: 55.1 us
  waiting for transfers between devices  29.2 us (53%)
  starting transfers between devices  13.1 us (24%)
  Pallas kernels  9.35 us (17%)
  local copies, waits for them, and re-layouts  2.31 us (4%)
  between operations  0.77 us (1%)
    ppermute x13, waiting for transfers between devices, exchange(): return lax.ppermute(value, AXES, pairs)  29.2 us
    ppermute x13, starting transfers between devices, exchange(): return lax.ppermute(value, AXES, pairs)  13.1 us
    pallas_call x1, Pallas kernels, shards(): pl.pallas_call(functools.partial(finish_kernel, times, people, chunk, spo...  6.86 us
    pallas_call x1, Pallas kernels, shards(): pl.pallas_call(functools.partial(partials_kernel, times), out_shape=[jax....  2.49 us
    unnamed x6, local copies, waits for them, and re-layouts  2.23 us
  transfers between devices with their start and end apart: 13, of which 9 were waited for; matrix products, arithmetic and copies ran while one was open for 0% of the time, Pallas kernels for 0%

profile of v1, /device:TPU:0, one launch (start us, length us, event | category | flops | bytes accessed | tf_op | source)
XLA Modules:
  0.0 55.1 jit_solution(13411506538293292611)
XLA Ops:
  0.7 0.1 pad_add_fusion.place_ref
  0.7 1.2 %copy-done = bf16[1,450,1024]{2,1,0:T(8,128)(2,1)S(1)} copy-done((bf16[1,450,1024]{2,1,0:T(8,128)(2,1)S(1)}, bf16[1,450,1024]{2,1,0:T(8,128)(2,1)}, u32[]{:S(2)}) %copy-start) | copy-done | bytes 921624
  1.9 1.0 %copy-done.2 = bf16[1,256,1024]{2,1,0:T(8,128)(2,1)S(1)} copy-done((bf16[1,256,1024]{2,1,0:T(8,128)(2,1)S(1)}, bf16[1,256,1024]{2,1,0:T(8,128)(2,1)}, u32[]{:S(2)}) %copy-start.2) | copy-done | bytes 524312
  3.0 2.5 %partials.1 = (f32[256,512]{1,0:T(8,128)S(1)}, f32[256,512]{1,0:T(8,128)S(1)}) custom-call(s32[3]{0:T(128)S(1)} %pad_add_fusion.place_ref, bf16[450,1024]{1,0:T(8,128)(2,1)S(1)} %bitcast.6, bf16[256,1024]{1,0:T(8,128)(2,1)S(1)} %bitcast.8), custom_call_target="tpu_custom_call" | custom-call | tf_op jit(solution)/shard_map/partials/pallas_call | solution.py:144
  5.5 0.5 collective-permute-start
  6.0 1.5 %collective-permute-done = f32[256,512]{1,0:T(8,128)S(1)} collective-permute-done((f32[256,512]{1,0:T(8,128)S(1)}, f32[256,512]{1,0:T(8,128)S(1)}, u32[]{:S(2)}, u32[]{:S(2)}) %collective-permute-start) | collective-permute-done | bytes 524320 | tf_op jit(solution)/shard_map/ppermute | solution.py:124
  7.5 0.1 add.60
  7.7 3.0 %collective-permute-start.1 = (f32[96,512]{1,0:T(8,128)S(1)}, f32[96,512]{1,0:T(8,128)S(1)}, u32[]{:S(2)}, u32[]{:S(2)}) collective-permute-start(f32[96,512]{1,0:T(8,128)S(1)} %pad_maximum_fusion), channel_id=1, source_target_pairs={{0,2},{1,3},{2,0},{3,1},{4,6},{5,7},{6,4},{7,5},{8,10},{9,11},{10,... | collective-permute-start | bytes 589832 | tf_op jit(solution)/shard_map/ppermute | solution.py:124
  10.7 1.4 %collective-permute-start.3 = (f32[32,512]{1,0:T(8,128)S(1)}, f32[32,512]{1,0:T(8,128)S(1)}, u32[]{:S(2)}, u32[]{:S(2)}) collective-permute-start(f32[32,512]{1,0:T(8,128)S(1)} %get-tuple-element.10), channel_id=1, source_target_pairs={{0,18},{1,19},{2,16},{3,17},{4,22},{5,23},{6,20},{7,21},{8,26},{9,... | collective-permute-start | bytes 196616 | tf_op jit(solution)/shard_map/ppermute | solution.py:124
  12.1 0.1 collective-permute-start.2
  12.2 5.1 %collective-permute-done.1 = f32[96,512]{1,0:T(8,128)S(1)} collective-permute-done((f32[96,512]{1,0:T(8,128)S(1)}, f32[96,512]{1,0:T(8,128)S(1)}, u32[]{:S(2)}, u32[]{:S(2)}) %collective-permute-start.1) | collective-permute-done | bytes 196640 | tf_op jit(solution)/shard_map/ppermute | solution.py:124
  17.3 0.0 copy-start.1
  17.3 0.0 collective-permute-done.3
  17.3 0.0 collective-permute-done.2
  17.4 1.9 %collective-permute-start.4 = (f32[96,512]{1,0:T(8,128)S(1)}, f32[96,512]{1,0:T(8,128)S(1)}, u32[]{:S(2)}, u32[]{:S(2)}) collective-permute-start(f32[96,512]{1,0:T(8,128)S(1)} %pad_maximum_fusion.1), channel_id=1, source_target_pairs={{0,4},{1,5},{2,6},{3,7},{4,0},{5,1},{6,2},{7,3},{8,12},{9,13},{10,... | collective-permute-start | bytes 589832 | tf_op jit(solution)/shard_map/ppermute | solution.py:124
  19.3 4.6 %collective-permute-done.4 = f32[96,512]{1,0:T(8,128)S(1)} collective-permute-done((f32[96,512]{1,0:T(8,128)S(1)}, f32[96,512]{1,0:T(8,128)S(1)}, u32[]{:S(2)}, u32[]{:S(2)}) %collective-permute-start.4) | collective-permute-done | bytes 196640 | tf_op jit(solution)/shard_map/ppermute | solution.py:124
  23.9 2.6 %collective-permute-start.5 = (f32[96,512]{1,0:T(8,128)S(1)}, f32[96,512]{1,0:T(8,128)S(1)}, u32[]{:S(2)}, u32[]{:S(2)}) collective-permute-start(f32[96,512]{1,0:T(8,128)S(1)} %fusion), channel_id=1, source_target_pairs={{0,8},{1,9},{2,10},{3,11},{4,12},{5,13},{6,14},{7,15},{8,0},{9,1},... | collective-permute-start | bytes 589832 | tf_op jit(solution)/shard_map/ppermute | solution.py:124
  26.5 8.2 %collective-permute-done.5 = f32[96,512]{1,0:T(8,128)S(1)} collective-permute-done((f32[96,512]{1,0:T(8,128)S(1)}, f32[96,512]{1,0:T(8,128)S(1)}, u32[]{:S(2)}, u32[]{:S(2)}) %collective-permute-start.5) | collective-permute-done | bytes 196640 | tf_op jit(solution)/shard_map/ppermute | solution.py:124
  34.7 1.1 %collective-permute-start.6 = (f32[96,512]{1,0:T(8,128)S(1)}, f32[96,512]{1,0:T(8,128)S(1)}, u32[]{:S(2)}, u32[]{:S(2)}) collective-permute-start(f32[96,512]{1,0:T(8,128)S(1)} %add.73.refs_0_), channel_id=1, source_target_pairs={{0,2},{1,3},{2,0},{3,1},{4,6},{5,7},{6,4},{7,5},{8,10},{9,11},{10,... | collective-permute-start | bytes 589832 | tf_op jit(solution)/shard_map/ppermute | solution.py:124
  35.8 0.0 collective-permute-start.9
  35.8 5.1 %collective-permute-done.6.refs_1_ = f32[96,512]{1,0:T(8,128)S(1)} collective-permute-done((f32[96,512]{1,0:T(8,128)S(1)}, f32[96,512]{1,0:T(8,128)S(1)}, u32[]{:S(2)}, u32[]{:S(2)}) %collective-permute-start.6) | collective-permute-done | bytes 196640 | tf_op jit(solution)/shard_map/ppermute | solution.py:124
  40.9 0.0 collective-permute-start.10
  40.9 1.6 %collective-permute-start.8 = (f32[32,512]{1,0:T(8,128)S(1)}, f32[32,512]{1,0:T(8,128)S(1)}, u32[]{:S(2)}, u32[]{:S(2)}) collective-permute-start(f32[32,512]{1,0:T(8,128)S(1)} %slice.15), channel_id=1, source_target_pairs={{0,18},{1,19},{2,16},{3,17},{4,22},{5,23},{6,20},{7,21},{8,26},{9,... | collective-permute-start | bytes 196616 | tf_op jit(solution)/shard_map/ppermute | solution.py:124
  42.6 0.5 collective-permute-start.7
  43.1 3.7 %collective-permute-done.8.refs_3_ = f32[32,512]{1,0:T(8,128)S(1)} collective-permute-done((f32[32,512]{1,0:T(8,128)S(1)}, f32[32,512]{1,0:T(8,128)S(1)}, u32[]{:S(2)}, u32[]{:S(2)}) %collective-permute-start.8) | collective-permute-done | bytes 65568 | tf_op jit(solution)/shard_map/ppermute | solution.py:124
  46.8 0.0 collective-permute-start.12
  46.8 0.1 collective-permute-done.7.refs_2_
  46.9 0.4 collective-permute-start.11
  47.3 0.7 %collective-permute-done.12.refs_7_ = f32[32,512]{1,0:T(8,128)S(1)} collective-permute-done((f32[32,512]{1,0:T(8,128)S(1)}, f32[32,512]{1,0:T(8,128)S(1)}, u32[]{:S(2)}, u32[]{:S(2)}) %collective-permute-start.12) | collective-permute-done | bytes 65568 | tf_op jit(solution)/shard_map/ppermute | solution.py:124
  48.1 0.2 collective-permute-done.11.refs_6_
  48.2 0.0 collective-permute-done.9.refs_4_
  48.2 6.9 %finish.1 = (f32[450,256]{1,0:T(8,128)}, bf16[256,1024]{1,0:T(8,128)(2,1)}) custom-call(s32[3]{0:T(128)S(1)} %pad_add_fusion.place_ref, bf16[450,1024]{1,0:T(8,128)(2,1)S(1)} %bitcast.7, f32[96,512]{1,0:T(8,128)S(1)} %add.73.refs_0_, f32[96,512]{1,0:T(8,128)S(1)} %collective-permute-done.6.refs_1_, f32[32,512]{1,0:T(8,128)S(1)} %collective-permute-done.7.refs_2_, ...), custom_call_target="tpu_custom_call" | custom-call | tf_op jit(solution)/shard_map/finish/pallas_call | solution.py:177
  (14 shorter events, 0.2 us)
Async XLA Ops:
  0.7 1.2 %copy-start = (bf16[1,450,1024]{2,1,0:T(8,128)(2,1)S(1)}, bf16[1,450,1024]{2,1,0:T(8,128)(2,1)}, u32[]{:S(2)}) copy-start(bf16[1,450,1024]{2,1,0:T(8,128)(2,1)} %param.2) | copy-start | bytes 2764804
  1.9 1.0 %copy-start.2 = (bf16[1,256,1024]{2,1,0:T(8,128)(2,1)S(1)}, bf16[1,256,1024]{2,1,0:T(8,128)(2,1)}, u32[]{:S(2)}) copy-start(bf16[1,256,1024]{2,1,0:T(8,128)(2,1)} %param.3) | copy-start | bytes 1572868
  5.5 2.0 %collective-permute-start = (f32[256,512]{1,0:T(8,128)S(1)}, f32[256,512]{1,0:T(8,128)S(1)}, u32[]{:S(2)}, u32[]{:S(2)}) collective-permute-start(f32[256,512]{1,0:T(8,128)S(1)} %get-tuple-element.7), channel_id=1, source_target_pairs={{0,1},{1,0},{2,3},{3,2},{4,5},{5,4},{6,7},{7,6},{8,9},{9,8},{10,11... | collective-permute-start | bytes 1572872 | tf_op jit(solution)/shard_map/ppermute | solution.py:124
  7.7 9.6 %collective-permute-start.1 = (f32[96,512]{1,0:T(8,128)S(1)}, f32[96,512]{1,0:T(8,128)S(1)}, u32[]{:S(2)}, u32[]{:S(2)}) collective-permute-start(f32[96,512]{1,0:T(8,128)S(1)} %pad_maximum_fusion), channel_id=1, source_target_pairs={{0,2},{1,3},{2,0},{3,1},{4,6},{5,7},{6,4},{7,5},{8,10},{9,11},{10,... | collective-permute-start | bytes 589832 | tf_op jit(solution)/shard_map/ppermute | solution.py:124
  10.7 6.7 %collective-permute-start.3 = (f32[32,512]{1,0:T(8,128)S(1)}, f32[32,512]{1,0:T(8,128)S(1)}, u32[]{:S(2)}, u32[]{:S(2)}) collective-permute-start(f32[32,512]{1,0:T(8,128)S(1)} %get-tuple-element.10), channel_id=1, source_target_pairs={{0,18},{1,19},{2,16},{3,17},{4,22},{5,23},{6,20},{7,21},{8,26},{9,... | collective-permute-start | bytes 196616 | tf_op jit(solution)/shard_map/ppermute | solution.py:124
  12.1 5.3 %collective-permute-start.2 = (f32[32,512]{1,0:T(8,128)S(1)}, f32[32,512]{1,0:T(8,128)S(1)}, u32[]{:S(2)}, u32[]{:S(2)}) collective-permute-start(f32[32,512]{1,0:T(8,128)S(1)} %get-tuple-element.11), channel_id=1, source_target_pairs={{0,16},{1,17},{2,18},{3,19},{4,20},{5,21},{6,22},{7,23},{8,24},{9,... | collective-permute-start | bytes 196616 | tf_op jit(solution)/shard_map/ppermute | solution.py:124
  17.3 30.9 %copy-start.1 = (bf16[1,450,1024]{2,1,0:T(8,128)(2,1)S(1)}, bf16[1,450,1024]{2,1,0:T(8,128)(2,1)}, u32[]{:S(2)}) copy-start(bf16[1,450,1024]{2,1,0:T(8,128)(2,1)} %param.2) | copy-start | bytes 2764804
  17.4 6.5 %collective-permute-start.4 = (f32[96,512]{1,0:T(8,128)S(1)}, f32[96,512]{1,0:T(8,128)S(1)}, u32[]{:S(2)}, u32[]{:S(2)}) collective-permute-start(f32[96,512]{1,0:T(8,128)S(1)} %pad_maximum_fusion.1), channel_id=1, source_target_pairs={{0,4},{1,5},{2,6},{3,7},{4,0},{5,1},{6,2},{7,3},{8,12},{9,13},{10,... | collective-permute-start | bytes 589832 | tf_op jit(solution)/shard_map/ppermute | solution.py:124
  23.9 10.7 %collective-permute-start.5 = (f32[96,512]{1,0:T(8,128)S(1)}, f32[96,512]{1,0:T(8,128)S(1)}, u32[]{:S(2)}, u32[]{:S(2)}) collective-permute-start(f32[96,512]{1,0:T(8,128)S(1)} %fusion), channel_id=1, source_target_pairs={{0,8},{1,9},{2,10},{3,11},{4,12},{5,13},{6,14},{7,15},{8,0},{9,1},... | collective-permute-start | bytes 589832 | tf_op jit(solution)/shard_map/ppermute | solution.py:124
  34.7 6.3 %collective-permute-start.6 = (f32[96,512]{1,0:T(8,128)S(1)}, f32[96,512]{1,0:T(8,128)S(1)}, u32[]{:S(2)}, u32[]{:S(2)}) collective-permute-start(f32[96,512]{1,0:T(8,128)S(1)} %add.73.refs_0_), channel_id=1, source_target_pairs={{0,2},{1,3},{2,0},{3,1},{4,6},{5,7},{6,4},{7,5},{8,10},{9,11},{10,... | collective-permute-start | bytes 589832 | tf_op jit(solution)/shard_map/ppermute | solution.py:124
  35.8 12.4 %collective-permute-start.9 = (f32[96,512]{1,0:T(8,128)S(1)}, f32[96,512]{1,0:T(8,128)S(1)}, u32[]{:S(2)}, u32[]{:S(2)}) collective-permute-start(f32[96,512]{1,0:T(8,128)S(1)} %add.73.refs_0_), channel_id=1, source_target_pairs={{0,1},{1,0},{2,3},{3,2},{4,5},{5,4},{6,7},{7,6},{8,9},{9,8},{10,11... | collective-permute-start | bytes 589832 | tf_op jit(solution)/shard_map/ppermute | solution.py:124
  40.9 7.3 %collective-permute-start.10 = (f32[96,512]{1,0:T(8,128)S(1)}, f32[96,512]{1,0:T(8,128)S(1)}, u32[]{:S(2)}, u32[]{:S(2)}) collective-permute-start(f32[96,512]{1,0:T(8,128)S(1)} %collective-permute-done.6.refs_1_), channel_id=1, source_target_pairs={{0,1},{1,0},{2,3},{3,2},{4,5},{5,4},{6,7},{7,6},{8,9},{9,8},{10,11... | collective-permute-start | bytes 589832 | tf_op jit(solution)/shard_map/ppermute | solution.py:124
  40.9 5.9 %collective-permute-start.8 = (f32[32,512]{1,0:T(8,128)S(1)}, f32[32,512]{1,0:T(8,128)S(1)}, u32[]{:S(2)}, u32[]{:S(2)}) collective-permute-start(f32[32,512]{1,0:T(8,128)S(1)} %slice.15), channel_id=1, source_target_pairs={{0,18},{1,19},{2,16},{3,17},{4,22},{5,23},{6,20},{7,21},{8,26},{9,... | collective-permute-start | bytes 196616 | tf_op jit(solution)/shard_map/ppermute | solution.py:124
  42.6 4.4 %collective-permute-start.7 = (f32[32,512]{1,0:T(8,128)S(1)}, f32[32,512]{1,0:T(8,128)S(1)}, u32[]{:S(2)}, u32[]{:S(2)}) collective-permute-start(f32[32,512]{1,0:T(8,128)S(1)} %slice.15), channel_id=1, source_target_pairs={{0,16},{1,17},{2,18},{3,19},{4,20},{5,21},{6,22},{7,23},{8,24},{9,... | collective-permute-start | bytes 196616 | tf_op jit(solution)/shard_map/ppermute | solution.py:124
  46.8 1.3 %collective-permute-start.12 = (f32[32,512]{1,0:T(8,128)S(1)}, f32[32,512]{1,0:T(8,128)S(1)}, u32[]{:S(2)}, u32[]{:S(2)}) collective-permute-start(f32[32,512]{1,0:T(8,128)S(1)} %collective-permute-done.8.refs_3_), channel_id=1, source_target_pairs={{0,1},{1,0},{2,3},{3,2},{4,5},{5,4},{6,7},{7,6},{8,9},{9,8},{10,11... | collective-permute-start | bytes 196616 | tf_op jit(solution)/shard_map/ppermute | solution.py:124
  46.9 1.3 %collective-permute-start.11 = (f32[32,512]{1,0:T(8,128)S(1)}, f32[32,512]{1,0:T(8,128)S(1)}, u32[]{:S(2)}, u32[]{:S(2)}) collective-permute-start(f32[32,512]{1,0:T(8,128)S(1)} %collective-permute-done.7.refs_2_), channel_id=1, source_target_pairs={{0,1},{1,0},{2,3},{3,2},{4,5},{5,4},{6,7},{7,6},{8,9},{9,8},{10,11... | collective-permute-start | bytes 196616 | tf_op jit(solution)/shard_map/ppermute | solution.py:124

commit v2 on v1

--- a/solution.py
+++ b/solution.py
@@ -59,20 +59,22 @@
 
 
 def finish_kernel(times, people, chunk, pieces, place_ref, data_ref, *refs):
-    own, other = refs[:pieces], refs[pieces : 2 * pieces]
-    response_ref, maps_ref, total, packed, padded, sem = refs[2 * pieces :]
+    own, other = refs[: pieces + 2], refs[pieces + 2 : 2 * pieces + 4]
+    response_ref, maps_ref, total, packed, padded, sem = refs[2 * pieces + 4 :]
     load = pltpu.make_async_copy(data_ref, padded, sem)
     load.start()
     comps, full = total.shape
     half, block = comps // 2, full // 2
-    core, spot, side = place_ref[0], place_ref[1], place_ref[2]
+    quarter, eighth = half // 2, half // 4
+    core, spot, side, level = place_ref[0], place_ref[1], place_ref[2], place_ref[3]
     for which, parts in ((core, own), (1 - core, other)):
         for d in range(pieces):
             at = pl.multiple_of(which * half + (spot ^ d) * chunk, 8)
-            total[pl.ds(at, chunk), :] = parts[d][0:chunk, :]
-        for d in range(2):
-            at = pl.multiple_of(which * half + (side ^ d) * (half // 2), 8)
-            packed[pl.ds(at, half // 2), :] = parts[d][chunk:, :]
+            total[pl.ds(at, chunk), :] = parts[2 + d][...]
+        for d in range(4):
+            at = which * half + (side ^ (d >> 1)) * quarter + (level ^ (d & 1)) * eighth
+            piece = parts[d >> 1][(d & 1) * eighth : (d & 1) * eighth + eighth, :]
+            packed[pl.ds(pl.multiple_of(at, 8), eighth), :] = piece
     response = total[...] / people
     response_ref[...] = response.T[0:times, :]
     signal = response.astype(jnp.bfloat16)
@@ -135,8 +137,8 @@
     swap = functools.partial(exchange, subjects=subjects, voxels=voxels)
     s, v = lax.axis_index("subj"), lax.axis_index("vox")
     core, side = v % 2, v // 2 % 2
-    spot = s * 2 + side
-    place = jnp.stack([core, spot, side]).astype(jnp.int32)
+    spot, level = s * 2 + side, v // 4 % 2
+    place = jnp.stack([core, spot, side, level]).astype(jnp.int32)
     smem = pl.BlockSpec(memory_space=pltpu.SMEM)
     vmem = pl.BlockSpec(memory_space=pltpu.VMEM)
     params = pltpu.CompilerParams(vmem_limit_bytes=VMEM_LIMIT)
@@ -152,26 +154,27 @@
     )(place, data[0], maps[0])
     halves = keep + swap(send, subj_step=0, vox_step=1)
 
-    def of_response(at):
-        return lax.dynamic_slice_in_dim(halves, at * chunk, chunk, 0)
-
-    def of_both(spot_at, side_at):
-        square = lax.dynamic_slice_in_dim(halves, half + side_at * (half // 2), half // 2, 0)
-        return jnp.concatenate([of_response(spot_at), square], 0)
-
-    def step_of(d):
+    def rows(value, at, size):
+        return lax.dynamic_slice_in_dim(value, at * size, size, 0)
+
+    def spot_step(d):
         return dict(subj_step=d >> 1, vox_step=2 * (d & 1))
 
-    got = [swap(of_both(spot ^ 1, side ^ 1), **step_of(1))]
-    got += [swap(of_response(spot ^ d), **step_of(d)) for d in range(2, spots)]
-    sums = of_both(spot, side) + got[0]
-    sums = jnp.concatenate([sums[:chunk] + sum(got[1:]), sums[chunk:]], 0)
-    step = 4
+    sums, square = halves[:half], halves[half:]
+    got = [swap(rows(sums, spot ^ d, chunk), **spot_step(d)) for d in range(1, spots)]
+    sums = rows(sums, spot, chunk) + sum(got)
+    quarter, eighth = half // 2, half // 4
+    square = rows(square, side, quarter) + swap(rows(square, side ^ 1, quarter), subj_step=0, vox_step=2)
+    square = rows(square, level, eighth) + swap(rows(square, level ^ 1, eighth), subj_step=0, vox_step=4)
+    sums = sums + swap(sums, subj_step=0, vox_step=4)
+    step = 8
     while step < voxels:
+        square = square + swap(square, subj_step=0, vox_step=step)
         sums = sums + swap(sums, subj_step=0, vox_step=step)
         step *= 2
-    own = [sums, swap(sums, **step_of(1))]
-    own += [swap(sums[:chunk], **step_of(d)) for d in range(2, spots)]
+    square = jnp.concatenate([square, swap(square, subj_step=0, vox_step=4)], 0)
+    own = [square, swap(square, subj_step=0, vox_step=2), sums]
+    own += [swap(sums, **spot_step(d)) for d in range(1, spots)]
     other = [swap(piece, subj_step=0, vox_step=1) for piece in own]
 
     response, new_maps = pl.pallas_call(
@@ -180,7 +183,7 @@
             jax.ShapeDtypeStruct((times, comps), jnp.float32),
             jax.ShapeDtypeStruct((comps, wide), jnp.bfloat16),
         ],
-        in_specs=[smem, pl.BlockSpec(memory_space=pl.ANY)] + [vmem] * (2 * spots),
+        in_specs=[smem, pl.BlockSpec(memory_space=pl.ANY)] + [vmem] * (2 * spots + 4),
         out_specs=[vmem, vmem],
         scratch_shapes=[
             pltpu.VMEM((comps, full), jnp.float32),

time: 55.3 us -> 49.4 us (0.89)
  waiting for transfers between devices: 29.2 us -> 16.2 us
  starting transfers between devices: 13.1 us -> 20.3 us
    ppermute x13 -> x20, waiting for transfers between devices: 29.2 us -> 16.2 us  [exchange(): return lax.ppermute(value, AXES, pairs)]
    ppermute x13 -> x20, starting transfers between devices: 13.1 us -> 20.3 us  [exchange(): return lax.ppermute(value, AXES, pairs)]
  transfers between devices with their start and end apart: 13 -> 20, of which waited for: 9 -> 12; matrix products, arithmetic and copies ran while one was open for 0% -> 0% of each run, Pallas kernels for 0% -> 0%
where the time goes in v2:
time: 49.4 us; the launch traced here: 49.2 us
  starting transfers between devices  20.3 us (41%)
  waiting for transfers between devices  16.2 us (33%)
  Pallas kernels  9.35 us (19%)
  local copies, waits for them, and re-layouts  2.32 us (5%)
  between operations  0.79 us (2%)
    ppermute x20, starting transfers between devices, exchange(): return lax.ppermute(value, AXES, pairs)  20.3 us
    ppermute x20, waiting for transfers between devices, exchange(): return lax.ppermute(value, AXES, pairs)  16.2 us
    pallas_call x1, Pallas kernels, shards(): pl.pallas_call(functools.partial(finish_kernel, times, people, chunk, spo...  6.87 us
    pallas_call x1, Pallas kernels, shards(): pl.pallas_call(functools.partial(partials_kernel, times), out_shape=[jax....  2.48 us
    unnamed x6, local copies, waits for them, and re-layouts  2.23 us
  transfers between devices with their start and end apart: 20, of which 12 were waited for; matrix products, arithmetic and copies ran while one was open for 0% of the time, Pallas kernels for 0%

profile of v2, /device:TPU:0, one launch (start us, length us, event | category | flops | bytes accessed | tf_op | source)
XLA Modules:
  0.0 49.2 jit_solution(15443511777698894333)
XLA Ops:
  0.8 1.2 %copy-done = bf16[1,450,1024]{2,1,0:T(8,128)(2,1)S(1)} copy-done((bf16[1,450,1024]{2,1,0:T(8,128)(2,1)S(1)}, bf16[1,450,1024]{2,1,0:T(8,128)(2,1)}, u32[]{:S(2)}) %copy-start) | copy-done | bytes 921624
  2.0 1.0 %copy-done.2 = bf16[1,256,1024]{2,1,0:T(8,128)(2,1)S(1)} copy-done((bf16[1,256,1024]{2,1,0:T(8,128)(2,1)S(1)}, bf16[1,256,1024]{2,1,0:T(8,128)(2,1)}, u32[]{:S(2)}) %copy-start.2) | copy-done | bytes 524312
  3.0 2.5 %partials.1 = (f32[256,512]{1,0:T(8,128)S(1)}, f32[256,512]{1,0:T(8,128)S(1)}) custom-call(s32[4]{0:T(128)S(1)} %pad_add_fusion.place_ref, bf16[450,1024]{1,0:T(8,128)(2,1)S(1)} %bitcast.7, bf16[256,1024]{1,0:T(8,128)(2,1)S(1)} %bitcast.9), custom_call_target="tpu_custom_call" | custom-call | tf_op jit(solution)/shard_map/partials/pallas_call | solution.py:146
  5.5 0.5 %collective-permute-start = (f32[256,512]{1,0:T(8,128)S(1)}, f32[256,512]{1,0:T(8,128)S(1)}, u32[]{:S(2)}, u32[]{:S(2)}) collective-permute-start(f32[256,512]{1,0:T(8,128)S(1)} %get-tuple-element.7), channel_id=1, source_target_pairs={{0,1},{1,0},{2,3},{3,2},{4,5},{5,4},{6,7},{7,6},{8,9},{9,8},{10,11... | collective-permute-start | bytes 1572872 | tf_op jit(solution)/shard_map/ppermute | solution.py:126
  6.0 1.5 %collective-permute-done = f32[256,512]{1,0:T(8,128)S(1)} collective-permute-done((f32[256,512]{1,0:T(8,128)S(1)}, f32[256,512]{1,0:T(8,128)S(1)}, u32[]{:S(2)}, u32[]{:S(2)}) %collective-permute-start) | collective-permute-done | bytes 524320 | tf_op jit(solution)/shard_map/ppermute | solution.py:126
  7.5 0.1 add.70
  7.7 3.0 %collective-permute-start.1 = (f32[64,512]{1,0:T(8,128)S(1)}, f32[64,512]{1,0:T(8,128)S(1)}, u32[]{:S(2)}, u32[]{:S(2)}) collective-permute-start(f32[64,512]{1,0:T(8,128)S(1)} %constant_dynamic-slice_fusion.4), channel_id=1, source_target_pairs={{0,2},{1,3},{2,0},{3,1},{4,6},{5,7},{6,4},{7,5},{8,10},{9,11},{10,... | collective-permute-start | bytes 393224 | tf_op jit(solution)/shard_map/ppermute | solution.py:126
  10.6 3.8 %collective-permute-done.1 = f32[64,512]{1,0:T(8,128)S(1)} collective-permute-done((f32[64,512]{1,0:T(8,128)S(1)}, f32[64,512]{1,0:T(8,128)S(1)}, u32[]{:S(2)}, u32[]{:S(2)}) %collective-permute-start.1) | collective-permute-done | bytes 131104 | tf_op jit(solution)/shard_map/ppermute | solution.py:126
  14.5 1.9 %collective-permute-start.2 = (f32[32,512]{1,0:T(8,128)S(1)}, f32[32,512]{1,0:T(8,128)S(1)}, u32[]{:S(2)}, u32[]{:S(2)}) collective-permute-start(f32[32,512]{1,0:T(8,128)S(1)} %constant_dynamic-slice_fusion.3), channel_id=1, source_target_pairs={{0,4},{1,5},{2,6},{3,7},{4,0},{5,1},{6,2},{7,3},{8,12},{9,13},{10,... | collective-permute-start | bytes 196616 | tf_op jit(solution)/shard_map/ppermute | solution.py:126
  16.4 1.6 %collective-permute-start.7 = (f32[32,512]{1,0:T(8,128)S(1)}, f32[32,512]{1,0:T(8,128)S(1)}, u32[]{:S(2)}, u32[]{:S(2)}) collective-permute-start(f32[32,512]{1,0:T(8,128)S(1)} %get-tuple-element.12), channel_id=1, source_target_pairs={{0,16},{1,17},{2,18},{3,19},{4,20},{5,21},{6,22},{7,23},{8,24},{9,... | collective-permute-start | bytes 196616 | tf_op jit(solution)/shard_map/ppermute | solution.py:126
  17.9 1.5 %collective-permute-start.8 = (f32[32,512]{1,0:T(8,128)S(1)}, f32[32,512]{1,0:T(8,128)S(1)}, u32[]{:S(2)}, u32[]{:S(2)}) collective-permute-start(f32[32,512]{1,0:T(8,128)S(1)} %get-tuple-element.13), channel_id=1, source_target_pairs={{0,18},{1,19},{2,16},{3,17},{4,22},{5,23},{6,20},{7,21},{8,26},{9,... | collective-permute-start | bytes 196616 | tf_op jit(solution)/shard_map/ppermute | solution.py:126
  19.4 0.5 %collective-permute-start.6 = (f32[32,512]{1,0:T(8,128)S(1)}, f32[32,512]{1,0:T(8,128)S(1)}, u32[]{:S(2)}, u32[]{:S(2)}) collective-permute-start(f32[32,512]{1,0:T(8,128)S(1)} %get-tuple-element.14), channel_id=1, source_target_pairs={{0,2},{1,3},{2,0},{3,1},{4,6},{5,7},{6,4},{7,5},{8,10},{9,11},{10,... | collective-permute-start | bytes 196616 | tf_op jit(solution)/shard_map/ppermute | solution.py:126
  20.0 2.7 %collective-permute-start.3 = (f32[32,512]{1,0:T(8,128)S(1)}, f32[32,512]{1,0:T(8,128)S(1)}, u32[]{:S(2)}, u32[]{:S(2)}) collective-permute-start(f32[32,512]{1,0:T(8,128)S(1)} %dynamic-slice_add_fusion.1), channel_id=1, source_target_pairs={{0,8},{1,9},{2,10},{3,11},{4,12},{5,13},{6,14},{7,15},{8,0},{9,1},... | collective-permute-start | bytes 196616 | tf_op jit(solution)/shard_map/ppermute | solution.py:126
  22.6 0.5 collective-permute-done.8
  23.1 0.7 %collective-permute-done.6 = f32[32,512]{1,0:T(8,128)S(1)} collective-permute-done((f32[32,512]{1,0:T(8,128)S(1)}, f32[32,512]{1,0:T(8,128)S(1)}, u32[]{:S(2)}, u32[]{:S(2)}) %collective-permute-start.6) | collective-permute-done | bytes 65568 | tf_op jit(solution)/shard_map/ppermute | solution.py:126
  23.8 0.5 %collective-permute-start.9 = (f32[32,512]{1,0:T(8,128)S(1)}, f32[32,512]{1,0:T(8,128)S(1)}, u32[]{:S(2)}, u32[]{:S(2)}) collective-permute-start(f32[32,512]{1,0:T(8,128)S(1)} %add_add_fusion), channel_id=1, source_target_pairs={{0,4},{1,5},{2,6},{3,7},{4,0},{5,1},{6,2},{7,3},{8,12},{9,13},{10,... | collective-permute-start | bytes 196616 | tf_op jit(solution)/shard_map/ppermute | solution.py:126
  24.4 1.5 %collective-permute-done.3 = f32[32,512]{1,0:T(8,128)S(1)} collective-permute-done((f32[32,512]{1,0:T(8,128)S(1)}, f32[32,512]{1,0:T(8,128)S(1)}, u32[]{:S(2)}, u32[]{:S(2)}) %collective-permute-start.3) | collective-permute-done | bytes 65568 | tf_op jit(solution)/shard_map/ppermute | solution.py:126
  25.9 0.2 collective-permute-start.4
  26.1 2.1 %collective-permute-done.9 = f32[32,512]{1,0:T(8,128)S(1)} collective-permute-done((f32[32,512]{1,0:T(8,128)S(1)}, f32[32,512]{1,0:T(8,128)S(1)}, u32[]{:S(2)}, u32[]{:S(2)}) %collective-permute-start.9) | collective-permute-done | bytes 65568 | tf_op jit(solution)/shard_map/ppermute | solution.py:126
  28.2 2.7 %collective-permute-start.10 = (f32[32,512]{1,0:T(8,128)S(1)}, f32[32,512]{1,0:T(8,128)S(1)}, u32[]{:S(2)}, u32[]{:S(2)}) collective-permute-start(f32[32,512]{1,0:T(8,128)S(1)} %add.85), channel_id=1, source_target_pairs={{0,8},{1,9},{2,10},{3,11},{4,12},{5,13},{6,14},{7,15},{8,0},{9,1},... | collective-permute-start | bytes 196616 | tf_op jit(solution)/shard_map/ppermute | solution.py:126
  30.9 1.2 %collective-permute-start.5 = (f32[64,512]{1,0:T(8,128)S(1)}, f32[64,512]{1,0:T(8,128)S(1)}, u32[]{:S(2)}, u32[]{:S(2)}) collective-permute-start(f32[64,512]{1,0:T(8,128)S(1)} %pad_maximum_fusion.refs_0_), channel_id=1, source_target_pairs={{0,2},{1,3},{2,0},{3,1},{4,6},{5,7},{6,4},{7,5},{8,10},{9,11},{10,... | collective-permute-start | bytes 393224 | tf_op jit(solution)/shard_map/ppermute | solution.py:126
  32.0 2.0 %collective-permute-done.10 = f32[32,512]{1,0:T(8,128)S(1)} collective-permute-done((f32[32,512]{1,0:T(8,128)S(1)}, f32[32,512]{1,0:T(8,128)S(1)}, u32[]{:S(2)}, u32[]{:S(2)}) %collective-permute-start.10) | collective-permute-done | bytes 65568 | tf_op jit(solution)/shard_map/ppermute | solution.py:126
  34.1 1.8 %collective-permute-start.13 = (f32[32,512]{1,0:T(8,128)S(1)}, f32[32,512]{1,0:T(8,128)S(1)}, u32[]{:S(2)}, u32[]{:S(2)}) collective-permute-start(f32[32,512]{1,0:T(8,128)S(1)} %add.86.refs_2_), channel_id=1, source_target_pairs={{0,18},{1,19},{2,16},{3,17},{4,22},{5,23},{6,20},{7,21},{8,26},{9,... | collective-permute-start | bytes 196616 | tf_op jit(solution)/shard_map/ppermute | solution.py:126
  35.9 1.0 %collective-permute-start.12 = (f32[32,512]{1,0:T(8,128)S(1)}, f32[32,512]{1,0:T(8,128)S(1)}, u32[]{:S(2)}, u32[]{:S(2)}) collective-permute-start(f32[32,512]{1,0:T(8,128)S(1)} %add.86.refs_2_), channel_id=1, source_target_pairs={{0,16},{1,17},{2,18},{3,19},{4,20},{5,21},{6,22},{7,23},{8,24},{9,... | collective-permute-start | bytes 196616 | tf_op jit(solution)/shard_map/ppermute | solution.py:126
  36.8 0.8 %collective-permute-start.11 = (f32[32,512]{1,0:T(8,128)S(1)}, f32[32,512]{1,0:T(8,128)S(1)}, u32[]{:S(2)}, u32[]{:S(2)}) collective-permute-start(f32[32,512]{1,0:T(8,128)S(1)} %add.86.refs_2_), channel_id=1, source_target_pairs={{0,2},{1,3},{2,0},{3,1},{4,6},{5,7},{6,4},{7,5},{8,10},{9,11},{10,... | collective-permute-start | bytes 196616 | tf_op jit(solution)/shard_map/ppermute | solution.py:126
  37.7 0.5 %collective-permute-start.15 = (f32[64,512]{1,0:T(8,128)S(1)}, f32[64,512]{1,0:T(8,128)S(1)}, u32[]{:S(2)}, u32[]{:S(2)}) collective-permute-start(f32[64,512]{1,0:T(8,128)S(1)} %collective-permute-done.5.refs_1_), channel_id=1, source_target_pairs={{0,1},{1,0},{2,3},{3,2},{4,5},{5,4},{6,7},{7,6},{8,9},{9,8},{10,11... | collective-permute-start | bytes 393224 | tf_op jit(solution)/shard_map/ppermute | solution.py:126
  38.2 1.4 %collective-permute-done.13.refs_5_ = f32[32,512]{1,0:T(8,128)S(1)} collective-permute-done((f32[32,512]{1,0:T(8,128)S(1)}, f32[32,512]{1,0:T(8,128)S(1)}, u32[]{:S(2)}, u32[]{:S(2)}) %collective-permute-start.13) | collective-permute-done | bytes 65568 | tf_op jit(solution)/shard_map/ppermute | solution.py:126
  39.5 1.1 %collective-permute-done.12.refs_4_ = f32[32,512]{1,0:T(8,128)S(1)} collective-permute-done((f32[32,512]{1,0:T(8,128)S(1)}, f32[32,512]{1,0:T(8,128)S(1)}, u32[]{:S(2)}, u32[]{:S(2)}) %collective-permute-start.12) | collective-permute-done | bytes 65568 | tf_op jit(solution)/shard_map/ppermute | solution.py:126
  40.6 0.4 collective-permute-done.11.refs_3_
  41.1 0.7 %collective-permute-done.18.refs_10_ = f32[32,512]{1,0:T(8,128)S(1)} collective-permute-done((f32[32,512]{1,0:T(8,128)S(1)}, f32[32,512]{1,0:T(8,128)S(1)}, u32[]{:S(2)}, u32[]{:S(2)}) %collective-permute-start.18) | collective-permute-done | bytes 65568 | tf_op jit(solution)/shard_map/ppermute | solution.py:126
  41.9 0.4 collective-permute-done.17.refs_9_
  42.3 6.9 %finish.1 = (f32[450,256]{1,0:T(8,128)}, bf16[256,1024]{1,0:T(8,128)(2,1)}) custom-call(s32[4]{0:T(128)S(1)} %pad_add_fusion.place_ref, bf16[450,1024]{1,0:T(8,128)(2,1)S(1)} %bitcast.8, f32[64,512]{1,0:T(8,128)S(1)} %pad_maximum_fusion.refs_0_, f32[64,512]{1,0:T(8,128)S(1)} %collective-permute-done.5.refs_1_, f32[32,512]{1,0:T(8,128)S(1)} %add.86.refs_2_, ...), custom_call_target="tpu_custom_call" | custom-call | tf_op jit(solution)/shard_map/finish/pallas_call | solution.py:180
  (29 shorter events, 0.4 us)
Async XLA Ops:
  0.8 1.2 %copy-start = (bf16[1,450,1024]{2,1,0:T(8,128)(2,1)S(1)}, bf16[1,450,1024]{2,1,0:T(8,128)(2,1)}, u32[]{:S(2)}) copy-start(bf16[1,450,1024]{2,1,0:T(8,128)(2,1)} %param.2) | copy-start | bytes 2764804
  2.0 1.0 %copy-start.2 = (bf16[1,256,1024]{2,1,0:T(8,128)(2,1)S(1)}, bf16[1,256,1024]{2,1,0:T(8,128)(2,1)}, u32[]{:S(2)}) copy-start(bf16[1,256,1024]{2,1,0:T(8,128)(2,1)} %param.3) | copy-start | bytes 1572868
  5.5 2.1 %collective-permute-start = (f32[256,512]{1,0:T(8,128)S(1)}, f32[256,512]{1,0:T(8,128)S(1)}, u32[]{:S(2)}, u32[]{:S(2)}) collective-permute-start(f32[256,512]{1,0:T(8,128)S(1)} %get-tuple-element.7), channel_id=1, source_target_pairs={{0,1},{1,0},{2,3},{3,2},{4,5},{5,4},{6,7},{7,6},{8,9},{9,8},{10,11... | collective-permute-start | bytes 1572872 | tf_op jit(solution)/shard_map/ppermute | solution.py:126
  7.7 6.8 %collective-permute-start.1 = (f32[64,512]{1,0:T(8,128)S(1)}, f32[64,512]{1,0:T(8,128)S(1)}, u32[]{:S(2)}, u32[]{:S(2)}) collective-permute-start(f32[64,512]{1,0:T(8,128)S(1)} %constant_dynamic-slice_fusion.4), channel_id=1, source_target_pairs={{0,2},{1,3},{2,0},{3,1},{4,6},{5,7},{6,4},{7,5},{8,10},{9,11},{10,... | collective-permute-start | bytes 393224 | tf_op jit(solution)/shard_map/ppermute | solution.py:126
  14.5 27.9 %copy-start.1 = (bf16[1,450,1024]{2,1,0:T(8,128)(2,1)S(1)}, bf16[1,450,1024]{2,1,0:T(8,128)(2,1)}, u32[]{:S(2)}) copy-start(bf16[1,450,1024]{2,1,0:T(8,128)(2,1)} %param.2) | copy-start | bytes 2764804
  14.5 5.4 %collective-permute-start.2 = (f32[32,512]{1,0:T(8,128)S(1)}, f32[32,512]{1,0:T(8,128)S(1)}, u32[]{:S(2)}, u32[]{:S(2)}) collective-permute-start(f32[32,512]{1,0:T(8,128)S(1)} %constant_dynamic-slice_fusion.3), channel_id=1, source_target_pairs={{0,4},{1,5},{2,6},{3,7},{4,0},{5,1},{6,2},{7,3},{8,12},{9,13},{10,... | collective-permute-start | bytes 196616 | tf_op jit(solution)/shard_map/ppermute | solution.py:126
  16.4 6.2 %collective-permute-start.7 = (f32[32,512]{1,0:T(8,128)S(1)}, f32[32,512]{1,0:T(8,128)S(1)}, u32[]{:S(2)}, u32[]{:S(2)}) collective-permute-start(f32[32,512]{1,0:T(8,128)S(1)} %get-tuple-element.12), channel_id=1, source_target_pairs={{0,16},{1,17},{2,18},{3,19},{4,20},{5,21},{6,22},{7,23},{8,24},{9,... | collective-permute-start | bytes 196616 | tf_op jit(solution)/shard_map/ppermute | solution.py:126
  17.9 5.2 %collective-permute-start.8 = (f32[32,512]{1,0:T(8,128)S(1)}, f32[32,512]{1,0:T(8,128)S(1)}, u32[]{:S(2)}, u32[]{:S(2)}) collective-permute-start(f32[32,512]{1,0:T(8,128)S(1)} %get-tuple-element.13), channel_id=1, source_target_pairs={{0,18},{1,19},{2,16},{3,17},{4,22},{5,23},{6,20},{7,21},{8,26},{9,... | collective-permute-start | bytes 196616 | tf_op jit(solution)/shard_map/ppermute | solution.py:126
  19.4 4.4 %collective-permute-start.6 = (f32[32,512]{1,0:T(8,128)S(1)}, f32[32,512]{1,0:T(8,128)S(1)}, u32[]{:S(2)}, u32[]{:S(2)}) collective-permute-start(f32[32,512]{1,0:T(8,128)S(1)} %get-tuple-element.14), channel_id=1, source_target_pairs={{0,2},{1,3},{2,0},{3,1},{4,6},{5,7},{6,4},{7,5},{8,10},{9,11},{10,... | collective-permute-start | bytes 196616 | tf_op jit(solution)/shard_map/ppermute | solution.py:126
  20.0 5.9 %collective-permute-start.3 = (f32[32,512]{1,0:T(8,128)S(1)}, f32[32,512]{1,0:T(8,128)S(1)}, u32[]{:S(2)}, u32[]{:S(2)}) collective-permute-start(f32[32,512]{1,0:T(8,128)S(1)} %dynamic-slice_add_fusion.1), channel_id=1, source_target_pairs={{0,8},{1,9},{2,10},{3,11},{4,12},{5,13},{6,14},{7,15},{8,0},{9,1},... | collective-permute-start | bytes 196616 | tf_op jit(solution)/shard_map/ppermute | solution.py:126
  23.8 4.3 %collective-permute-start.9 = (f32[32,512]{1,0:T(8,128)S(1)}, f32[32,512]{1,0:T(8,128)S(1)}, u32[]{:S(2)}, u32[]{:S(2)}) collective-permute-start(f32[32,512]{1,0:T(8,128)S(1)} %add_add_fusion), channel_id=1, source_target_pairs={{0,4},{1,5},{2,6},{3,7},{4,0},{5,1},{6,2},{7,3},{8,12},{9,13},{10,... | collective-permute-start | bytes 196616 | tf_op jit(solution)/shard_map/ppermute | solution.py:126
  25.9 4.9 %collective-permute-start.4 = (f32[32,512]{1,0:T(8,128)S(1)}, f32[32,512]{1,0:T(8,128)S(1)}, u32[]{:S(2)}, u32[]{:S(2)}) collective-permute-start(f32[32,512]{1,0:T(8,128)S(1)} %add.77), channel_id=1, source_target_pairs={{0,4},{1,5},{2,6},{3,7},{4,0},{5,1},{6,2},{7,3},{8,12},{9,13},{10,... | collective-permute-start | bytes 196616 | tf_op jit(solution)/shard_map/ppermute | solution.py:126
  28.2 5.8 %collective-permute-start.10 = (f32[32,512]{1,0:T(8,128)S(1)}, f32[32,512]{1,0:T(8,128)S(1)}, u32[]{:S(2)}, u32[]{:S(2)}) collective-permute-start(f32[32,512]{1,0:T(8,128)S(1)} %add.85), channel_id=1, source_target_pairs={{0,8},{1,9},{2,10},{3,11},{4,12},{5,13},{6,14},{7,15},{8,0},{9,1},... | collective-permute-start | bytes 196616 | tf_op jit(solution)/shard_map/ppermute | solution.py:126
  30.9 6.8 %collective-permute-start.5 = (f32[64,512]{1,0:T(8,128)S(1)}, f32[64,512]{1,0:T(8,128)S(1)}, u32[]{:S(2)}, u32[]{:S(2)}) collective-permute-start(f32[64,512]{1,0:T(8,128)S(1)} %pad_maximum_fusion.refs_0_), channel_id=1, source_target_pairs={{0,2},{1,3},{2,0},{3,1},{4,6},{5,7},{6,4},{7,5},{8,10},{9,11},{10,... | collective-permute-start | bytes 393224 | tf_op jit(solution)/shard_map/ppermute | solution.py:126
  34.0 3.6 %collective-permute-start.16 = (f32[32,512]{1,0:T(8,128)S(1)}, f32[32,512]{1,0:T(8,128)S(1)}, u32[]{:S(2)}, u32[]{:S(2)}) collective-permute-start(f32[32,512]{1,0:T(8,128)S(1)} %add.86.refs_2_), channel_id=1, source_target_pairs={{0,1},{1,0},{2,3},{3,2},{4,5},{5,4},{6,7},{7,6},{8,9},{9,8},{10,11... | collective-permute-start | bytes 196616 | tf_op jit(solution)/shard_map/ppermute | solution.py:126
  34.1 5.4 %collective-permute-start.13 = (f32[32,512]{1,0:T(8,128)S(1)}, f32[32,512]{1,0:T(8,128)S(1)}, u32[]{:S(2)}, u32[]{:S(2)}) collective-permute-start(f32[32,512]{1,0:T(8,128)S(1)} %add.86.refs_2_), channel_id=1, source_target_pairs={{0,18},{1,19},{2,16},{3,17},{4,22},{5,23},{6,20},{7,21},{8,26},{9,... | collective-permute-start | bytes 196616 | tf_op jit(solution)/shard_map/ppermute | solution.py:126
  35.9 4.8 %collective-permute-start.12 = (f32[32,512]{1,0:T(8,128)S(1)}, f32[32,512]{1,0:T(8,128)S(1)}, u32[]{:S(2)}, u32[]{:S(2)}) collective-permute-start(f32[32,512]{1,0:T(8,128)S(1)} %add.86.refs_2_), channel_id=1, source_target_pairs={{0,16},{1,17},{2,18},{3,19},{4,20},{5,21},{6,22},{7,23},{8,24},{9,... | collective-permute-start | bytes 196616 | tf_op jit(solution)/shard_map/ppermute | solution.py:126
  36.8 4.3 %collective-permute-start.11 = (f32[32,512]{1,0:T(8,128)S(1)}, f32[32,512]{1,0:T(8,128)S(1)}, u32[]{:S(2)}, u32[]{:S(2)}) collective-permute-start(f32[32,512]{1,0:T(8,128)S(1)} %add.86.refs_2_), channel_id=1, source_target_pairs={{0,2},{1,3},{2,0},{3,1},{4,6},{5,7},{6,4},{7,5},{8,10},{9,11},{10,... | collective-permute-start | bytes 196616 | tf_op jit(solution)/shard_map/ppermute | solution.py:126
  37.7 4.7 %collective-permute-start.14 = (f32[64,512]{1,0:T(8,128)S(1)}, f32[64,512]{1,0:T(8,128)S(1)}, u32[]{:S(2)}, u32[]{:S(2)}) collective-permute-start(f32[64,512]{1,0:T(8,128)S(1)} %pad_maximum_fusion.refs_0_), channel_id=1, source_target_pairs={{0,1},{1,0},{2,3},{3,2},{4,5},{5,4},{6,7},{7,6},{8,9},{9,8},{10,11... | collective-permute-start | bytes 393224 | tf_op jit(solution)/shard_map/ppermute | solution.py:126
  37.7 4.7 %collective-permute-start.15 = (f32[64,512]{1,0:T(8,128)S(1)}, f32[64,512]{1,0:T(8,128)S(1)}, u32[]{:S(2)}, u32[]{:S(2)}) collective-permute-start(f32[64,512]{1,0:T(8,128)S(1)} %collective-permute-done.5.refs_1_), channel_id=1, source_target_pairs={{0,1},{1,0},{2,3},{3,2},{4,5},{5,4},{6,7},{7,6},{8,9},{9,8},{10,11... | collective-permute-start | bytes 393224 | tf_op jit(solution)/shard_map/ppermute | solution.py:126
  39.5 1.6 %collective-permute-start.19 = (f32[32,512]{1,0:T(8,128)S(1)}, f32[32,512]{1,0:T(8,128)S(1)}, u32[]{:S(2)}, u32[]{:S(2)}) collective-permute-start(f32[32,512]{1,0:T(8,128)S(1)} %collective-permute-done.13.refs_5_), channel_id=1, source_target_pairs={{0,1},{1,0},{2,3},{3,2},{4,5},{5,4},{6,7},{7,6},{8,9},{9,8},{10,11... | collective-permute-start | bytes 196616 | tf_op jit(solution)/shard_map/ppermute | solution.py:126
  40.6 1.3 %collective-permute-start.18 = (f32[32,512]{1,0:T(8,128)S(1)}, f32[32,512]{1,0:T(8,128)S(1)}, u32[]{:S(2)}, u32[]{:S(2)}) collective-permute-start(f32[32,512]{1,0:T(8,128)S(1)} %collective-permute-done.12.refs_4_), channel_id=1, source_target_pairs={{0,1},{1,0},{2,3},{3,2},{4,5},{5,4},{6,7},{7,6},{8,9},{9,8},{10,11... | collective-permute-start | bytes 196616 | tf_op jit(solution)/shard_map/ppermute | solution.py:126
  41.1 1.3 %collective-permute-start.17 = (f32[32,512]{1,0:T(8,128)S(1)}, f32[32,512]{1,0:T(8,128)S(1)}, u32[]{:S(2)}, u32[]{:S(2)}) collective-permute-start(f32[32,512]{1,0:T(8,128)S(1)} %collective-permute-done.11.refs_3_), channel_id=1, source_target_pairs={{0,1},{1,0},{2,3},{3,2},{4,5},{5,4},{6,7},{7,6},{8,9},{9,8},{10,11... | collective-permute-start | bytes 196616 | tf_op jit(solution)/shard_map/ppermute | solution.py:126

commit v3 on v2

--- a/solution.py
+++ b/solution.py
@@ -38,30 +38,39 @@
     )
 
 
-def partials_kernel(times, place_ref, data_ref, maps_ref, send_ref, keep_ref, padded):
-    full, comps = padded.shape[0], maps_ref.shape[0]
-    half, block = comps // 2, full // 2
+def partials_kernel(times, data_ref, maps_ref, sums_ref, square_ref, raw, weights, padded, cross, sems):
+    parts = raw.shape[0]
+    part = raw.shape[2]
+    loads = []
+    for k in range(parts):
+        at = pl.ds(k * part, part)
+        loads.append(pltpu.make_async_copy(data_ref.at[:, at], raw.at[k], sems.at[0, k]))
+        loads.append(pltpu.make_async_copy(maps_ref.at[:, at], weights.at[k], sems.at[1, k]))
+    for load in loads:
+        load.start()
+    full, comps = padded.shape[0], weights.shape[1]
     tail = times // 16 * 16
-    padded[tail:, :] = jnp.zeros((full - tail, padded.shape[1]), padded.dtype)
-    padded[0:times, :] = data_ref[...]
-    core = place_ref[0]
-    every = padded[...]
-    for which, out_ref in ((1 - core, send_ref), (core, keep_ref)):
-        start = pl.multiple_of(which * half, half)
-        out_ref[0:half, :] = dot_nt(maps_ref[pl.ds(start, half), :], every)
-        upper = dot_nt(padded[pl.ds(start, half), :], every)
-        lower = dot_nt(padded[pl.ds(block + start, half), :], padded[block:, :])
-        row, col = grid_of(half, block)
-        row = row + start
-        diagonal = jnp.sum(jnp.where(row == col, lower, 0.0), axis=1, keepdims=True)
-        out_ref[half:, 0:block] = jnp.where(col >= row, upper[:, 0:block], lower)
-        out_ref[half:, block:] = jnp.where(col == times - block, diagonal, upper[:, block:])
+    padded[tail:, :] = jnp.zeros((full - tail, part), padded.dtype)
+    for k in range(parts):
+        loads[2 * k].wait()
+        loads[2 * k + 1].wait()
+        padded[0:times, :] = raw[k]
+        every = padded[...]
+        upper, lower = every[0:comps], every[comps:]
+        terms = dot_nt(weights[k], every), dot_nt(upper, every), dot_nt(lower, lower)
+        for ref, term in zip((sums_ref, square_ref, cross), terms):
+            ref[...] = term if k == 0 else ref[...] + term
+    row, col = grid_of(comps, comps)
+    lower = cross[...]
+    diagonal = jnp.sum(jnp.where(row == col, lower, 0.0), axis=1, keepdims=True)
+    square_ref[:, 0:comps] = jnp.where(col >= row, square_ref[:, 0:comps], lower)
+    square_ref[:, comps:] = jnp.where(col == times - comps, diagonal, square_ref[:, comps:])
 
 
 def finish_kernel(times, people, chunk, pieces, place_ref, data_ref, *refs):
     own, other = refs[: pieces + 2], refs[pieces + 2 : 2 * pieces + 4]
-    response_ref, maps_ref, total, packed, padded, sem = refs[2 * pieces + 4 :]
-    load = pltpu.make_async_copy(data_ref, padded, sem)
+    response_ref, maps_ref, total, packed, raw, turned, new, sems = refs[2 * pieces + 4 :]
+    load = pltpu.make_async_copy(data_ref, raw, sems.at[0])
     load.start()
     comps, full = total.shape
     half, block = comps // 2, full // 2
@@ -76,7 +85,9 @@
             piece = parts[d >> 1][(d & 1) * eighth : (d & 1) * eighth + eighth, :]
             packed[pl.ds(pl.multiple_of(at, 8), eighth), :] = piece
     response = total[...] / people
-    response_ref[...] = response.T[0:times, :]
+    turned[...] = response.T[0:times, :]
+    answer = pltpu.make_async_copy(turned, response_ref, sems.at[1])
+    answer.start()
     signal = response.astype(jnp.bfloat16)
     first, second = signal[:, 0:block], signal[:, block:]
     row, col = grid_of(comps, block)
@@ -111,10 +122,18 @@
     factor = inverse / jnp.sqrt(scale)
     fh, fl = split(factor)
     weights = dot(fh, signal) + dot(fl, signal)
-    wh, wl = split(weights[:, 0:times])
+    both = jnp.concatenate(split(weights[:, 0:times]), 0)
     load.wait()
-    data = padded[...]
-    maps_ref[...] = (dot(wh, data) + dot(wl, data)).astype(jnp.bfloat16)
+    stores = []
+    part = new.shape[2]
+    for k in range(new.shape[0]):
+        at = pl.ds(k * part, part)
+        result = dot(both, raw[:, at])
+        new[k] = (result[0:comps] + result[comps:]).astype(jnp.bfloat16)
+        stores.append(pltpu.make_async_copy(new.at[k], maps_ref.at[:, at], sems.at[2 + k]))
+        stores[-1].start()
+    for store in [answer, *stores]:
+        store.wait()
 
 
 def exchange(value, subjects, voxels, subj_step, vox_step):
@@ -136,23 +155,30 @@
     chunk = half // spots
     swap = functools.partial(exchange, subjects=subjects, voxels=voxels)
     s, v = lax.axis_index("subj"), lax.axis_index("vox")
-    core, side = v % 2, v // 2 % 2
-    spot, level = s * 2 + side, v // 4 % 2
+    core, side = v & 1, (v >> 1) & 1
+    spot, level = s * 2 + side, (v >> 2) & 1
     place = jnp.stack([core, spot, side, level]).astype(jnp.int32)
     smem = pl.BlockSpec(memory_space=pltpu.SMEM)
     vmem = pl.BlockSpec(memory_space=pltpu.VMEM)
     params = pltpu.CompilerParams(vmem_limit_bytes=VMEM_LIMIT)
 
-    send, keep = pl.pallas_call(
+    whole = pl.BlockSpec(memory_space=pltpu.HBM)
+    parts = 2 if wide % 512 == 0 else 1
+    sums, square = pl.pallas_call(
         functools.partial(partials_kernel, times),
         out_shape=[jax.ShapeDtypeStruct((comps, full), jnp.float32)] * 2,
-        in_specs=[smem, vmem, vmem],
+        in_specs=[whole, whole],
         out_specs=[vmem, vmem],
-        scratch_shapes=[pltpu.VMEM((full, wide), jnp.bfloat16)],
+        scratch_shapes=[
+            pltpu.VMEM((parts, times, wide // parts), jnp.bfloat16),
+            pltpu.VMEM((parts, comps, wide // parts), jnp.bfloat16),
+            pltpu.VMEM((full, wide // parts), jnp.bfloat16),
+            pltpu.VMEM((comps, comps), jnp.float32),
+            pltpu.SemaphoreType.DMA((2, parts)),
+        ],
         compiler_params=params,
         name="partials",
-    )(place, data[0], maps[0])
-    halves = keep + swap(send, subj_step=0, vox_step=1)
+    )(*(pltpu.with_memory_space_constraint(value[0], pltpu.HBM) for value in (data, maps)))
 
     def rows(value, at, size):
         return lax.dynamic_slice_in_dim(value, at * size, size, 0)
@@ -160,11 +186,12 @@
     def spot_step(d):
         return dict(subj_step=d >> 1, vox_step=2 * (d & 1))
 
-    sums, square = halves[:half], halves[half:]
+    square = rows(square, core, half) + swap(rows(square, 1 - core, half), subj_step=0, vox_step=1)
+    sums = rows(sums, core, half) + swap(rows(sums, 1 - core, half), subj_step=0, vox_step=1)
+    quarter, eighth = half // 2, half // 4
+    square = rows(square, side, quarter) + swap(rows(square, side ^ 1, quarter), subj_step=0, vox_step=2)
     got = [swap(rows(sums, spot ^ d, chunk), **spot_step(d)) for d in range(1, spots)]
     sums = rows(sums, spot, chunk) + sum(got)
-    quarter, eighth = half // 2, half // 4
-    square = rows(square, side, quarter) + swap(rows(square, side ^ 1, quarter), subj_step=0, vox_step=2)
     square = rows(square, level, eighth) + swap(rows(square, level ^ 1, eighth), subj_step=0, vox_step=4)
     sums = sums + swap(sums, subj_step=0, vox_step=4)
     step = 8
@@ -173,6 +200,7 @@
         sums = sums + swap(sums, subj_step=0, vox_step=step)
         step *= 2
     square = jnp.concatenate([square, swap(square, subj_step=0, vox_step=4)], 0)
+    square, sums = lax.optimization_barrier((square, sums))
     own = [square, swap(square, subj_step=0, vox_step=2), sums]
     own += [swap(sums, **spot_step(d)) for d in range(1, spots)]
     other = [swap(piece, subj_step=0, vox_step=1) for piece in own]
@@ -183,13 +211,15 @@
             jax.ShapeDtypeStruct((times, comps), jnp.float32),
             jax.ShapeDtypeStruct((comps, wide), jnp.bfloat16),
         ],
-        in_specs=[smem, pl.BlockSpec(memory_space=pl.ANY)] + [vmem] * (2 * spots + 4),
-        out_specs=[vmem, vmem],
+        in_specs=[smem, whole] + [vmem] * (2 * spots + 4),
+        out_specs=[whole, whole],
         scratch_shapes=[
             pltpu.VMEM((comps, full), jnp.float32),
             pltpu.VMEM((comps, full), jnp.float32),
             pltpu.VMEM((times, wide), jnp.bfloat16),
-            pltpu.SemaphoreType.DMA,
+            pltpu.VMEM((times, comps), jnp.float32),
+            pltpu.VMEM((parts, comps, wide // parts), jnp.bfloat16),
+            pltpu.SemaphoreType.DMA((2 + parts,)),
         ],
         compiler_params=params,
         name="finish",

time: 49.4 us -> 44.4 us (0.90)
  waiting for transfers between devices: 16.2 us -> 11.4 us
  starting transfers between devices: 20.3 us -> 22.6 us
  local copies, waits for them, and re-layouts: 2.32 us -> 0.11 us
  Pallas kernels: 9.35 us -> 8.82 us
    ppermute x20 -> x21, waiting for transfers between devices: 16.2 us -> 11.4 us  [exchange(): return lax.ppermute(value, AXES, pairs)]
    ppermute x20 -> x21, starting transfers between devices: 20.3 us -> 22.6 us  [exchange(): return lax.ppermute(value, AXES, pairs)]
    unnamed x6 -> x2, local copies, waits for them, and re-layouts: 2.23 us -> 0.01 us
  transfers between devices with their start and end apart: 20 -> 21, of which waited for: 12 -> 11; matrix products, arithmetic and copies ran while one was open for 0% -> 1% of each run, Pallas kernels for 0% -> 0%
where the time goes in v3:
time: 44.4 us; the launch traced here: 43.8 us
  starting transfers between devices  22.6 us (51%)
  waiting for transfers between devices  11.4 us (26%)
  Pallas kernels  8.82 us (20%)
  between operations  0.74 us (2%)
    ppermute x21, starting transfers between devices, exchange(): return lax.ppermute(value, AXES, pairs)  22.6 us
    ppermute x21, waiting for transfers between devices, exchange(): return lax.ppermute(value, AXES, pairs)  11.4 us
    pallas_call x1, Pallas kernels, shards(): pl.pallas_call(functools.partial(finish_kernel, times, people, chunk, spo...  6.52 us
    pallas_call x1, Pallas kernels, shards(): pl.pallas_call(functools.partial(partials_kernel, times), out_shape=[jax....  2.3 us
  transfers between devices with their start and end apart: 21, of which 11 were waited for; matrix products, arithmetic and copies ran while one was open for 1% of the time, Pallas kernels for 0%

profile of v3, /device:TPU:0, one launch (start us, length us, event | category | flops | bytes accessed | tf_op | source)
XLA Modules:
  0.0 43.8 jit_solution(3809123731617573168)
XLA Ops:
  0.6 2.3 %partials.1 = (f32[256,512]{1,0:T(8,128)S(1)}, f32[256,512]{1,0:T(8,128)S(1)}) custom-call(bf16[450,1024]{1,0:T(8,128)(2,1)} %bitcast.7, bf16[256,1024]{1,0:T(8,128)(2,1)} %bitcast.9), custom_call_target="tpu_custom_call" | custom-call | tf_op jit(solution)/shard_map/partials/pallas_call | solution.py:167
  3.0 0.5 %collective-permute-start = (f32[128,512]{1,0:T(8,128)S(1)}, f32[128,512]{1,0:T(8,128)S(1)}, u32[]{:S(2)}, u32[]{:S(2)}) collective-permute-start(f32[128,512]{1,0:T(8,128)S(1)} %constant_dynamic-slice_fusion.6), channel_id=1, source_target_pairs={{0,1},{1,0},{2,3},{3,2},{4,5},{5,4},{6,7},{7,6},{8,9},{9,8},{10,11... | collective-permute-start | bytes 786440 | tf_op jit(solution)/shard_map/ppermute | solution.py:145
  3.5 0.1 collective-permute-start.5
  3.6 1.0 %collective-permute-done = f32[128,512]{1,0:T(8,128)S(1)} collective-permute-done((f32[128,512]{1,0:T(8,128)S(1)}, f32[128,512]{1,0:T(8,128)S(1)}, u32[]{:S(2)}, u32[]{:S(2)}) %collective-permute-start) | collective-permute-done | bytes 262176 | tf_op jit(solution)/shard_map/ppermute | solution.py:145
  4.7 3.0 %collective-permute-start.1 = (f32[64,512]{1,0:T(8,128)S(1)}, f32[64,512]{1,0:T(8,128)S(1)}, u32[]{:S(2)}, u32[]{:S(2)}) collective-permute-start(f32[64,512]{1,0:T(8,128)S(1)} %constant_dynamic-slice_fusion.5), channel_id=1, source_target_pairs={{0,2},{1,3},{2,0},{3,1},{4,6},{5,7},{6,4},{7,5},{8,10},{9,11},{10,... | collective-permute-start | bytes 393224 | tf_op jit(solution)/shard_map/ppermute | solution.py:145
  7.7 0.0 collective-permute-done.5
  7.8 1.5 %collective-permute-start.7 = (f32[32,512]{1,0:T(8,128)S(1)}, f32[32,512]{1,0:T(8,128)S(1)}, u32[]{:S(2)}, u32[]{:S(2)}) collective-permute-start(f32[32,512]{1,0:T(8,128)S(1)} %get-tuple-element.14), channel_id=1, source_target_pairs={{0,16},{1,17},{2,18},{3,19},{4,20},{5,21},{6,22},{7,23},{8,24},{9,... | collective-permute-start | bytes 196616 | tf_op jit(solution)/shard_map/ppermute | solution.py:145
  9.3 0.2 collective-permute-start.8
  9.5 1.8 %collective-permute-start.6 = (f32[32,512]{1,0:T(8,128)S(1)}, f32[32,512]{1,0:T(8,128)S(1)}, u32[]{:S(2)}, u32[]{:S(2)}) collective-permute-start(f32[32,512]{1,0:T(8,128)S(1)} %get-tuple-element.16), channel_id=1, source_target_pairs={{0,2},{1,3},{2,0},{3,1},{4,6},{5,7},{6,4},{7,5},{8,10},{9,11},{10,... | collective-permute-start | bytes 196616 | tf_op jit(solution)/shard_map/ppermute | solution.py:145
  11.3 0.2 collective-permute-done.1
  11.5 1.9 %collective-permute-start.2 = (f32[32,512]{1,0:T(8,128)S(1)}, f32[32,512]{1,0:T(8,128)S(1)}, u32[]{:S(2)}, u32[]{:S(2)}) collective-permute-start(f32[32,512]{1,0:T(8,128)S(1)} %constant_dynamic-slice_fusion.4), channel_id=1, source_target_pairs={{0,4},{1,5},{2,6},{3,7},{4,0},{5,1},{6,2},{7,3},{8,12},{9,13},{10,... | collective-permute-start | bytes 196616 | tf_op jit(solution)/shard_map/ppermute | solution.py:145
  13.4 1.2 %collective-permute-done.8 = f32[32,512]{1,0:T(8,128)S(1)} collective-permute-done((f32[32,512]{1,0:T(8,128)S(1)}, f32[32,512]{1,0:T(8,128)S(1)}, u32[]{:S(2)}, u32[]{:S(2)}) %collective-permute-start.8) | collective-permute-done | bytes 65568 | tf_op jit(solution)/shard_map/ppermute | solution.py:145
  14.6 0.0 collective-permute-done.6
  14.6 1.8 %collective-permute-start.9 = (f32[32,512]{1,0:T(8,128)S(1)}, f32[32,512]{1,0:T(8,128)S(1)}, u32[]{:S(2)}, u32[]{:S(2)}) collective-permute-start(f32[32,512]{1,0:T(8,128)S(1)} %add_add_fusion), channel_id=1, source_target_pairs={{0,4},{1,5},{2,6},{3,7},{4,0},{5,1},{6,2},{7,3},{8,12},{9,13},{10,... | collective-permute-start | bytes 196616 | tf_op jit(solution)/shard_map/ppermute | solution.py:145
  16.4 2.7 %collective-permute-start.3 = (f32[32,512]{1,0:T(8,128)S(1)}, f32[32,512]{1,0:T(8,128)S(1)}, u32[]{:S(2)}, u32[]{:S(2)}) collective-permute-start(f32[32,512]{1,0:T(8,128)S(1)} %dynamic-slice_add_fusion.3), channel_id=1, source_target_pairs={{0,8},{1,9},{2,10},{3,11},{4,12},{5,13},{6,14},{7,15},{8,0},{9,1},... | collective-permute-start | bytes 196616 | tf_op jit(solution)/shard_map/ppermute | solution.py:145
  19.1 0.5 %collective-permute-done.9 = f32[32,512]{1,0:T(8,128)S(1)} collective-permute-done((f32[32,512]{1,0:T(8,128)S(1)}, f32[32,512]{1,0:T(8,128)S(1)}, u32[]{:S(2)}, u32[]{:S(2)}) %collective-permute-start.9) | collective-permute-done | bytes 65568 | tf_op jit(solution)/shard_map/ppermute | solution.py:145
  19.6 2.2 %collective-permute-start.10 = (f32[32,512]{1,0:T(8,128)S(1)}, f32[32,512]{1,0:T(8,128)S(1)}, u32[]{:S(2)}, u32[]{:S(2)}) collective-permute-start(f32[32,512]{1,0:T(8,128)S(1)} %add.84), channel_id=1, source_target_pairs={{0,8},{1,9},{2,10},{3,11},{4,12},{5,13},{6,14},{7,15},{8,0},{9,1},... | collective-permute-start | bytes 196616 | tf_op jit(solution)/shard_map/ppermute | solution.py:145
  21.8 1.5 %collective-permute-done.3 = f32[32,512]{1,0:T(8,128)S(1)} collective-permute-done((f32[32,512]{1,0:T(8,128)S(1)}, f32[32,512]{1,0:T(8,128)S(1)}, u32[]{:S(2)}, u32[]{:S(2)}) %collective-permute-start.3) | collective-permute-done | bytes 65568 | tf_op jit(solution)/shard_map/ppermute | solution.py:145
  23.3 0.7 %collective-permute-start.4 = (f32[32,512]{1,0:T(8,128)S(1)}, f32[32,512]{1,0:T(8,128)S(1)}, u32[]{:S(2)}, u32[]{:S(2)}) collective-permute-start(f32[32,512]{1,0:T(8,128)S(1)} %add.75), channel_id=1, source_target_pairs={{0,4},{1,5},{2,6},{3,7},{4,0},{5,1},{6,2},{7,3},{8,12},{9,13},{10,... | collective-permute-start | bytes 196616 | tf_op jit(solution)/shard_map/ppermute | solution.py:145
  24.0 0.8 %collective-permute-done.10 = f32[32,512]{1,0:T(8,128)S(1)} collective-permute-done((f32[32,512]{1,0:T(8,128)S(1)}, f32[32,512]{1,0:T(8,128)S(1)}, u32[]{:S(2)}, u32[]{:S(2)}) %collective-permute-start.10) | collective-permute-done | bytes 65568 | tf_op jit(solution)/shard_map/ppermute | solution.py:145
  24.9 2.8 %collective-permute-done.4 = f32[32,512]{1,0:T(8,128)S(1)} collective-permute-done((f32[32,512]{1,0:T(8,128)S(1)}, f32[32,512]{1,0:T(8,128)S(1)}, u32[]{:S(2)}, u32[]{:S(2)}) %collective-permute-start.4) | collective-permute-done | bytes 65568 | tf_op jit(solution)/shard_map/ppermute | solution.py:145
  27.7 0.7 %collective-permute-start.11 = (f32[64,512]{1,0:T(8,128)S(1)}, f32[64,512]{1,0:T(8,128)S(1)}, u32[]{:S(2)}, u32[]{:S(2)}) collective-permute-start(f32[64,512]{1,0:T(8,128)S(1)} %pad_maximum_fusion.refs_0_), channel_id=1, source_target_pairs={{0,2},{1,3},{2,0},{3,1},{4,6},{5,7},{6,4},{7,5},{8,10},{9,11},{10,... | collective-permute-start | bytes 393224 | tf_op jit(solution)/shard_map/ppermute | solution.py:145
  28.3 3.3 %collective-permute-start.14 = (f32[32,512]{1,0:T(8,128)S(1)}, f32[32,512]{1,0:T(8,128)S(1)}, u32[]{:S(2)}, u32[]{:S(2)}) collective-permute-start(f32[32,512]{1,0:T(8,128)S(1)} %add.85.refs_2_), channel_id=1, source_target_pairs={{0,18},{1,19},{2,16},{3,17},{4,22},{5,23},{6,20},{7,21},{8,26},{9,... | collective-permute-start | bytes 196616 | tf_op jit(solution)/shard_map/ppermute | solution.py:145
  31.6 1.2 %collective-permute-start.12 = (f32[32,512]{1,0:T(8,128)S(1)}, f32[32,512]{1,0:T(8,128)S(1)}, u32[]{:S(2)}, u32[]{:S(2)}) collective-permute-start(f32[32,512]{1,0:T(8,128)S(1)} %add.85.refs_2_), channel_id=1, source_target_pairs={{0,2},{1,3},{2,0},{3,1},{4,6},{5,7},{6,4},{7,5},{8,10},{9,11},{10,... | collective-permute-start | bytes 196616 | tf_op jit(solution)/shard_map/ppermute | solution.py:145
  32.8 0.5 %collective-permute-start.16 = (f32[64,512]{1,0:T(8,128)S(1)}, f32[64,512]{1,0:T(8,128)S(1)}, u32[]{:S(2)}, u32[]{:S(2)}) collective-permute-start(f32[64,512]{1,0:T(8,128)S(1)} %collective-permute-done.11.refs_1_), channel_id=1, source_target_pairs={{0,1},{1,0},{2,3},{3,2},{4,5},{5,4},{6,7},{7,6},{8,9},{9,8},{10,11... | collective-permute-start | bytes 393224 | tf_op jit(solution)/shard_map/ppermute | solution.py:145
  33.3 1.0 %collective-permute-done.14.refs_5_ = f32[32,512]{1,0:T(8,128)S(1)} collective-permute-done((f32[32,512]{1,0:T(8,128)S(1)}, f32[32,512]{1,0:T(8,128)S(1)}, u32[]{:S(2)}, u32[]{:S(2)}) %collective-permute-start.14) | collective-permute-done | bytes 65568 | tf_op jit(solution)/shard_map/ppermute | solution.py:145
  34.4 1.5 %collective-permute-done.13.refs_4_ = f32[32,512]{1,0:T(8,128)S(1)} collective-permute-done((f32[32,512]{1,0:T(8,128)S(1)}, f32[32,512]{1,0:T(8,128)S(1)}, u32[]{:S(2)}, u32[]{:S(2)}) %collective-permute-start.13) | collective-permute-done | bytes 65568 | tf_op jit(solution)/shard_map/ppermute | solution.py:145
  35.9 0.5 %collective-permute-start.18 = (f32[32,512]{1,0:T(8,128)S(1)}, f32[32,512]{1,0:T(8,128)S(1)}, u32[]{:S(2)}, u32[]{:S(2)}) collective-permute-start(f32[32,512]{1,0:T(8,128)S(1)} %collective-permute-done.12.refs_3_), channel_id=1, source_target_pairs={{0,1},{1,0},{2,3},{3,2},{4,5},{5,4},{6,7},{7,6},{8,9},{9,8},{10,11... | collective-permute-start | bytes 196616 | tf_op jit(solution)/shard_map/ppermute | solution.py:145
  36.4 0.1 pad_add_fusion.place_ref
  36.5 0.7 %collective-permute-done.19.refs_10_ = f32[32,512]{1,0:T(8,128)S(1)} collective-permute-done((f32[32,512]{1,0:T(8,128)S(1)}, f32[32,512]{1,0:T(8,128)S(1)}, u32[]{:S(2)}, u32[]{:S(2)}) %collective-permute-start.19) | collective-permute-done | bytes 65568 | tf_op jit(solution)/shard_map/ppermute | solution.py:145
  37.1 0.2 collective-permute-done.18.refs_9_
  37.3 6.5 %finish.1 = (f32[450,256]{1,0:T(8,128)}, bf16[256,1024]{1,0:T(8,128)(2,1)}) custom-call(s32[4]{0:T(128)S(1)} %pad_add_fusion.place_ref, bf16[450,1024]{1,0:T(8,128)(2,1)S(1)} %bitcast.8, f32[64,512]{1,0:T(8,128)S(1)} %pad_maximum_fusion.refs_0_, f32[64,512]{1,0:T(8,128)S(1)} %collective-permute-done.11.refs_1_, f32[32,512]{1,0:T(8,128)S(1)} %add.85.refs_2_, ...), custom_call_target="tpu_custom_call" | custom-call | tf_op jit(solution)/shard_map/finish/pallas_call | solution.py:208
  (29 shorter events, 0.3 us)
Async XLA Ops:
  3.0 1.7 %collective-permute-start = (f32[128,512]{1,0:T(8,128)S(1)}, f32[128,512]{1,0:T(8,128)S(1)}, u32[]{:S(2)}, u32[]{:S(2)}) collective-permute-start(f32[128,512]{1,0:T(8,128)S(1)} %constant_dynamic-slice_fusion.6), channel_id=1, source_target_pairs={{0,1},{1,0},{2,3},{3,2},{4,5},{5,4},{6,7},{7,6},{8,9},{9,8},{10,11... | collective-permute-start | bytes 786440 | tf_op jit(solution)/shard_map/ppermute | solution.py:145
  3.5 4.2 %collective-permute-start.5 = (f32[128,512]{1,0:T(8,128)S(1)}, f32[128,512]{1,0:T(8,128)S(1)}, u32[]{:S(2)}, u32[]{:S(2)}) collective-permute-start(f32[128,512]{1,0:T(8,128)S(1)} %constant_dynamic-slice_fusion.3), channel_id=1, source_target_pairs={{0,1},{1,0},{2,3},{3,2},{4,5},{5,4},{6,7},{7,6},{8,9},{9,8},{10,11... | collective-permute-start | bytes 786440 | tf_op jit(solution)/shard_map/ppermute | solution.py:145
  4.7 6.8 %collective-permute-start.1 = (f32[64,512]{1,0:T(8,128)S(1)}, f32[64,512]{1,0:T(8,128)S(1)}, u32[]{:S(2)}, u32[]{:S(2)}) collective-permute-start(f32[64,512]{1,0:T(8,128)S(1)} %constant_dynamic-slice_fusion.5), channel_id=1, source_target_pairs={{0,2},{1,3},{2,0},{3,1},{4,6},{5,7},{6,4},{7,5},{8,10},{9,11},{10,... | collective-permute-start | bytes 393224 | tf_op jit(solution)/shard_map/ppermute | solution.py:145
  7.8 5.6 %collective-permute-start.7 = (f32[32,512]{1,0:T(8,128)S(1)}, f32[32,512]{1,0:T(8,128)S(1)}, u32[]{:S(2)}, u32[]{:S(2)}) collective-permute-start(f32[32,512]{1,0:T(8,128)S(1)} %get-tuple-element.14), channel_id=1, source_target_pairs={{0,16},{1,17},{2,18},{3,19},{4,20},{5,21},{6,22},{7,23},{8,24},{9,... | collective-permute-start | bytes 196616 | tf_op jit(solution)/shard_map/ppermute | solution.py:145
  9.3 5.3 %collective-permute-start.8 = (f32[32,512]{1,0:T(8,128)S(1)}, f32[32,512]{1,0:T(8,128)S(1)}, u32[]{:S(2)}, u32[]{:S(2)}) collective-permute-start(f32[32,512]{1,0:T(8,128)S(1)} %get-tuple-element.15), channel_id=1, source_target_pairs={{0,18},{1,19},{2,16},{3,17},{4,22},{5,23},{6,20},{7,21},{8,26},{9,... | collective-permute-start | bytes 196616 | tf_op jit(solution)/shard_map/ppermute | solution.py:145
  9.5 27.8 %copy-start = (bf16[1,450,1024]{2,1,0:T(8,128)(2,1)S(1)}, bf16[1,450,1024]{2,1,0:T(8,128)(2,1)}, u32[]{:S(2)}) copy-start(bf16[1,450,1024]{2,1,0:T(8,128)(2,1)} %param.2) | copy-start | bytes 2764804
  9.5 5.1 %collective-permute-start.6 = (f32[32,512]{1,0:T(8,128)S(1)}, f32[32,512]{1,0:T(8,128)S(1)}, u32[]{:S(2)}, u32[]{:S(2)}) collective-permute-start(f32[32,512]{1,0:T(8,128)S(1)} %get-tuple-element.16), channel_id=1, source_target_pairs={{0,2},{1,3},{2,0},{3,1},{4,6},{5,7},{6,4},{7,5},{8,10},{9,11},{10,... | collective-permute-start | bytes 196616 | tf_op jit(solution)/shard_map/ppermute | solution.py:145
  11.5 4.9 %collective-permute-start.2 = (f32[32,512]{1,0:T(8,128)S(1)}, f32[32,512]{1,0:T(8,128)S(1)}, u32[]{:S(2)}, u32[]{:S(2)}) collective-permute-start(f32[32,512]{1,0:T(8,128)S(1)} %constant_dynamic-slice_fusion.4), channel_id=1, source_target_pairs={{0,4},{1,5},{2,6},{3,7},{4,0},{5,1},{6,2},{7,3},{8,12},{9,13},{10,... | collective-permute-start | bytes 196616 | tf_op jit(solution)/shard_map/ppermute | solution.py:145
  14.6 5.0 %collective-permute-start.9 = (f32[32,512]{1,0:T(8,128)S(1)}, f32[32,512]{1,0:T(8,128)S(1)}, u32[]{:S(2)}, u32[]{:S(2)}) collective-permute-start(f32[32,512]{1,0:T(8,128)S(1)} %add_add_fusion), channel_id=1, source_target_pairs={{0,4},{1,5},{2,6},{3,7},{4,0},{5,1},{6,2},{7,3},{8,12},{9,13},{10,... | collective-permute-start | bytes 196616 | tf_op jit(solution)/shard_map/ppermute | solution.py:145
  16.4 6.9 %collective-permute-start.3 = (f32[32,512]{1,0:T(8,128)S(1)}, f32[32,512]{1,0:T(8,128)S(1)}, u32[]{:S(2)}, u32[]{:S(2)}) collective-permute-start(f32[32,512]{1,0:T(8,128)S(1)} %dynamic-slice_add_fusion.3), channel_id=1, source_target_pairs={{0,8},{1,9},{2,10},{3,11},{4,12},{5,13},{6,14},{7,15},{8,0},{9,1},... | collective-permute-start | bytes 196616 | tf_op jit(solution)/shard_map/ppermute | solution.py:145
  19.6 5.2 %collective-permute-start.10 = (f32[32,512]{1,0:T(8,128)S(1)}, f32[32,512]{1,0:T(8,128)S(1)}, u32[]{:S(2)}, u32[]{:S(2)}) collective-permute-start(f32[32,512]{1,0:T(8,128)S(1)} %add.84), channel_id=1, source_target_pairs={{0,8},{1,9},{2,10},{3,11},{4,12},{5,13},{6,14},{7,15},{8,0},{9,1},... | collective-permute-start | bytes 196616 | tf_op jit(solution)/shard_map/ppermute | solution.py:145
  23.3 4.3 %collective-permute-start.4 = (f32[32,512]{1,0:T(8,128)S(1)}, f32[32,512]{1,0:T(8,128)S(1)}, u32[]{:S(2)}, u32[]{:S(2)}) collective-permute-start(f32[32,512]{1,0:T(8,128)S(1)} %add.75), channel_id=1, source_target_pairs={{0,4},{1,5},{2,6},{3,7},{4,0},{5,1},{6,2},{7,3},{8,12},{9,13},{10,... | collective-permute-start | bytes 196616 | tf_op jit(solution)/shard_map/ppermute | solution.py:145
  27.7 5.2 %collective-permute-start.11 = (f32[64,512]{1,0:T(8,128)S(1)}, f32[64,512]{1,0:T(8,128)S(1)}, u32[]{:S(2)}, u32[]{:S(2)}) collective-permute-start(f32[64,512]{1,0:T(8,128)S(1)} %pad_maximum_fusion.refs_0_), channel_id=1, source_target_pairs={{0,2},{1,3},{2,0},{3,1},{4,6},{5,7},{6,4},{7,5},{8,10},{9,11},{10,... | collective-permute-start | bytes 393224 | tf_op jit(solution)/shard_map/ppermute | solution.py:145
  28.3 4.5 %collective-permute-start.17 = (f32[32,512]{1,0:T(8,128)S(1)}, f32[32,512]{1,0:T(8,128)S(1)}, u32[]{:S(2)}, u32[]{:S(2)}) collective-permute-start(f32[32,512]{1,0:T(8,128)S(1)} %add.85.refs_2_), channel_id=1, source_target_pairs={{0,1},{1,0},{2,3},{3,2},{4,5},{5,4},{6,7},{7,6},{8,9},{9,8},{10,11... | collective-permute-start | bytes 196616 | tf_op jit(solution)/shard_map/ppermute | solution.py:145
  28.3 6.0 %collective-permute-start.14 = (f32[32,512]{1,0:T(8,128)S(1)}, f32[32,512]{1,0:T(8,128)S(1)}, u32[]{:S(2)}, u32[]{:S(2)}) collective-permute-start(f32[32,512]{1,0:T(8,128)S(1)} %add.85.refs_2_), channel_id=1, source_target_pairs={{0,18},{1,19},{2,16},{3,17},{4,22},{5,23},{6,20},{7,21},{8,26},{9,... | collective-permute-start | bytes 196616 | tf_op jit(solution)/shard_map/ppermute | solution.py:145
  31.6 4.3 %collective-permute-start.13 = (f32[32,512]{1,0:T(8,128)S(1)}, f32[32,512]{1,0:T(8,128)S(1)}, u32[]{:S(2)}, u32[]{:S(2)}) collective-permute-start(f32[32,512]{1,0:T(8,128)S(1)} %add.85.refs_2_), channel_id=1, source_target_pairs={{0,16},{1,17},{2,18},{3,19},{4,20},{5,21},{6,22},{7,23},{8,24},{9,... | collective-permute-start | bytes 196616 | tf_op jit(solution)/shard_map/ppermute | solution.py:145
  31.6 4.3 %collective-permute-start.12 = (f32[32,512]{1,0:T(8,128)S(1)}, f32[32,512]{1,0:T(8,128)S(1)}, u32[]{:S(2)}, u32[]{:S(2)}) collective-permute-start(f32[32,512]{1,0:T(8,128)S(1)} %add.85.refs_2_), channel_id=1, source_target_pairs={{0,2},{1,3},{2,0},{3,1},{4,6},{5,7},{6,4},{7,5},{8,10},{9,11},{10,... | collective-permute-start | bytes 196616 | tf_op jit(solution)/shard_map/ppermute | solution.py:145
  32.8 4.5 %collective-permute-start.15 = (f32[64,512]{1,0:T(8,128)S(1)}, f32[64,512]{1,0:T(8,128)S(1)}, u32[]{:S(2)}, u32[]{:S(2)}) collective-permute-start(f32[64,512]{1,0:T(8,128)S(1)} %pad_maximum_fusion.refs_0_), channel_id=1, source_target_pairs={{0,1},{1,0},{2,3},{3,2},{4,5},{5,4},{6,7},{7,6},{8,9},{9,8},{10,11... | collective-permute-start | bytes 393224 | tf_op jit(solution)/shard_map/ppermute | solution.py:145
  32.8 4.5 %collective-permute-start.16 = (f32[64,512]{1,0:T(8,128)S(1)}, f32[64,512]{1,0:T(8,128)S(1)}, u32[]{:S(2)}, u32[]{:S(2)}) collective-permute-start(f32[64,512]{1,0:T(8,128)S(1)} %collective-permute-done.11.refs_1_), channel_id=1, source_target_pairs={{0,1},{1,0},{2,3},{3,2},{4,5},{5,4},{6,7},{7,6},{8,9},{9,8},{10,11... | collective-permute-start | bytes 393224 | tf_op jit(solution)/shard_map/ppermute | solution.py:145
  34.4 2.1 %collective-permute-start.20 = (f32[32,512]{1,0:T(8,128)S(1)}, f32[32,512]{1,0:T(8,128)S(1)}, u32[]{:S(2)}, u32[]{:S(2)}) collective-permute-start(f32[32,512]{1,0:T(8,128)S(1)} %collective-permute-done.14.refs_5_), channel_id=1, source_target_pairs={{0,1},{1,0},{2,3},{3,2},{4,5},{5,4},{6,7},{7,6},{8,9},{9,8},{10,11... | collective-permute-start | bytes 196616 | tf_op jit(solution)/shard_map/ppermute | solution.py:145
  35.9 1.3 %collective-permute-start.19 = (f32[32,512]{1,0:T(8,128)S(1)}, f32[32,512]{1,0:T(8,128)S(1)}, u32[]{:S(2)}, u32[]{:S(2)}) collective-permute-start(f32[32,512]{1,0:T(8,128)S(1)} %collective-permute-done.13.refs_4_), channel_id=1, source_target_pairs={{0,1},{1,0},{2,3},{3,2},{4,5},{5,4},{6,7},{7,6},{8,9},{9,8},{10,11... | collective-permute-start | bytes 196616 | tf_op jit(solution)/shard_map/ppermute | solution.py:145
  35.9 1.4 %collective-permute-start.18 = (f32[32,512]{1,0:T(8,128)S(1)}, f32[32,512]{1,0:T(8,128)S(1)}, u32[]{:S(2)}, u32[]{:S(2)}) collective-permute-start(f32[32,512]{1,0:T(8,128)S(1)} %collective-permute-done.12.refs_3_), channel_id=1, source_target_pairs={{0,1},{1,0},{2,3},{3,2},{4,5},{5,4},{6,7},{7,6},{8,9},{9,8},{10,11... | collective-permute-start | bytes 196616 | tf_op jit(solution)/shard_map/ppermute | solution.py:145

commit v4 on v3

v4 whole, which is shorter than its diff:
```python
import functools

import jax
import jax.numpy as jnp
from jax import lax
from jax.experimental import pallas as pl
from jax.experimental.pallas import tpu as pltpu
from jax.sharding import PartitionSpec as P

TILE = 128
VMEM_LIMIT = 40 * 1024 * 1024
AXES = ("subj", "vox")
NT = (((1,), (1,)), ((), ()))


def dot(a, b):
    return jnp.dot(a, b, preferred_element_type=jnp.float32)


def dot_nt(a, b):
    return lax.dot_general(a, b, NT, preferred_element_type=jnp.float32)


def split(a):
    high = a.astype(jnp.bfloat16)
    return high, (a - high.astype(jnp.float32)).astype(jnp.bfloat16)


def dot3(a, b):
    (ah, al), (bh, bl) = split(a), split(b)
    return dot(ah, bh) + (dot(ah, bl) + dot(al, bh))


def grid_of(rows, cols):
    return (
        lax.broadcasted_iota(jnp.int32, (rows, cols), 0),
        lax.broadcasted_iota(jnp.int32, (rows, cols), 1),
    )


def response_kernel(times, data_ref, maps_ref, sums_ref, padded_ref, raw, weights, sems):
    parts, comps, part = weights.shape
    loads = []
    for k in range(parts):
        at = pl.ds(k * part, part)
        loads.append(pltpu.make_async_copy(data_ref.at[:, at], raw.at[k], sems.at[0, k]))
        loads.append(pltpu.make_async_copy(maps_ref.at[:, at], weights.at[k], sems.at[1, k]))
    for load in loads:
        load.start()
    full, wide = padded_ref.shape
    tail = times // 16 * 16
    padded_ref[tail:, :] = jnp.zeros((full - tail, wide), padded_ref.dtype)
    for k in range(parts):
        at = pl.ds(k * part, part)
        loads[2 * k].wait()
        loads[2 * k + 1].wait()
        padded_ref[0:times, at] = raw[k]
        term = dot_nt(weights[k], padded_ref[:, at])
        sums_ref[...] = term if k == 0 else sums_ref[...] + term


def square_kernel(times, padded_ref, square_ref):
    comps = square_ref.shape[0]
    upper = dot_nt(padded_ref[0:comps, :], padded_ref[...])
    lower = dot_nt(padded_ref[comps:, :], padded_ref[comps:, :])
    row, col = grid_of(comps, comps)
    diagonal = jnp.sum(jnp.where(row == col, lower, 0.0), axis=1, keepdims=True)
    square_ref[:, 0:comps] = jnp.where(col >= row, upper[:, 0:comps], lower)
    square_ref[:, comps:] = jnp.where(col == times - comps, diagonal, upper[:, comps:])


def finish_kernel(times, people, chunk, place_ref, data_ref, *refs):
    pieces, (response_ref, maps_ref, total, packed, turned, new, sems) = refs[:8], refs[8:]
    comps, full = total.shape
    half, block = comps // 2, full // 2
    quarter, eighth = half // 2, half // 4
    core, spot, side, level = place_ref[0], place_ref[1], place_ref[2], place_ref[3]
    for which, parts in ((core, pieces[0:4]), (1 - core, pieces[4:8])):
        for d in range(half // chunk):
            at = which * half + (spot ^ d) * chunk
            piece = parts[d * chunk // quarter][d * chunk % quarter : d * chunk % quarter + chunk, :]
            total[pl.ds(pl.multiple_of(at, 8), chunk), :] = piece
        for d in range(4):
            at = which * half + (side ^ (d >> 1)) * quarter + (level ^ (d & 1)) * eighth
            piece = parts[2 + (d >> 1)][(d & 1) * eighth : (d & 1) * eighth + eighth, :]
            packed[pl.ds(pl.multiple_of(at, 8), eighth), :] = piece
    response = total[...] / people

    def turn(k):
        size = min(times - k * TILE, TILE)
        turned[k * TILE : k * TILE + size, :] = response[:, k * TILE : (k + 1) * TILE].T[0:size, :]

    signal = response.astype(jnp.bfloat16)
    first, second = signal[:, 0:block], signal[:, block:]
    row, col = grid_of(comps, block)
    corner = packed[:, 0:block]
    beside = packed[:, block:]
    last = jnp.sum(jnp.where(col == times - block, beside, 0.0), axis=1, keepdims=True)
    u11 = jnp.where(col > row, corner, jnp.where(col == row, 0.5 * corner, 0.0))
    u22 = jnp.where(col < row, corner, jnp.where(col == row, 0.5 * last, 0.0))
    u12 = jnp.where(col < times - block, beside, 0.0)

    def dot2(a, b):
        high, low = split(b)
        return dot(a, high) + dot(a, low)

    left = dot2(first, u11)
    right = dot2(first, u12) + dot2(second, u22)
    lh, ll = split(left)
    rh, rl = split(right)
    product = (dot_nt(lh, first) + dot_nt(ll, first)) + (dot_nt(rh, second) + dot_nt(rl, second))
    gram = product + product.T
    squared = jnp.sum(gram * gram) + 1e-06
    scale = jnp.sqrt(squared)
    row, col = grid_of(comps, comps)
    diagonal = jnp.where(row == col, 1.0, 0.0)

    def two_steps(t, t2):
        inner = 1.6875 * diagonal - 0.5625 * t + 0.0625 * t2
        return 2.25 * diagonal - 2.4375 * t + dot3(t2, inner)

    t2 = dot3(gram, gram) / squared
    t = gram / scale
    turn(0)
    inverse = two_steps(t, t2)
    turn(1)
    t = dot3(dot3(t, inverse), inverse)
    turn(2)
    step = two_steps(t, dot3(t, t))
    turn(3)
    t = dot3(dot3(t, step), step)
    inverse = dot3(inverse, step)
    answer = pltpu.make_async_copy(turned, response_ref, sems.at[0])
    answer.start()
    inverse = 1.5 * inverse - 0.5 * dot3(inverse, t)
    factor = inverse / jnp.sqrt(scale)
    fh, fl = split(factor)
    weights = dot(fh, signal) + dot(fl, signal)
    both = jnp.concatenate(split(weights), 0)
    stores = []
    part = new.shape[2]
    for k in range(new.shape[0]):
        at = pl.ds(k * part, part)
        result = dot(both, data_ref[:, at])
        new[k] = (result[0:comps] + result[comps:]).astype(jnp.bfloat16)
        stores.append(pltpu.make_async_copy(new.at[k], maps_ref.at[:, at], sems.at[1 + k]))
        stores[-1].start()
    for store in [answer, *stores]:
        store.wait()


def exchange(value, subjects, voxels, subj_step, vox_step):
    pairs = [
        (s * voxels + v, (s ^ subj_step) * voxels + (v ^ vox_step))
        for s in range(subjects)
        for v in range(voxels)
    ]
    return lax.ppermute(value, AXES, pairs)


def shards(data, maps):
    subjects, voxels = lax.axis_size("subj"), lax.axis_size("vox")
    _, times, wide = data.shape
    comps = maps.shape[1]
    people = subjects * data.shape[0]
    full, half = 2 * comps, comps // 2
    spots = 2 * subjects
    chunk = half // spots
    swap = functools.partial(exchange, subjects=subjects, voxels=voxels)
    s, v = lax.axis_index("subj"), lax.axis_index("vox")
    core, side = v & 1, (v >> 1) & 1
    spot, level = s * 2 + side, (v >> 2) & 1
    place = jnp.stack([core, spot, side, level]).astype(jnp.int32)
    smem = pl.BlockSpec(memory_space=pltpu.SMEM)
    vmem = pl.BlockSpec(memory_space=pltpu.VMEM)
    params = pltpu.CompilerParams(vmem_limit_bytes=VMEM_LIMIT)

    whole = pl.BlockSpec(memory_space=pltpu.HBM)
    parts = 2 if wide % 512 == 0 else 1
    sums, padded = pl.pallas_call(
        functools.partial(response_kernel, times),
        out_shape=[
            jax.ShapeDtypeStruct((comps, full), jnp.float32),
            jax.ShapeDtypeStruct((full, wide), jnp.bfloat16),
        ],
        in_specs=[whole, whole],
        out_specs=[vmem, vmem],
        scratch_shapes=[
            pltpu.VMEM((parts, times, wide // parts), jnp.bfloat16),
            pltpu.VMEM((parts, comps, wide // parts), jnp.bfloat16),
            pltpu.SemaphoreType.DMA((2, parts)),
        ],
        compiler_params=params,
        name="response_terms",
    )(*(pltpu.with_memory_space_constraint(value[0], pltpu.HBM) for value in (data, maps)))
    square = pl.pallas_call(
        functools.partial(square_kernel, times),
        out_shape=jax.ShapeDtypeStruct((comps, full), jnp.float32),
        in_specs=[vmem],
        out_specs=vmem,
        compiler_params=params,
        cost_estimate=pl.CostEstimate(flops=6 * comps * comps * wide, bytes_accessed=full * wide * 2, transcendentals=0),
        name="square_terms",
    )(padded)

    def rows(value, at, size):
        return lax.dynamic_slice_in_dim(value, at * size, size, 0)

    def over_core(value):
        return swap(value, subj_step=0, vox_step=1)

    def over_side(value):
        return swap(value, subj_step=0, vox_step=2)

    quarter, eighth = half // 2, half // 4
    sums = rows(sums, core, half) + over_core(rows(sums, 1 - core, half))
    square = rows(square, core, half) + over_core(rows(square, 1 - core, half))

    bits = [1 << k for k in range(subjects.bit_length() - 1)]
    for bit in reversed(bits):
        size = sums.shape[0] // 2
        mine = jnp.where(s & bit > 0, 1, 0)
        sums = rows(sums, mine, size) + swap(rows(sums, 1 - mine, size), subj_step=bit, vox_step=0)
    sums = rows(sums, side, chunk) + over_side(rows(sums, 1 - side, chunk))
    step = 4
    while step < voxels:
        sums = sums + swap(sums, subj_step=0, vox_step=step)
        step *= 2
    sums = jnp.concatenate([sums, over_side(sums)], 0)
    for bit in bits[:-1]:
        sums = jnp.concatenate([sums, swap(sums, subj_step=bit, vox_step=0)], 0)
    responses = [sums, swap(sums, subj_step=bits[-1], vox_step=0)]

    square = rows(square, side, quarter) + over_side(rows(square, 1 - side, quarter))
    square = rows(square, level, eighth) + swap(rows(square, 1 - level, eighth), subj_step=0, vox_step=4)
    step = 8
    while step < voxels:
        square = square + swap(square, subj_step=0, vox_step=step)
        step *= 2
    square = jnp.concatenate([square, swap(square, subj_step=0, vox_step=4)], 0)
    squares = [square, over_side(square)]
    pieces = responses + squares
    pieces += [over_core(piece) for piece in pieces]

    response, new_maps = pl.pallas_call(
        functools.partial(finish_kernel, times, people, chunk),
        out_shape=[
            jax.ShapeDtypeStruct((times, comps), jnp.float32),
            jax.ShapeDtypeStruct((comps, wide), jnp.bfloat16),
        ],
        in_specs=[smem, vmem] + [vmem] * len(pieces),
        out_specs=[whole, whole],
        scratch_shapes=[
            pltpu.VMEM((comps, full), jnp.float32),
            pltpu.VMEM((comps, full), jnp.float32),
            pltpu.VMEM((times, comps), jnp.float32),
            pltpu.VMEM((parts, comps, wide // parts), jnp.bfloat16),
            pltpu.SemaphoreType.DMA((1 + parts,)),
        ],
        compiler_params=params,
        name="finish",
    )(place, padded, *pieces)
    return response, new_maps[None]


def solution(mesh):
    in_specs = (P("subj", None, "vox"), P("subj", None, "vox"))
    out_specs = (P(), P("subj", None, "vox"))
    return jax.shard_map(shards, mesh=mesh, in_specs=in_specs, out_specs=out_specs, check_vma=False)
```

time: 44.4 us -> 42.4 us (0.955); the launches traced: 43.8 us -> 42.3 us
  starting transfers between devices: 22.6 us -> 20.1 us
  waiting for transfers between devices: 11.4 us -> 12.8 us
  Pallas kernels: 8.82 us -> 8.31 us
    ppermute x21 -> x17, starting transfers between devices: 22.6 us -> 20.1 us  [exchange(): return lax.ppermute(value, AXES, pairs)]
    ppermute x21 -> x17, waiting for transfers between devices: 11.4 us -> 12.8 us  [exchange(): return lax.ppermute(value, AXES, pairs)]
    pallas_call x2 -> x3, Pallas kernels: 8.82 us -> 8.31 us  [the longest x1 5.88 us: shards(): pl.pallas_call(functools.partial(finish_kernel, times, people, chunk), ou...]
  transfers between devices with their start and end apart: 21 -> 17, of which waited for: 11 -> 11; matrix products, arithmetic and copies ran while one was open for 1% -> 1% of each run, Pallas kernels for 0% -> 2%
where the time goes in v4:
time: 42.4 us; the launch traced here: 42.3 us
  starting transfers between devices  20.1 us (47%)
  waiting for transfers between devices  12.8 us (30%)
  Pallas kernels  8.31 us (20%)
  between operations  0.75 us (2%)
    ppermute x17, starting transfers between devices, exchange(): return lax.ppermute(value, AXES, pairs)  20.1 us
    ppermute x17, waiting for transfers between devices, exchange(): return lax.ppermute(value, AXES, pairs)  12.8 us
    pallas_call x1, Pallas kernels, shards(): pl.pallas_call(functools.partial(finish_kernel, times, people, chunk), ou...  5.88 us
    pallas_call x1, Pallas kernels, shards(): pl.pallas_call(functools.partial(response_kernel, times), out_shape=[jax....  1.74 us
  transfers between devices with their start and end apart: 17, of which 11 were waited for; matrix products, arithmetic and copies ran while one was open for 1% of the time, Pallas kernels for 2%

profile of v4, /device:TPU:0, one launch (start us, length us, event | category | flops | bytes accessed | tf_op | source)
XLA Modules:
  0.0 42.3 jit_solution(9374929584758004116)
XLA Ops:
  0.6 1.7 %response_terms.1 = (f32[256,512]{1,0:T(8,128)S(1)}, bf16[512,1024]{1,0:T(8,128)(2,1)S(1)}) custom-call(bf16[450,1024]{1,0:T(8,128)(2,1)} %bitcast.7, bf16[256,1024]{1,0:T(8,128)(2,1)} %bitcast.8), custom_call_target="tpu_custom_call" | custom-call | tf_op jit(solution)/shard_map/response_terms/pallas_call | solution.py:180
  2.4 0.5 %collective-permute-start = (f32[128,512]{1,0:T(8,128)S(1)}, f32[128,512]{1,0:T(8,128)S(1)}, u32[]{:S(2)}, u32[]{:S(2)}) collective-permute-start(f32[128,512]{1,0:T(8,128)S(1)} %constant_dynamic-slice_fusion.5), channel_id=1, source_target_pairs={{0,1},{1,0},{2,3},{3,2},{4,5},{5,4},{6,7},{7,6},{8,9},{9,8},{10,11... | collective-permute-start | bytes 786440 | tf_op jit(solution)/shard_map/ppermute | solution.py:158
  2.9 0.7 %square_terms.1 = f32[256,512]{1,0:T(8,128)S(1)} custom-call(bf16[512,1024]{1,0:T(8,128)(2,1)S(1)} %get-tuple-element.6.padded_ref.data_ref), custom_call_target="tpu_custom_call" | custom-call | flops 402653184 | bytes 1048576 | tf_op jit(solution)/shard_map/square_terms/pallas_call | solution.py:196
  3.7 0.1 collective-permute-start.7
  3.8 0.3 collective-permute-done
  4.2 2.9 %collective-permute-start.1 = (f32[64,512]{1,0:T(8,128)S(1)}, f32[64,512]{1,0:T(8,128)S(1)}, u32[]{:S(2)}, u32[]{:S(2)}) collective-permute-start(f32[64,512]{1,0:T(8,128)S(1)} %constant_dynamic-slice_fusion.4), channel_id=1, source_target_pairs={{0,16},{1,17},{2,18},{3,19},{4,20},{5,21},{6,22},{7,23},{8,24},{9,... | collective-permute-start | bytes 393224 | tf_op jit(solution)/shard_map/ppermute | solution.py:158
  7.1 0.0 collective-permute-done.7
  7.2 1.6 %collective-permute-start.8 = (f32[64,512]{1,0:T(8,128)S(1)}, f32[64,512]{1,0:T(8,128)S(1)}, u32[]{:S(2)}, u32[]{:S(2)}) collective-permute-start(f32[64,512]{1,0:T(8,128)S(1)} %constant_dynamic-slice_fusion.1), channel_id=1, source_target_pairs={{0,2},{1,3},{2,0},{3,1},{4,6},{5,7},{6,4},{7,5},{8,10},{9,11},{10,... | collective-permute-start | bytes 393224 | tf_op jit(solution)/shard_map/ppermute | solution.py:158
  8.8 2.1 %collective-permute-done.1 = f32[64,512]{1,0:T(8,128)S(1)} collective-permute-done((f32[64,512]{1,0:T(8,128)S(1)}, f32[64,512]{1,0:T(8,128)S(1)}, u32[]{:S(2)}, u32[]{:S(2)}) %collective-permute-start.1) | collective-permute-done | bytes 131104 | tf_op jit(solution)/shard_map/ppermute | solution.py:158
  10.9 1.8 %collective-permute-start.2 = (f32[32,512]{1,0:T(8,128)S(1)}, f32[32,512]{1,0:T(8,128)S(1)}, u32[]{:S(2)}, u32[]{:S(2)}) collective-permute-start(f32[32,512]{1,0:T(8,128)S(1)} %constant_dynamic-slice_fusion.3), channel_id=1, source_target_pairs={{0,2},{1,3},{2,0},{3,1},{4,6},{5,7},{6,4},{7,5},{8,10},{9,11},{10,... | collective-permute-start | bytes 196616 | tf_op jit(solution)/shard_map/ppermute | solution.py:158
  12.8 0.0 collective-permute-done.8
  12.8 1.6 %collective-permute-start.9 = (f32[32,512]{1,0:T(8,128)S(1)}, f32[32,512]{1,0:T(8,128)S(1)}, u32[]{:S(2)}, u32[]{:S(2)}) collective-permute-start(f32[32,512]{1,0:T(8,128)S(1)} %constant_dynamic-slice_fusion), channel_id=1, source_target_pairs={{0,4},{1,5},{2,6},{3,7},{4,0},{5,1},{6,2},{7,3},{8,12},{9,13},{10,... | collective-permute-start | bytes 196616 | tf_op jit(solution)/shard_map/ppermute | solution.py:158
  14.5 0.8 %collective-permute-done.2 = f32[32,512]{1,0:T(8,128)S(1)} collective-permute-done((f32[32,512]{1,0:T(8,128)S(1)}, f32[32,512]{1,0:T(8,128)S(1)}, u32[]{:S(2)}, u32[]{:S(2)}) %collective-permute-start.2) | collective-permute-done | bytes 65568 | tf_op jit(solution)/shard_map/ppermute | solution.py:158
  15.3 1.9 %collective-permute-start.3 = (f32[32,512]{1,0:T(8,128)S(1)}, f32[32,512]{1,0:T(8,128)S(1)}, u32[]{:S(2)}, u32[]{:S(2)}) collective-permute-start(f32[32,512]{1,0:T(8,128)S(1)} %dynamic-slice_add_fusion.5), channel_id=1, source_target_pairs={{0,4},{1,5},{2,6},{3,7},{4,0},{5,1},{6,2},{7,3},{8,12},{9,13},{10,... | collective-permute-start | bytes 196616 | tf_op jit(solution)/shard_map/ppermute | solution.py:158
  17.2 0.7 %collective-permute-done.9 = f32[32,512]{1,0:T(8,128)S(1)} collective-permute-done((f32[32,512]{1,0:T(8,128)S(1)}, f32[32,512]{1,0:T(8,128)S(1)}, u32[]{:S(2)}, u32[]{:S(2)}) %collective-permute-start.9) | collective-permute-done | bytes 65568 | tf_op jit(solution)/shard_map/ppermute | solution.py:158
  17.8 2.6 %collective-permute-start.10 = (f32[32,512]{1,0:T(8,128)S(1)}, f32[32,512]{1,0:T(8,128)S(1)}, u32[]{:S(2)}, u32[]{:S(2)}) collective-permute-start(f32[32,512]{1,0:T(8,128)S(1)} %dynamic-slice_add_fusion.4), channel_id=1, source_target_pairs={{0,8},{1,9},{2,10},{3,11},{4,12},{5,13},{6,14},{7,15},{8,0},{9,1},... | collective-permute-start | bytes 196616 | tf_op jit(solution)/shard_map/ppermute | solution.py:158
  20.4 2.1 %collective-permute-start.4 = (f32[32,512]{1,0:T(8,128)S(1)}, f32[32,512]{1,0:T(8,128)S(1)}, u32[]{:S(2)}, u32[]{:S(2)}) collective-permute-start(f32[32,512]{1,0:T(8,128)S(1)} %add.72), channel_id=1, source_target_pairs={{0,8},{1,9},{2,10},{3,11},{4,12},{5,13},{6,14},{7,15},{8,0},{9,1},... | collective-permute-start | bytes 196616 | tf_op jit(solution)/shard_map/ppermute | solution.py:158
  22.5 1.9 %collective-permute-done.10 = f32[32,512]{1,0:T(8,128)S(1)} collective-permute-done((f32[32,512]{1,0:T(8,128)S(1)}, f32[32,512]{1,0:T(8,128)S(1)}, u32[]{:S(2)}, u32[]{:S(2)}) %collective-permute-start.10) | collective-permute-done | bytes 65568 | tf_op jit(solution)/shard_map/ppermute | solution.py:158
  24.5 0.4 %collective-permute-start.11 = (f32[32,512]{1,0:T(8,128)S(1)}, f32[32,512]{1,0:T(8,128)S(1)}, u32[]{:S(2)}, u32[]{:S(2)}) collective-permute-start(f32[32,512]{1,0:T(8,128)S(1)} %add.81), channel_id=1, source_target_pairs={{0,4},{1,5},{2,6},{3,7},{4,0},{5,1},{6,2},{7,3},{8,12},{9,13},{10,... | collective-permute-start | bytes 196616 | tf_op jit(solution)/shard_map/ppermute | solution.py:158
  24.9 0.8 %collective-permute-done.4 = f32[32,512]{1,0:T(8,128)S(1)} collective-permute-done((f32[32,512]{1,0:T(8,128)S(1)}, f32[32,512]{1,0:T(8,128)S(1)}, u32[]{:S(2)}, u32[]{:S(2)}) %collective-permute-start.4) | collective-permute-done | bytes 65568 | tf_op jit(solution)/shard_map/ppermute | solution.py:158
  25.7 1.2 %collective-permute-start.5 = (f32[32,512]{1,0:T(8,128)S(1)}, f32[32,512]{1,0:T(8,128)S(1)}, u32[]{:S(2)}, u32[]{:S(2)}) collective-permute-start(f32[32,512]{1,0:T(8,128)S(1)} %add.73), channel_id=1, source_target_pairs={{0,2},{1,3},{2,0},{3,1},{4,6},{5,7},{6,4},{7,5},{8,10},{9,11},{10,... | collective-permute-start | bytes 196616 | tf_op jit(solution)/shard_map/ppermute | solution.py:158
  26.9 1.9 %collective-permute-done.11 = f32[32,512]{1,0:T(8,128)S(1)} collective-permute-done((f32[32,512]{1,0:T(8,128)S(1)}, f32[32,512]{1,0:T(8,128)S(1)}, u32[]{:S(2)}, u32[]{:S(2)}) %collective-permute-start.11) | collective-permute-done | bytes 65568 | tf_op jit(solution)/shard_map/ppermute | solution.py:158
  28.8 1.2 %collective-permute-start.12 = (f32[64,512]{1,0:T(8,128)S(1)}, f32[64,512]{1,0:T(8,128)S(1)}, u32[]{:S(2)}, u32[]{:S(2)}) collective-permute-start(f32[64,512]{1,0:T(8,128)S(1)} %pad_maximum_fusion.1.refs_2_), channel_id=1, source_target_pairs={{0,2},{1,3},{2,0},{3,1},{4,6},{5,7},{6,4},{7,5},{8,10},{9,11},{10,... | collective-permute-start | bytes 393224 | tf_op jit(solution)/shard_map/ppermute | solution.py:158
  30.0 0.0 collective-permute-done.5
  30.0 1.6 %collective-permute-start.6 = (f32[64,512]{1,0:T(8,128)S(1)}, f32[64,512]{1,0:T(8,128)S(1)}, u32[]{:S(2)}, u32[]{:S(2)}) collective-permute-start(f32[64,512]{1,0:T(8,128)S(1)} %pad_maximum_fusion.refs_0_), channel_id=1, source_target_pairs={{0,16},{1,17},{2,18},{3,19},{4,20},{5,21},{6,22},{7,23},{8,24},{9,... | collective-permute-start | bytes 393224 | tf_op jit(solution)/shard_map/ppermute | solution.py:158
  31.7 0.5 %collective-permute-start.13 = (f32[64,512]{1,0:T(8,128)S(1)}, f32[64,512]{1,0:T(8,128)S(1)}, u32[]{:S(2)}, u32[]{:S(2)}) collective-permute-start(f32[64,512]{1,0:T(8,128)S(1)} %pad_maximum_fusion.refs_0_), channel_id=1, source_target_pairs={{0,1},{1,0},{2,3},{3,2},{4,5},{5,4},{6,7},{7,6},{8,9},{9,8},{10,11... | collective-permute-start | bytes 393224 | tf_op jit(solution)/shard_map/ppermute | solution.py:158
  32.2 1.7 %collective-permute-done.12.refs_3_ = f32[64,512]{1,0:T(8,128)S(1)} collective-permute-done((f32[64,512]{1,0:T(8,128)S(1)}, f32[64,512]{1,0:T(8,128)S(1)}, u32[]{:S(2)}, u32[]{:S(2)}) %collective-permute-start.12) | collective-permute-done | bytes 131104 | tf_op jit(solution)/shard_map/ppermute | solution.py:158
  33.9 1.2 %collective-permute-done.6.refs_1_ = f32[64,512]{1,0:T(8,128)S(1)} collective-permute-done((f32[64,512]{1,0:T(8,128)S(1)}, f32[64,512]{1,0:T(8,128)S(1)}, u32[]{:S(2)}, u32[]{:S(2)}) %collective-permute-start.6) | collective-permute-done | bytes 131104 | tf_op jit(solution)/shard_map/ppermute | solution.py:158
  35.1 0.1 pad_add_fusion.place_ref
  35.1 0.1 collective-permute-done.16.refs_7_
  35.2 1.2 %collective-permute-done.14.refs_5_ = f32[64,512]{1,0:T(8,128)S(1)} collective-permute-done((f32[64,512]{1,0:T(8,128)S(1)}, f32[64,512]{1,0:T(8,128)S(1)}, u32[]{:S(2)}, u32[]{:S(2)}) %collective-permute-start.14) | collective-permute-done | bytes 131104 | tf_op jit(solution)/shard_map/ppermute | solution.py:158
  36.4 5.9 %finish.1 = (f32[450,256]{1,0:T(8,128)}, bf16[256,1024]{1,0:T(8,128)(2,1)}) custom-call(s32[4]{0:T(128)S(1)} %pad_add_fusion.place_ref, bf16[512,1024]{1,0:T(8,128)(2,1)S(1)} %get-tuple-element.6.padded_ref.data_ref, f32[64,512]{1,0:T(8,128)S(1)} %pad_maximum_fusion.refs_0_, f32[64,512]{1,0:T(8,128)S(1)} %collective-permute-done.6.refs_1_, ...), custom_call_target="tpu_custom_call" | custom-call | tf_op jit(solution)/shard_map/finish/pallas_call | solution.py:245
  (23 shorter events, 0.3 us)
Async XLA Ops:
  2.4 1.7 %collective-permute-start = (f32[128,512]{1,0:T(8,128)S(1)}, f32[128,512]{1,0:T(8,128)S(1)}, u32[]{:S(2)}, u32[]{:S(2)}) collective-permute-start(f32[128,512]{1,0:T(8,128)S(1)} %constant_dynamic-slice_fusion.5), channel_id=1, source_target_pairs={{0,1},{1,0},{2,3},{3,2},{4,5},{5,4},{6,7},{7,6},{8,9},{9,8},{10,11... | collective-permute-start | bytes 786440 | tf_op jit(solution)/shard_map/ppermute | solution.py:158
  3.7 3.4 %collective-permute-start.7 = (f32[128,512]{1,0:T(8,128)S(1)}, f32[128,512]{1,0:T(8,128)S(1)}, u32[]{:S(2)}, u32[]{:S(2)}) collective-permute-start(f32[128,512]{1,0:T(8,128)S(1)} %constant_dynamic-slice_fusion.2), channel_id=1, source_target_pairs={{0,1},{1,0},{2,3},{3,2},{4,5},{5,4},{6,7},{7,6},{8,9},{9,8},{10,11... | collective-permute-start | bytes 786440 | tf_op jit(solution)/shard_map/ppermute | solution.py:158
  4.2 6.7 %collective-permute-start.1 = (f32[64,512]{1,0:T(8,128)S(1)}, f32[64,512]{1,0:T(8,128)S(1)}, u32[]{:S(2)}, u32[]{:S(2)}) collective-permute-start(f32[64,512]{1,0:T(8,128)S(1)} %constant_dynamic-slice_fusion.4), channel_id=1, source_target_pairs={{0,16},{1,17},{2,18},{3,19},{4,20},{5,21},{6,22},{7,23},{8,24},{9,... | collective-permute-start | bytes 393224 | tf_op jit(solution)/shard_map/ppermute | solution.py:158
  7.2 5.6 %collective-permute-start.8 = (f32[64,512]{1,0:T(8,128)S(1)}, f32[64,512]{1,0:T(8,128)S(1)}, u32[]{:S(2)}, u32[]{:S(2)}) collective-permute-start(f32[64,512]{1,0:T(8,128)S(1)} %constant_dynamic-slice_fusion.1), channel_id=1, source_target_pairs={{0,2},{1,3},{2,0},{3,1},{4,6},{5,7},{6,4},{7,5},{8,10},{9,11},{10,... | collective-permute-start | bytes 393224 | tf_op jit(solution)/shard_map/ppermute | solution.py:158
  10.9 4.3 %collective-permute-start.2 = (f32[32,512]{1,0:T(8,128)S(1)}, f32[32,512]{1,0:T(8,128)S(1)}, u32[]{:S(2)}, u32[]{:S(2)}) collective-permute-start(f32[32,512]{1,0:T(8,128)S(1)} %constant_dynamic-slice_fusion.3), channel_id=1, source_target_pairs={{0,2},{1,3},{2,0},{3,1},{4,6},{5,7},{6,4},{7,5},{8,10},{9,11},{10,... | collective-permute-start | bytes 196616 | tf_op jit(solution)/shard_map/ppermute | solution.py:158
  12.8 5.0 %collective-permute-start.9 = (f32[32,512]{1,0:T(8,128)S(1)}, f32[32,512]{1,0:T(8,128)S(1)}, u32[]{:S(2)}, u32[]{:S(2)}) collective-permute-start(f32[32,512]{1,0:T(8,128)S(1)} %constant_dynamic-slice_fusion), channel_id=1, source_target_pairs={{0,4},{1,5},{2,6},{3,7},{4,0},{5,1},{6,2},{7,3},{8,12},{9,13},{10,... | collective-permute-start | bytes 196616 | tf_op jit(solution)/shard_map/ppermute | solution.py:158
  15.3 5.1 %collective-permute-start.3 = (f32[32,512]{1,0:T(8,128)S(1)}, f32[32,512]{1,0:T(8,128)S(1)}, u32[]{:S(2)}, u32[]{:S(2)}) collective-permute-start(f32[32,512]{1,0:T(8,128)S(1)} %dynamic-slice_add_fusion.5), channel_id=1, source_target_pairs={{0,4},{1,5},{2,6},{3,7},{4,0},{5,1},{6,2},{7,3},{8,12},{9,13},{10,... | collective-permute-start | bytes 196616 | tf_op jit(solution)/shard_map/ppermute | solution.py:158
  17.8 6.6 %collective-permute-start.10 = (f32[32,512]{1,0:T(8,128)S(1)}, f32[32,512]{1,0:T(8,128)S(1)}, u32[]{:S(2)}, u32[]{:S(2)}) collective-permute-start(f32[32,512]{1,0:T(8,128)S(1)} %dynamic-slice_add_fusion.4), channel_id=1, source_target_pairs={{0,8},{1,9},{2,10},{3,11},{4,12},{5,13},{6,14},{7,15},{8,0},{9,1},... | collective-permute-start | bytes 196616 | tf_op jit(solution)/shard_map/ppermute | solution.py:158
  20.4 5.2 %collective-permute-start.4 = (f32[32,512]{1,0:T(8,128)S(1)}, f32[32,512]{1,0:T(8,128)S(1)}, u32[]{:S(2)}, u32[]{:S(2)}) collective-permute-start(f32[32,512]{1,0:T(8,128)S(1)} %add.72), channel_id=1, source_target_pairs={{0,8},{1,9},{2,10},{3,11},{4,12},{5,13},{6,14},{7,15},{8,0},{9,1},... | collective-permute-start | bytes 196616 | tf_op jit(solution)/shard_map/ppermute | solution.py:158
  24.5 4.3 %collective-permute-start.11 = (f32[32,512]{1,0:T(8,128)S(1)}, f32[32,512]{1,0:T(8,128)S(1)}, u32[]{:S(2)}, u32[]{:S(2)}) collective-permute-start(f32[32,512]{1,0:T(8,128)S(1)} %add.81), channel_id=1, source_target_pairs={{0,4},{1,5},{2,6},{3,7},{4,0},{5,1},{6,2},{7,3},{8,12},{9,13},{10,... | collective-permute-start | bytes 196616 | tf_op jit(solution)/shard_map/ppermute | solution.py:158
  25.7 4.3 %collective-permute-start.5 = (f32[32,512]{1,0:T(8,128)S(1)}, f32[32,512]{1,0:T(8,128)S(1)}, u32[]{:S(2)}, u32[]{:S(2)}) collective-permute-start(f32[32,512]{1,0:T(8,128)S(1)} %add.73), channel_id=1, source_target_pairs={{0,2},{1,3},{2,0},{3,1},{4,6},{5,7},{6,4},{7,5},{8,10},{9,11},{10,... | collective-permute-start | bytes 196616 | tf_op jit(solution)/shard_map/ppermute | solution.py:158
  28.8 5.0 %collective-permute-start.12 = (f32[64,512]{1,0:T(8,128)S(1)}, f32[64,512]{1,0:T(8,128)S(1)}, u32[]{:S(2)}, u32[]{:S(2)}) collective-permute-start(f32[64,512]{1,0:T(8,128)S(1)} %pad_maximum_fusion.1.refs_2_), channel_id=1, source_target_pairs={{0,2},{1,3},{2,0},{3,1},{4,6},{5,7},{6,4},{7,5},{8,10},{9,11},{10,... | collective-permute-start | bytes 393224 | tf_op jit(solution)/shard_map/ppermute | solution.py:158
  30.0 5.0 %collective-permute-start.6 = (f32[64,512]{1,0:T(8,128)S(1)}, f32[64,512]{1,0:T(8,128)S(1)}, u32[]{:S(2)}, u32[]{:S(2)}) collective-permute-start(f32[64,512]{1,0:T(8,128)S(1)} %pad_maximum_fusion.refs_0_), channel_id=1, source_target_pairs={{0,16},{1,17},{2,18},{3,19},{4,20},{5,21},{6,22},{7,23},{8,24},{9,... | collective-permute-start | bytes 393224 | tf_op jit(solution)/shard_map/ppermute | solution.py:158
  31.7 3.5 %collective-permute-start.15 = (f32[64,512]{1,0:T(8,128)S(1)}, f32[64,512]{1,0:T(8,128)S(1)}, u32[]{:S(2)}, u32[]{:S(2)}) collective-permute-start(f32[64,512]{1,0:T(8,128)S(1)} %pad_maximum_fusion.1.refs_2_), channel_id=1, source_target_pairs={{0,1},{1,0},{2,3},{3,2},{4,5},{5,4},{6,7},{7,6},{8,9},{9,8},{10,11... | collective-permute-start | bytes 393224 | tf_op jit(solution)/shard_map/ppermute | solution.py:158
  31.7 3.5 %collective-permute-start.13 = (f32[64,512]{1,0:T(8,128)S(1)}, f32[64,512]{1,0:T(8,128)S(1)}, u32[]{:S(2)}, u32[]{:S(2)}) collective-permute-start(f32[64,512]{1,0:T(8,128)S(1)} %pad_maximum_fusion.refs_0_), channel_id=1, source_target_pairs={{0,1},{1,0},{2,3},{3,2},{4,5},{5,4},{6,7},{7,6},{8,9},{9,8},{10,11... | collective-permute-start | bytes 393224 | tf_op jit(solution)/shard_map/ppermute | solution.py:158
  33.9 1.3 %collective-permute-start.16 = (f32[64,512]{1,0:T(8,128)S(1)}, f32[64,512]{1,0:T(8,128)S(1)}, u32[]{:S(2)}, u32[]{:S(2)}) collective-permute-start(f32[64,512]{1,0:T(8,128)S(1)} %collective-permute-done.12.refs_3_), channel_id=1, source_target_pairs={{0,1},{1,0},{2,3},{3,2},{4,5},{5,4},{6,7},{7,6},{8,9},{9,8},{10,11... | collective-permute-start | bytes 393224 | tf_op jit(solution)/shard_map/ppermute | solution.py:158
  35.1 1.3 %collective-permute-start.14 = (f32[64,512]{1,0:T(8,128)S(1)}, f32[64,512]{1,0:T(8,128)S(1)}, u32[]{:S(2)}, u32[]{:S(2)}) collective-permute-start(f32[64,512]{1,0:T(8,128)S(1)} %collective-permute-done.6.refs_1_), channel_id=1, source_target_pairs={{0,1},{1,0},{2,3},{3,2},{4,5},{5,4},{6,7},{7,6},{8,9},{9,8},{10,11... | collective-permute-start | bytes 393224 | tf_op jit(solution)/shard_map/ppermute | solution.py:158

commit v5 on v4

--- a/solution.py
+++ b/solution.py
@@ -28,7 +28,9 @@
 
 def dot3(a, b):
     (ah, al), (bh, bl) = split(a), split(b)
-    return dot(ah, bh) + (dot(ah, bl) + dot(al, bh))
+    rows = a.shape[0]
+    product = dot(jnp.concatenate([ah, al], 0), bh)
+    return product[:rows] + (product[rows:] + dot(ah, bl))
 
 
 def grid_of(rows, cols):
@@ -110,8 +112,7 @@
     rh, rl = split(right)
     product = (dot_nt(lh, first) + dot_nt(ll, first)) + (dot_nt(rh, second) + dot_nt(rl, second))
     gram = product + product.T
-    squared = jnp.sum(gram * gram) + 1e-06
-    scale = jnp.sqrt(squared)
+    scale = jnp.sqrt(jnp.sum(gram * gram) + 1e-06)
     row, col = grid_of(comps, comps)
     diagonal = jnp.where(row == col, 1.0, 0.0)
 
@@ -119,20 +120,23 @@
         inner = 1.6875 * diagonal - 0.5625 * t + 0.0625 * t2
         return 2.25 * diagonal - 2.4375 * t + dot3(t2, inner)
 
-    t2 = dot3(gram, gram) / squared
     t = gram / scale
+    t2 = dot3(t, t)
     turn(0)
-    inverse = two_steps(t, t2)
+    first_two = two_steps(t, t2)
     turn(1)
-    t = dot3(dot3(t, inverse), inverse)
+    t = dot3(dot3(t, first_two), first_two)
     turn(2)
-    step = two_steps(t, dot3(t, t))
+    t2 = dot3(t, t)
+    moved = dot3(first_two, t)
+    next_two = two_steps(t, t2)
     turn(3)
-    t = dot3(dot3(t, step), step)
-    inverse = dot3(inverse, step)
+    inverse = dot3(first_two, next_two)
+    moved = dot3(moved, next_two)
+    cubed = dot3(next_two, next_two)
     answer = pltpu.make_async_copy(turned, response_ref, sems.at[0])
     answer.start()
-    inverse = 1.5 * inverse - 0.5 * dot3(inverse, t)
+    inverse = 1.5 * inverse - 0.5 * dot3(moved, cubed)
     factor = inverse / jnp.sqrt(scale)
     fh, fl = split(factor)
     weights = dot(fh, signal) + dot(fl, signal)

time: 42.4 us -> 42.5 us (level)
  no operation moved by 1% of the time
where the time goes in v5:
time: 42.5 us; the launch traced here: 42.3 us
  starting transfers between devices  20.1 us (47%)
  waiting for transfers between devices  12.8 us (30%)
  Pallas kernels  8.35 us (20%)
  between operations  0.75 us (2%)
    ppermute x17, starting transfers between devices, exchange(): return lax.ppermute(value, AXES, pairs)  20.1 us
    ppermute x17, waiting for transfers between devices, exchange(): return lax.ppermute(value, AXES, pairs)  12.8 us
    pallas_call x1, Pallas kernels, shards(): pl.pallas_call(functools.partial(finish_kernel, times, people, chunk), ou...  5.93 us
    pallas_call x1, Pallas kernels, shards(): pl.pallas_call(functools.partial(response_kernel, times), out_shape=[jax....  1.74 us
  transfers between devices with their start and end apart: 17, of which 11 were waited for; matrix products, arithmetic and copies ran while one was open for 1% of the time, Pallas kernels for 2%

profile of v5, /device:TPU:0, one launch (start us, length us, event | category | flops | bytes accessed | tf_op | source)
XLA Modules:
  0.0 42.3 jit_solution(836129205936217940)
XLA Ops:
  0.6 1.7 %response_terms.1 = (f32[256,512]{1,0:T(8,128)S(1)}, bf16[512,1024]{1,0:T(8,128)(2,1)S(1)}) custom-call(bf16[450,1024]{1,0:T(8,128)(2,1)} %bitcast.7, bf16[256,1024]{1,0:T(8,128)(2,1)} %bitcast.8), custom_call_target="tpu_custom_call" | custom-call | tf_op jit(solution)/shard_map/response_terms/pallas_call | solution.py:184
  2.4 0.5 %collective-permute-start = (f32[128,512]{1,0:T(8,128)S(1)}, f32[128,512]{1,0:T(8,128)S(1)}, u32[]{:S(2)}, u32[]{:S(2)}) collective-permute-start(f32[128,512]{1,0:T(8,128)S(1)} %constant_dynamic-slice_fusion.5), channel_id=1, source_target_pairs={{0,1},{1,0},{2,3},{3,2},{4,5},{5,4},{6,7},{7,6},{8,9},{9,8},{10,11... | collective-permute-start | bytes 786440 | tf_op jit(solution)/shard_map/ppermute | solution.py:162
  2.9 0.7 %square_terms.1 = f32[256,512]{1,0:T(8,128)S(1)} custom-call(bf16[512,1024]{1,0:T(8,128)(2,1)S(1)} %get-tuple-element.6.padded_ref.data_ref), custom_call_target="tpu_custom_call" | custom-call | flops 402653184 | bytes 1048576 | tf_op jit(solution)/shard_map/square_terms/pallas_call | solution.py:200
  3.7 0.1 collective-permute-start.7
  3.8 0.3 collective-permute-done
  4.2 2.9 %collective-permute-start.1 = (f32[64,512]{1,0:T(8,128)S(1)}, f32[64,512]{1,0:T(8,128)S(1)}, u32[]{:S(2)}, u32[]{:S(2)}) collective-permute-start(f32[64,512]{1,0:T(8,128)S(1)} %constant_dynamic-slice_fusion.4), channel_id=1, source_target_pairs={{0,16},{1,17},{2,18},{3,19},{4,20},{5,21},{6,22},{7,23},{8,24},{9,... | collective-permute-start | bytes 393224 | tf_op jit(solution)/shard_map/ppermute | solution.py:162
  7.1 0.0 collective-permute-done.7
  7.2 1.6 %collective-permute-start.8 = (f32[64,512]{1,0:T(8,128)S(1)}, f32[64,512]{1,0:T(8,128)S(1)}, u32[]{:S(2)}, u32[]{:S(2)}) collective-permute-start(f32[64,512]{1,0:T(8,128)S(1)} %constant_dynamic-slice_fusion.1), channel_id=1, source_target_pairs={{0,2},{1,3},{2,0},{3,1},{4,6},{5,7},{6,4},{7,5},{8,10},{9,11},{10,... | collective-permute-start | bytes 393224 | tf_op jit(solution)/shard_map/ppermute | solution.py:162
  8.8 2.1 %collective-permute-done.1 = f32[64,512]{1,0:T(8,128)S(1)} collective-permute-done((f32[64,512]{1,0:T(8,128)S(1)}, f32[64,512]{1,0:T(8,128)S(1)}, u32[]{:S(2)}, u32[]{:S(2)}) %collective-permute-start.1) | collective-permute-done | bytes 131104 | tf_op jit(solution)/shard_map/ppermute | solution.py:162
  10.9 1.8 %collective-permute-start.2 = (f32[32,512]{1,0:T(8,128)S(1)}, f32[32,512]{1,0:T(8,128)S(1)}, u32[]{:S(2)}, u32[]{:S(2)}) collective-permute-start(f32[32,512]{1,0:T(8,128)S(1)} %constant_dynamic-slice_fusion.3), channel_id=1, source_target_pairs={{0,2},{1,3},{2,0},{3,1},{4,6},{5,7},{6,4},{7,5},{8,10},{9,11},{10,... | collective-permute-start | bytes 196616 | tf_op jit(solution)/shard_map/ppermute | solution.py:162
  12.8 1.6 %collective-permute-start.9 = (f32[32,512]{1,0:T(8,128)S(1)}, f32[32,512]{1,0:T(8,128)S(1)}, u32[]{:S(2)}, u32[]{:S(2)}) collective-permute-start(f32[32,512]{1,0:T(8,128)S(1)} %constant_dynamic-slice_fusion), channel_id=1, source_target_pairs={{0,4},{1,5},{2,6},{3,7},{4,0},{5,1},{6,2},{7,3},{8,12},{9,13},{10,... | collective-permute-start | bytes 196616 | tf_op jit(solution)/shard_map/ppermute | solution.py:162
  14.5 0.8 %collective-permute-done.2 = f32[32,512]{1,0:T(8,128)S(1)} collective-permute-done((f32[32,512]{1,0:T(8,128)S(1)}, f32[32,512]{1,0:T(8,128)S(1)}, u32[]{:S(2)}, u32[]{:S(2)}) %collective-permute-start.2) | collective-permute-done | bytes 65568 | tf_op jit(solution)/shard_map/ppermute | solution.py:162
  15.3 1.9 %collective-permute-start.3 = (f32[32,512]{1,0:T(8,128)S(1)}, f32[32,512]{1,0:T(8,128)S(1)}, u32[]{:S(2)}, u32[]{:S(2)}) collective-permute-start(f32[32,512]{1,0:T(8,128)S(1)} %dynamic-slice_add_fusion.5), channel_id=1, source_target_pairs={{0,4},{1,5},{2,6},{3,7},{4,0},{5,1},{6,2},{7,3},{8,12},{9,13},{10,... | collective-permute-start | bytes 196616 | tf_op jit(solution)/shard_map/ppermute | solution.py:162
  17.2 0.7 %collective-permute-done.9 = f32[32,512]{1,0:T(8,128)S(1)} collective-permute-done((f32[32,512]{1,0:T(8,128)S(1)}, f32[32,512]{1,0:T(8,128)S(1)}, u32[]{:S(2)}, u32[]{:S(2)}) %collective-permute-start.9) | collective-permute-done | bytes 65568 | tf_op jit(solution)/shard_map/ppermute | solution.py:162
  17.8 2.6 %collective-permute-start.10 = (f32[32,512]{1,0:T(8,128)S(1)}, f32[32,512]{1,0:T(8,128)S(1)}, u32[]{:S(2)}, u32[]{:S(2)}) collective-permute-start(f32[32,512]{1,0:T(8,128)S(1)} %dynamic-slice_add_fusion.4), channel_id=1, source_target_pairs={{0,8},{1,9},{2,10},{3,11},{4,12},{5,13},{6,14},{7,15},{8,0},{9,1},... | collective-permute-start | bytes 196616 | tf_op jit(solution)/shard_map/ppermute | solution.py:162
  20.4 2.1 %collective-permute-start.4 = (f32[32,512]{1,0:T(8,128)S(1)}, f32[32,512]{1,0:T(8,128)S(1)}, u32[]{:S(2)}, u32[]{:S(2)}) collective-permute-start(f32[32,512]{1,0:T(8,128)S(1)} %add.72), channel_id=1, source_target_pairs={{0,8},{1,9},{2,10},{3,11},{4,12},{5,13},{6,14},{7,15},{8,0},{9,1},... | collective-permute-start | bytes 196616 | tf_op jit(solution)/shard_map/ppermute | solution.py:162
  22.5 1.9 %collective-permute-done.10 = f32[32,512]{1,0:T(8,128)S(1)} collective-permute-done((f32[32,512]{1,0:T(8,128)S(1)}, f32[32,512]{1,0:T(8,128)S(1)}, u32[]{:S(2)}, u32[]{:S(2)}) %collective-permute-start.10) | collective-permute-done | bytes 65568 | tf_op jit(solution)/shard_map/ppermute | solution.py:162
  24.5 0.4 %collective-permute-start.11 = (f32[32,512]{1,0:T(8,128)S(1)}, f32[32,512]{1,0:T(8,128)S(1)}, u32[]{:S(2)}, u32[]{:S(2)}) collective-permute-start(f32[32,512]{1,0:T(8,128)S(1)} %add.81), channel_id=1, source_target_pairs={{0,4},{1,5},{2,6},{3,7},{4,0},{5,1},{6,2},{7,3},{8,12},{9,13},{10,... | collective-permute-start | bytes 196616 | tf_op jit(solution)/shard_map/ppermute | solution.py:162
  24.9 0.8 %collective-permute-done.4 = f32[32,512]{1,0:T(8,128)S(1)} collective-permute-done((f32[32,512]{1,0:T(8,128)S(1)}, f32[32,512]{1,0:T(8,128)S(1)}, u32[]{:S(2)}, u32[]{:S(2)}) %collective-permute-start.4) | collective-permute-done | bytes 65568 | tf_op jit(solution)/shard_map/ppermute | solution.py:162
  25.7 1.2 %collective-permute-start.5 = (f32[32,512]{1,0:T(8,128)S(1)}, f32[32,512]{1,0:T(8,128)S(1)}, u32[]{:S(2)}, u32[]{:S(2)}) collective-permute-start(f32[32,512]{1,0:T(8,128)S(1)} %add.73), channel_id=1, source_target_pairs={{0,2},{1,3},{2,0},{3,1},{4,6},{5,7},{6,4},{7,5},{8,10},{9,11},{10,... | collective-permute-start | bytes 196616 | tf_op jit(solution)/shard_map/ppermute | solution.py:162
  26.9 1.9 %collective-permute-done.11 = f32[32,512]{1,0:T(8,128)S(1)} collective-permute-done((f32[32,512]{1,0:T(8,128)S(1)}, f32[32,512]{1,0:T(8,128)S(1)}, u32[]{:S(2)}, u32[]{:S(2)}) %collective-permute-start.11) | collective-permute-done | bytes 65568 | tf_op jit(solution)/shard_map/ppermute | solution.py:162
  28.8 1.2 %collective-permute-start.12 = (f32[64,512]{1,0:T(8,128)S(1)}, f32[64,512]{1,0:T(8,128)S(1)}, u32[]{:S(2)}, u32[]{:S(2)}) collective-permute-start(f32[64,512]{1,0:T(8,128)S(1)} %pad_maximum_fusion.1.refs_2_), channel_id=1, source_target_pairs={{0,2},{1,3},{2,0},{3,1},{4,6},{5,7},{6,4},{7,5},{8,10},{9,11},{10,... | collective-permute-start | bytes 393224 | tf_op jit(solution)/shard_map/ppermute | solution.py:162
  30.0 0.0 collective-permute-done.5
  30.0 1.6 %collective-permute-start.6 = (f32[64,512]{1,0:T(8,128)S(1)}, f32[64,512]{1,0:T(8,128)S(1)}, u32[]{:S(2)}, u32[]{:S(2)}) collective-permute-start(f32[64,512]{1,0:T(8,128)S(1)} %pad_maximum_fusion.refs_0_), channel_id=1, source_target_pairs={{0,16},{1,17},{2,18},{3,19},{4,20},{5,21},{6,22},{7,23},{8,24},{9,... | collective-permute-start | bytes 393224 | tf_op jit(solution)/shard_map/ppermute | solution.py:162
  31.7 0.5 %collective-permute-start.13 = (f32[64,512]{1,0:T(8,128)S(1)}, f32[64,512]{1,0:T(8,128)S(1)}, u32[]{:S(2)}, u32[]{:S(2)}) collective-permute-start(f32[64,512]{1,0:T(8,128)S(1)} %pad_maximum_fusion.refs_0_), channel_id=1, source_target_pairs={{0,1},{1,0},{2,3},{3,2},{4,5},{5,4},{6,7},{7,6},{8,9},{9,8},{10,11... | collective-permute-start | bytes 393224 | tf_op jit(solution)/shard_map/ppermute | solution.py:162
  32.2 1.7 %collective-permute-done.12.refs_3_ = f32[64,512]{1,0:T(8,128)S(1)} collective-permute-done((f32[64,512]{1,0:T(8,128)S(1)}, f32[64,512]{1,0:T(8,128)S(1)}, u32[]{:S(2)}, u32[]{:S(2)}) %collective-permute-start.12) | collective-permute-done | bytes 131104 | tf_op jit(solution)/shard_map/ppermute | solution.py:162
  33.9 0.0 collective-permute-start.16
  33.9 1.2 %collective-permute-done.6.refs_1_ = f32[64,512]{1,0:T(8,128)S(1)} collective-permute-done((f32[64,512]{1,0:T(8,128)S(1)}, f32[64,512]{1,0:T(8,128)S(1)}, u32[]{:S(2)}, u32[]{:S(2)}) %collective-permute-start.6) | collective-permute-done | bytes 131104 | tf_op jit(solution)/shard_map/ppermute | solution.py:162
  35.1 0.1 pad_add_fusion.place_ref
  35.1 0.1 collective-permute-done.16.refs_7_
  35.2 1.2 %collective-permute-done.14.refs_5_ = f32[64,512]{1,0:T(8,128)S(1)} collective-permute-done((f32[64,512]{1,0:T(8,128)S(1)}, f32[64,512]{1,0:T(8,128)S(1)}, u32[]{:S(2)}, u32[]{:S(2)}) %collective-permute-start.14) | collective-permute-done | bytes 131104 | tf_op jit(solution)/shard_map/ppermute | solution.py:162
  36.4 5.9 %finish.1 = (f32[450,256]{1,0:T(8,128)}, bf16[256,1024]{1,0:T(8,128)(2,1)}) custom-call(s32[4]{0:T(128)S(1)} %pad_add_fusion.place_ref, bf16[512,1024]{1,0:T(8,128)(2,1)S(1)} %get-tuple-element.6.padded_ref.data_ref, f32[64,512]{1,0:T(8,128)S(1)} %pad_maximum_fusion.refs_0_, f32[64,512]{1,0:T(8,128)S(1)} %collective-permute-done.6.refs_1_, ...), custom_call_target="tpu_custom_call" | custom-call | tf_op jit(solution)/shard_map/finish/pallas_call | solution.py:249
  (23 shorter events, 0.3 us)
Async XLA Ops:
  2.4 1.7 %collective-permute-start = (f32[128,512]{1,0:T(8,128)S(1)}, f32[128,512]{1,0:T(8,128)S(1)}, u32[]{:S(2)}, u32[]{:S(2)}) collective-permute-start(f32[128,512]{1,0:T(8,128)S(1)} %constant_dynamic-slice_fusion.5), channel_id=1, source_target_pairs={{0,1},{1,0},{2,3},{3,2},{4,5},{5,4},{6,7},{7,6},{8,9},{9,8},{10,11... | collective-permute-start | bytes 786440 | tf_op jit(solution)/shard_map/ppermute | solution.py:162
  3.7 3.4 %collective-permute-start.7 = (f32[128,512]{1,0:T(8,128)S(1)}, f32[128,512]{1,0:T(8,128)S(1)}, u32[]{:S(2)}, u32[]{:S(2)}) collective-permute-start(f32[128,512]{1,0:T(8,128)S(1)} %constant_dynamic-slice_fusion.2), channel_id=1, source_target_pairs={{0,1},{1,0},{2,3},{3,2},{4,5},{5,4},{6,7},{7,6},{8,9},{9,8},{10,11... | collective-permute-start | bytes 786440 | tf_op jit(solution)/shard_map/ppermute | solution.py:162
  4.2 6.7 %collective-permute-start.1 = (f32[64,512]{1,0:T(8,128)S(1)}, f32[64,512]{1,0:T(8,128)S(1)}, u32[]{:S(2)}, u32[]{:S(2)}) collective-permute-start(f32[64,512]{1,0:T(8,128)S(1)} %constant_dynamic-slice_fusion.4), channel_id=1, source_target_pairs={{0,16},{1,17},{2,18},{3,19},{4,20},{5,21},{6,22},{7,23},{8,24},{9,... | collective-permute-start | bytes 393224 | tf_op jit(solution)/shard_map/ppermute | solution.py:162
  7.2 5.6 %collective-permute-start.8 = (f32[64,512]{1,0:T(8,128)S(1)}, f32[64,512]{1,0:T(8,128)S(1)}, u32[]{:S(2)}, u32[]{:S(2)}) collective-permute-start(f32[64,512]{1,0:T(8,128)S(1)} %constant_dynamic-slice_fusion.1), channel_id=1, source_target_pairs={{0,2},{1,3},{2,0},{3,1},{4,6},{5,7},{6,4},{7,5},{8,10},{9,11},{10,... | collective-permute-start | bytes 393224 | tf_op jit(solution)/shard_map/ppermute | solution.py:162
  10.9 4.3 %collective-permute-start.2 = (f32[32,512]{1,0:T(8,128)S(1)}, f32[32,512]{1,0:T(8,128)S(1)}, u32[]{:S(2)}, u32[]{:S(2)}) collective-permute-start(f32[32,512]{1,0:T(8,128)S(1)} %constant_dynamic-slice_fusion.3), channel_id=1, source_target_pairs={{0,2},{1,3},{2,0},{3,1},{4,6},{5,7},{6,4},{7,5},{8,10},{9,11},{10,... | collective-permute-start | bytes 196616 | tf_op jit(solution)/shard_map/ppermute | solution.py:162
  12.8 5.0 %collective-permute-start.9 = (f32[32,512]{1,0:T(8,128)S(1)}, f32[32,512]{1,0:T(8,128)S(1)}, u32[]{:S(2)}, u32[]{:S(2)}) collective-permute-start(f32[32,512]{1,0:T(8,128)S(1)} %constant_dynamic-slice_fusion), channel_id=1, source_target_pairs={{0,4},{1,5},{2,6},{3,7},{4,0},{5,1},{6,2},{7,3},{8,12},{9,13},{10,... | collective-permute-start | bytes 196616 | tf_op jit(solution)/shard_map/ppermute | solution.py:162
  15.3 5.1 %collective-permute-start.3 = (f32[32,512]{1,0:T(8,128)S(1)}, f32[32,512]{1,0:T(8,128)S(1)}, u32[]{:S(2)}, u32[]{:S(2)}) collective-permute-start(f32[32,512]{1,0:T(8,128)S(1)} %dynamic-slice_add_fusion.5), channel_id=1, source_target_pairs={{0,4},{1,5},{2,6},{3,7},{4,0},{5,1},{6,2},{7,3},{8,12},{9,13},{10,... | collective-permute-start | bytes 196616 | tf_op jit(solution)/shard_map/ppermute | solution.py:162
  17.8 6.6 %collective-permute-start.10 = (f32[32,512]{1,0:T(8,128)S(1)}, f32[32,512]{1,0:T(8,128)S(1)}, u32[]{:S(2)}, u32[]{:S(2)}) collective-permute-start(f32[32,512]{1,0:T(8,128)S(1)} %dynamic-slice_add_fusion.4), channel_id=1, source_target_pairs={{0,8},{1,9},{2,10},{3,11},{4,12},{5,13},{6,14},{7,15},{8,0},{9,1},... | collective-permute-start | bytes 196616 | tf_op jit(solution)/shard_map/ppermute | solution.py:162
  20.4 5.2 %collective-permute-start.4 = (f32[32,512]{1,0:T(8,128)S(1)}, f32[32,512]{1,0:T(8,128)S(1)}, u32[]{:S(2)}, u32[]{:S(2)}) collective-permute-start(f32[32,512]{1,0:T(8,128)S(1)} %add.72), channel_id=1, source_target_pairs={{0,8},{1,9},{2,10},{3,11},{4,12},{5,13},{6,14},{7,15},{8,0},{9,1},... | collective-permute-start | bytes 196616 | tf_op jit(solution)/shard_map/ppermute | solution.py:162
  24.5 4.3 %collective-permute-start.11 = (f32[32,512]{1,0:T(8,128)S(1)}, f32[32,512]{1,0:T(8,128)S(1)}, u32[]{:S(2)}, u32[]{:S(2)}) collective-permute-start(f32[32,512]{1,0:T(8,128)S(1)} %add.81), channel_id=1, source_target_pairs={{0,4},{1,5},{2,6},{3,7},{4,0},{5,1},{6,2},{7,3},{8,12},{9,13},{10,... | collective-permute-start | bytes 196616 | tf_op jit(solution)/shard_map/ppermute | solution.py:162
  25.7 4.3 %collective-permute-start.5 = (f32[32,512]{1,0:T(8,128)S(1)}, f32[32,512]{1,0:T(8,128)S(1)}, u32[]{:S(2)}, u32[]{:S(2)}) collective-permute-start(f32[32,512]{1,0:T(8,128)S(1)} %add.73), channel_id=1, source_target_pairs={{0,2},{1,3},{2,0},{3,1},{4,6},{5,7},{6,4},{7,5},{8,10},{9,11},{10,... | collective-permute-start | bytes 196616 | tf_op jit(solution)/shard_map/ppermute | solution.py:162
  28.8 5.0 %collective-permute-start.12 = (f32[64,512]{1,0:T(8,128)S(1)}, f32[64,512]{1,0:T(8,128)S(1)}, u32[]{:S(2)}, u32[]{:S(2)}) collective-permute-start(f32[64,512]{1,0:T(8,128)S(1)} %pad_maximum_fusion.1.refs_2_), channel_id=1, source_target_pairs={{0,2},{1,3},{2,0},{3,1},{4,6},{5,7},{6,4},{7,5},{8,10},{9,11},{10,... | collective-permute-start | bytes 393224 | tf_op jit(solution)/shard_map/ppermute | solution.py:162
  30.0 5.0 %collective-permute-start.6 = (f32[64,512]{1,0:T(8,128)S(1)}, f32[64,512]{1,0:T(8,128)S(1)}, u32[]{:S(2)}, u32[]{:S(2)}) collective-permute-start(f32[64,512]{1,0:T(8,128)S(1)} %pad_maximum_fusion.refs_0_), channel_id=1, source_target_pairs={{0,16},{1,17},{2,18},{3,19},{4,20},{5,21},{6,22},{7,23},{8,24},{9,... | collective-permute-start | bytes 393224 | tf_op jit(solution)/shard_map/ppermute | solution.py:162
  31.7 3.5 %collective-permute-start.15 = (f32[64,512]{1,0:T(8,128)S(1)}, f32[64,512]{1,0:T(8,128)S(1)}, u32[]{:S(2)}, u32[]{:S(2)}) collective-permute-start(f32[64,512]{1,0:T(8,128)S(1)} %pad_maximum_fusion.1.refs_2_), channel_id=1, source_target_pairs={{0,1},{1,0},{2,3},{3,2},{4,5},{5,4},{6,7},{7,6},{8,9},{9,8},{10,11... | collective-permute-start | bytes 393224 | tf_op jit(solution)/shard_map/ppermute | solution.py:162
  31.7 3.5 %collective-permute-start.13 = (f32[64,512]{1,0:T(8,128)S(1)}, f32[64,512]{1,0:T(8,128)S(1)}, u32[]{:S(2)}, u32[]{:S(2)}) collective-permute-start(f32[64,512]{1,0:T(8,128)S(1)} %pad_maximum_fusion.refs_0_), channel_id=1, source_target_pairs={{0,1},{1,0},{2,3},{3,2},{4,5},{5,4},{6,7},{7,6},{8,9},{9,8},{10,11... | collective-permute-start | bytes 393224 | tf_op jit(solution)/shard_map/ppermute | solution.py:162
  33.9 1.3 %collective-permute-start.16 = (f32[64,512]{1,0:T(8,128)S(1)}, f32[64,512]{1,0:T(8,128)S(1)}, u32[]{:S(2)}, u32[]{:S(2)}) collective-permute-start(f32[64,512]{1,0:T(8,128)S(1)} %collective-permute-done.12.refs_3_), channel_id=1, source_target_pairs={{0,1},{1,0},{2,3},{3,2},{4,5},{5,4},{6,7},{7,6},{8,9},{9,8},{10,11... | collective-permute-start | bytes 393224 | tf_op jit(solution)/shard_map/ppermute | solution.py:162
  35.1 1.3 %collective-permute-start.14 = (f32[64,512]{1,0:T(8,128)S(1)}, f32[64,512]{1,0:T(8,128)S(1)}, u32[]{:S(2)}, u32[]{:S(2)}) collective-permute-start(f32[64,512]{1,0:T(8,128)S(1)} %collective-permute-done.6.refs_1_), channel_id=1, source_target_pairs={{0,1},{1,0},{2,3},{3,2},{4,5},{5,4},{6,7},{7,6},{8,9},{9,8},{10,11... | collective-permute-start | bytes 393224 | tf_op jit(solution)/shard_map/ppermute | solution.py:162

commit v6 on v5

--- a/solution.py
+++ b/solution.py
@@ -71,21 +71,61 @@
     square_ref[:, comps:] = jnp.where(col == times - comps, diagonal, upper[:, comps:])
 
 
-def finish_kernel(times, people, chunk, place_ref, data_ref, *refs):
-    pieces, (response_ref, maps_ref, total, packed, turned, new, sems) = refs[:8], refs[8:]
+def dot2(a, high, low):
+    return dot(a, high) + dot(a, low)
+
+
+def gram_terms(signal, high_ref, low_ref):
+    comps = high_ref.shape[1]
+    first, second = signal[:, 0:comps], signal[:, comps:]
+    left = dot2(first, high_ref[0], low_ref[0])
+    right = dot2(first, high_ref[1], low_ref[1]) + dot2(second, high_ref[2], low_ref[2])
+    return left, right
+
+
+def unpack_kernel(times, people, chunk, place_ref, *refs):
+    pieces, own, (high_ref, low_ref, terms_ref, packed, mine) = refs[:4], refs[4:6], refs[6:]
+    comps, full = packed.shape
+    half = comps // 2
+    quarter, eighth = half // 2, half // 4
+    core, spot, side, level = place_ref[0], place_ref[1], place_ref[2], place_ref[3]
+    for which, parts in ((core, pieces[0:2]), (1 - core, pieces[2:4])):
+        for d in range(4):
+            at = which * half + (side ^ (d >> 1)) * quarter + (level ^ (d & 1)) * eighth
+            piece = parts[d >> 1][(d & 1) * eighth : (d & 1) * eighth + eighth, :]
+            packed[pl.ds(pl.multiple_of(at, 8), eighth), :] = piece
+    for d in range(half // chunk):
+        piece = own[d * chunk // quarter][d * chunk % quarter : d * chunk % quarter + chunk, :]
+        mine[pl.ds(pl.multiple_of((spot ^ d) * chunk, 8), chunk), :] = piece
+    row, col = grid_of(comps, comps)
+    corner, beside = packed[:, 0:comps], packed[:, comps:]
+    last = jnp.sum(jnp.where(col == times - comps, beside, 0.0), axis=1, keepdims=True)
+    u11 = jnp.where(col > row, corner, jnp.where(col == row, 0.5 * corner, 0.0))
+    u22 = jnp.where(col < row, corner, jnp.where(col == row, 0.5 * last, 0.0))
+    u12 = jnp.where(col < times - comps, beside, 0.0)
+    for k, part in enumerate((u11, u12, u22)):
+        high_ref[k], low_ref[k] = split(part)
+    signal = (mine[...] / people).astype(jnp.bfloat16)
+    terms_ref[:, 0:comps], terms_ref[:, comps:] = gram_terms(signal, high_ref, low_ref)
+
+
+def finish_kernel(times, people, chunk, place_ref, data_ref, high_ref, low_ref, terms_ref, *refs):
+    pieces, (response_ref, maps_ref, total, terms, turned, new, sems) = refs[:4], refs[4:]
     comps, full = total.shape
     half, block = comps // 2, full // 2
-    quarter, eighth = half // 2, half // 4
-    core, spot, side, level = place_ref[0], place_ref[1], place_ref[2], place_ref[3]
-    for which, parts in ((core, pieces[0:4]), (1 - core, pieces[4:8])):
+    quarter = half // 2
+    core, spot = place_ref[0], place_ref[1]
+    for which, parts in ((core, pieces[0:2]), (1 - core, pieces[2:4])):
         for d in range(half // chunk):
             at = which * half + (spot ^ d) * chunk
             piece = parts[d * chunk // quarter][d * chunk % quarter : d * chunk % quarter + chunk, :]
             total[pl.ds(pl.multiple_of(at, 8), chunk), :] = piece
-        for d in range(4):
-            at = which * half + (side ^ (d >> 1)) * quarter + (level ^ (d & 1)) * eighth
-            piece = parts[2 + (d >> 1)][(d & 1) * eighth : (d & 1) * eighth + eighth, :]
-            packed[pl.ds(pl.multiple_of(at, 8), eighth), :] = piece
+    mine, theirs = pl.multiple_of(core * half, 8), pl.multiple_of((1 - core) * half, 8)
+    terms[pl.ds(mine, half), :] = terms_ref[...]
+    signal = (total[pl.ds(theirs, half), :] / people).astype(jnp.bfloat16)
+    left, right = gram_terms(signal, high_ref, low_ref)
+    terms[pl.ds(theirs, half), 0:block] = left
+    terms[pl.ds(theirs, half), block:] = right
     response = total[...] / people
 
     def turn(k):
@@ -94,20 +134,7 @@
 
     signal = response.astype(jnp.bfloat16)
     first, second = signal[:, 0:block], signal[:, block:]
-    row, col = grid_of(comps, block)
-    corner = packed[:, 0:block]
-    beside = packed[:, block:]
-    last = jnp.sum(jnp.where(col == times - block, beside, 0.0), axis=1, keepdims=True)
-    u11 = jnp.where(col > row, corner, jnp.where(col == row, 0.5 * corner, 0.0))
-    u22 = jnp.where(col < row, corner, jnp.where(col == row, 0.5 * last, 0.0))
-    u12 = jnp.where(col < times - block, beside, 0.0)
-
-    def dot2(a, b):
-        high, low = split(b)
-        return dot(a, high) + dot(a, low)
-
-    left = dot2(first, u11)
-    right = dot2(first, u12) + dot2(second, u22)
+    left, right = terms[:, 0:block], terms[:, block:]
     lh, ll = split(left)
     rh, rl = split(right)
     product = (dot_nt(lh, first) + dot_nt(ll, first)) + (dot_nt(rh, second) + dot_nt(rl, second))
@@ -243,8 +270,19 @@
         step *= 2
     square = jnp.concatenate([square, swap(square, subj_step=0, vox_step=4)], 0)
     squares = [square, over_side(square)]
-    pieces = responses + squares
-    pieces += [over_core(piece) for piece in pieces]
+    own = list(responses)
+    responses += [over_core(piece) for piece in responses]
+    squares += [over_core(piece) for piece in squares]
+    halves = pl.pallas_call(
+        functools.partial(unpack_kernel, times, people, chunk),
+        out_shape=[jax.ShapeDtypeStruct((3, comps, comps), jnp.bfloat16)] * 2
+        + [jax.ShapeDtypeStruct((half, full), jnp.float32)],
+        in_specs=[smem] + [vmem] * (len(squares) + 2),
+        out_specs=[vmem] * 3,
+        scratch_shapes=[pltpu.VMEM((comps, full), jnp.float32), pltpu.VMEM((half, full), jnp.float32)],
+        compiler_params=params,
+        name="unpack",
+    )(place, *squares, *own)
 
     response, new_maps = pl.pallas_call(
         functools.partial(finish_kernel, times, people, chunk),
@@ -252,7 +290,7 @@
             jax.ShapeDtypeStruct((times, comps), jnp.float32),
             jax.ShapeDtypeStruct((comps, wide), jnp.bfloat16),
         ],
-        in_specs=[smem, vmem] + [vmem] * len(pieces),
+        in_specs=[smem] + [vmem] * (4 + len(responses)),
         out_specs=[whole, whole],
         scratch_shapes=[
             pltpu.VMEM((comps, full), jnp.float32),
@@ -263,7 +301,7 @@
         ],
         compiler_params=params,
         name="finish",
-    )(place, padded, *pieces)
+    )(place, padded, *halves, *responses)
     return response, new_maps[None]
 
 

time: 42.5 us -> 42.5 us (level)
  waiting for transfers between devices: 12.8 us -> 11.8 us
  Pallas kernels: 8.35 us -> 9.34 us
    ppermute x17, waiting for transfers between devices: 12.8 us -> 11.8 us  [exchange(): return lax.ppermute(value, AXES, pairs)]
    pallas_call x0 -> x1, Pallas kernels: none -> 0.97 us  [shards(): pl.pallas_call(functools.partial(unpack_kernel, times, people, chunk), ou...]
  transfers between devices with their start and end apart: 17 -> 17, of which waited for: 11 -> 11; matrix products, arithmetic and copies ran while one was open for 1% -> 1% of each run, Pallas kernels for 2% -> 4%
where the time goes in v6:
time: 42.5 us; the launch traced here: 42.4 us
  starting transfers between devices  20.1 us (47%)
  waiting for transfers between devices  11.8 us (28%)
  Pallas kernels  9.34 us (22%)
  between operations  0.77 us (2%)
    ppermute x17, starting transfers between devices, exchange(): return lax.ppermute(value, AXES, pairs)  20.1 us
    ppermute x17, waiting for transfers between devices, exchange(): return lax.ppermute(value, AXES, pairs)  11.8 us
    pallas_call x1, Pallas kernels, shards(): pl.pallas_call(functools.partial(finish_kernel, times, people, chunk), ou...  5.95 us
    pallas_call x1, Pallas kernels, shards(): pl.pallas_call(functools.partial(response_kernel, times), out_shape=[jax....  1.74 us
    pallas_call x1, Pallas kernels, shards(): pl.pallas_call(functools.partial(unpack_kernel, times, people, chunk), ou...  0.97 us
  transfers between devices with their start and end apart: 17, of which 11 were waited for; matrix products, arithmetic and copies ran while one was open for 1% of the time, Pallas kernels for 4%

profile of v6, /device:TPU:0, one launch (start us, length us, event | category | flops | bytes accessed | tf_op | source)
XLA Modules:
  0.0 42.4 jit_solution(3447161241007540358)
XLA Ops:
  0.6 1.7 %response_terms.1 = (f32[256,512]{1,0:T(8,128)S(1)}, bf16[512,1024]{1,0:T(8,128)(2,1)S(1)}) custom-call(bf16[450,1024]{1,0:T(8,128)(2,1)} %bitcast.7, bf16[256,1024]{1,0:T(8,128)(2,1)} %bitcast.8), custom_call_target="tpu_custom_call" | custom-call | tf_op jit(solution)/shard_map/response_terms/pallas_call | solution.py:211
  2.4 0.5 %collective-permute-start.8 = (f32[128,512]{1,0:T(8,128)S(1)}, f32[128,512]{1,0:T(8,128)S(1)}, u32[]{:S(2)}, u32[]{:S(2)}) collective-permute-start(f32[128,512]{1,0:T(8,128)S(1)} %constant_dynamic-slice_fusion.2), channel_id=1, source_target_pairs={{0,1},{1,0},{2,3},{3,2},{4,5},{5,4},{6,7},{7,6},{8,9},{9,8},{10,11... | collective-permute-start | bytes 786440 | tf_op jit(solution)/shard_map/ppermute | solution.py:189
  2.9 0.7 %square_terms.1 = f32[256,512]{1,0:T(8,128)S(1)} custom-call(bf16[512,1024]{1,0:T(8,128)(2,1)S(1)} %get-tuple-element.9.padded_ref.data_ref), custom_call_target="tpu_custom_call" | custom-call | flops 402653184 | bytes 1048576 | tf_op jit(solution)/shard_map/square_terms/pallas_call | solution.py:227
  3.7 0.1 collective-permute-start
  3.8 0.3 collective-permute-done.8
  4.2 2.9 %collective-permute-start.9 = (f32[64,512]{1,0:T(8,128)S(1)}, f32[64,512]{1,0:T(8,128)S(1)}, u32[]{:S(2)}, u32[]{:S(2)}) collective-permute-start(f32[64,512]{1,0:T(8,128)S(1)} %constant_dynamic-slice_fusion.1), channel_id=1, source_target_pairs={{0,16},{1,17},{2,18},{3,19},{4,20},{5,21},{6,22},{7,23},{8,24},{9,... | collective-permute-start | bytes 393224 | tf_op jit(solution)/shard_map/ppermute | solution.py:189
  7.1 0.0 collective-permute-done
  7.2 1.6 %collective-permute-start.1 = (f32[64,512]{1,0:T(8,128)S(1)}, f32[64,512]{1,0:T(8,128)S(1)}, u32[]{:S(2)}, u32[]{:S(2)}) collective-permute-start(f32[64,512]{1,0:T(8,128)S(1)} %constant_dynamic-slice_fusion.4), channel_id=1, source_target_pairs={{0,2},{1,3},{2,0},{3,1},{4,6},{5,7},{6,4},{7,5},{8,10},{9,11},{10,... | collective-permute-start | bytes 393224 | tf_op jit(solution)/shard_map/ppermute | solution.py:189
  8.8 2.1 %collective-permute-done.9 = f32[64,512]{1,0:T(8,128)S(1)} collective-permute-done((f32[64,512]{1,0:T(8,128)S(1)}, f32[64,512]{1,0:T(8,128)S(1)}, u32[]{:S(2)}, u32[]{:S(2)}) %collective-permute-start.9) | collective-permute-done | bytes 131104 | tf_op jit(solution)/shard_map/ppermute | solution.py:189
  10.9 1.8 %collective-permute-start.10 = (f32[32,512]{1,0:T(8,128)S(1)}, f32[32,512]{1,0:T(8,128)S(1)}, u32[]{:S(2)}, u32[]{:S(2)}) collective-permute-start(f32[32,512]{1,0:T(8,128)S(1)} %constant_dynamic-slice_fusion), channel_id=1, source_target_pairs={{0,2},{1,3},{2,0},{3,1},{4,6},{5,7},{6,4},{7,5},{8,10},{9,11},{10,... | collective-permute-start | bytes 196616 | tf_op jit(solution)/shard_map/ppermute | solution.py:189
  12.8 1.6 %collective-permute-start.2 = (f32[32,512]{1,0:T(8,128)S(1)}, f32[32,512]{1,0:T(8,128)S(1)}, u32[]{:S(2)}, u32[]{:S(2)}) collective-permute-start(f32[32,512]{1,0:T(8,128)S(1)} %constant_dynamic-slice_fusion.3), channel_id=1, source_target_pairs={{0,4},{1,5},{2,6},{3,7},{4,0},{5,1},{6,2},{7,3},{8,12},{9,13},{10,... | collective-permute-start | bytes 196616 | tf_op jit(solution)/shard_map/ppermute | solution.py:189
  14.5 0.8 %collective-permute-done.10 = f32[32,512]{1,0:T(8,128)S(1)} collective-permute-done((f32[32,512]{1,0:T(8,128)S(1)}, f32[32,512]{1,0:T(8,128)S(1)}, u32[]{:S(2)}, u32[]{:S(2)}) %collective-permute-start.10) | collective-permute-done | bytes 65568 | tf_op jit(solution)/shard_map/ppermute | solution.py:189
  15.3 1.9 %collective-permute-start.11 = (f32[32,512]{1,0:T(8,128)S(1)}, f32[32,512]{1,0:T(8,128)S(1)}, u32[]{:S(2)}, u32[]{:S(2)}) collective-permute-start(f32[32,512]{1,0:T(8,128)S(1)} %dynamic-slice_add_fusion.4), channel_id=1, source_target_pairs={{0,4},{1,5},{2,6},{3,7},{4,0},{5,1},{6,2},{7,3},{8,12},{9,13},{10,... | collective-permute-start | bytes 196616 | tf_op jit(solution)/shard_map/ppermute | solution.py:189
  17.2 0.7 %collective-permute-done.2 = f32[32,512]{1,0:T(8,128)S(1)} collective-permute-done((f32[32,512]{1,0:T(8,128)S(1)}, f32[32,512]{1,0:T(8,128)S(1)}, u32[]{:S(2)}, u32[]{:S(2)}) %collective-permute-start.2) | collective-permute-done | bytes 65568 | tf_op jit(solution)/shard_map/ppermute | solution.py:189
  17.8 2.6 %collective-permute-start.3 = (f32[32,512]{1,0:T(8,128)S(1)}, f32[32,512]{1,0:T(8,128)S(1)}, u32[]{:S(2)}, u32[]{:S(2)}) collective-permute-start(f32[32,512]{1,0:T(8,128)S(1)} %dynamic-slice_add_fusion.5), channel_id=1, source_target_pairs={{0,8},{1,9},{2,10},{3,11},{4,12},{5,13},{6,14},{7,15},{8,0},{9,1},... | collective-permute-start | bytes 196616 | tf_op jit(solution)/shard_map/ppermute | solution.py:189
  20.4 2.1 %collective-permute-start.12 = (f32[32,512]{1,0:T(8,128)S(1)}, f32[32,512]{1,0:T(8,128)S(1)}, u32[]{:S(2)}, u32[]{:S(2)}) collective-permute-start(f32[32,512]{1,0:T(8,128)S(1)} %add.80), channel_id=1, source_target_pairs={{0,8},{1,9},{2,10},{3,11},{4,12},{5,13},{6,14},{7,15},{8,0},{9,1},... | collective-permute-start | bytes 196616 | tf_op jit(solution)/shard_map/ppermute | solution.py:189
  22.5 1.9 %collective-permute-done.3 = f32[32,512]{1,0:T(8,128)S(1)} collective-permute-done((f32[32,512]{1,0:T(8,128)S(1)}, f32[32,512]{1,0:T(8,128)S(1)}, u32[]{:S(2)}, u32[]{:S(2)}) %collective-permute-start.3) | collective-permute-done | bytes 65568 | tf_op jit(solution)/shard_map/ppermute | solution.py:189
  24.5 0.4 %collective-permute-start.4 = (f32[32,512]{1,0:T(8,128)S(1)}, f32[32,512]{1,0:T(8,128)S(1)}, u32[]{:S(2)}, u32[]{:S(2)}) collective-permute-start(f32[32,512]{1,0:T(8,128)S(1)} %add.72), channel_id=1, source_target_pairs={{0,4},{1,5},{2,6},{3,7},{4,0},{5,1},{6,2},{7,3},{8,12},{9,13},{10,... | collective-permute-start | bytes 196616 | tf_op jit(solution)/shard_map/ppermute | solution.py:189
  24.9 0.8 %collective-permute-done.12 = f32[32,512]{1,0:T(8,128)S(1)} collective-permute-done((f32[32,512]{1,0:T(8,128)S(1)}, f32[32,512]{1,0:T(8,128)S(1)}, u32[]{:S(2)}, u32[]{:S(2)}) %collective-permute-start.12) | collective-permute-done | bytes 65568 | tf_op jit(solution)/shard_map/ppermute | solution.py:189
  25.7 1.2 %collective-permute-start.13 = (f32[32,512]{1,0:T(8,128)S(1)}, f32[32,512]{1,0:T(8,128)S(1)}, u32[]{:S(2)}, u32[]{:S(2)}) collective-permute-start(f32[32,512]{1,0:T(8,128)S(1)} %add.81), channel_id=1, source_target_pairs={{0,2},{1,3},{2,0},{3,1},{4,6},{5,7},{6,4},{7,5},{8,10},{9,11},{10,... | collective-permute-start | bytes 196616 | tf_op jit(solution)/shard_map/ppermute | solution.py:189
  26.9 1.9 %collective-permute-done.4 = f32[32,512]{1,0:T(8,128)S(1)} collective-permute-done((f32[32,512]{1,0:T(8,128)S(1)}, f32[32,512]{1,0:T(8,128)S(1)}, u32[]{:S(2)}, u32[]{:S(2)}) %collective-permute-start.4) | collective-permute-done | bytes 65568 | tf_op jit(solution)/shard_map/ppermute | solution.py:189
  28.8 1.2 %collective-permute-start.5 = (f32[64,512]{1,0:T(8,128)S(1)}, f32[64,512]{1,0:T(8,128)S(1)}, u32[]{:S(2)}, u32[]{:S(2)}) collective-permute-start(f32[64,512]{1,0:T(8,128)S(1)} %pad_maximum_fusion.refs_0_), channel_id=1, source_target_pairs={{0,2},{1,3},{2,0},{3,1},{4,6},{5,7},{6,4},{7,5},{8,10},{9,11},{10,... | collective-permute-start | bytes 393224 | tf_op jit(solution)/shard_map/ppermute | solution.py:189
  30.0 0.0 collective-permute-done.13
  30.0 1.6 %collective-permute-start.14 = (f32[64,512]{1,0:T(8,128)S(1)}, f32[64,512]{1,0:T(8,128)S(1)}, u32[]{:S(2)}, u32[]{:S(2)}) collective-permute-start(f32[64,512]{1,0:T(8,128)S(1)} %pad_maximum_fusion.1.refs_4_.refs_0_), channel_id=1, source_target_pairs={{0,16},{1,17},{2,18},{3,19},{4,20},{5,21},{6,22},{7,23},{8,24},{9,... | collective-permute-start | bytes 393224 | tf_op jit(solution)/shard_map/ppermute | solution.py:189
  31.7 2.2 %collective-permute-done.5.refs_1_ = f32[64,512]{1,0:T(8,128)S(1)} collective-permute-done((f32[64,512]{1,0:T(8,128)S(1)}, f32[64,512]{1,0:T(8,128)S(1)}, u32[]{:S(2)}, u32[]{:S(2)}) %collective-permute-start.5) | collective-permute-done | bytes 131104 | tf_op jit(solution)/shard_map/ppermute | solution.py:189
  33.9 0.5 %collective-permute-start.15 = (f32[64,512]{1,0:T(8,128)S(1)}, f32[64,512]{1,0:T(8,128)S(1)}, u32[]{:S(2)}, u32[]{:S(2)}) collective-permute-start(f32[64,512]{1,0:T(8,128)S(1)} %pad_maximum_fusion.1.refs_4_.refs_0_), channel_id=1, source_target_pairs={{0,1},{1,0},{2,3},{3,2},{4,5},{5,4},{6,7},{7,6},{8,9},{9,8},{10,11... | collective-permute-start | bytes 393224 | tf_op jit(solution)/shard_map/ppermute | solution.py:189
  34.4 0.7 %collective-permute-done.14.refs_5_.refs_1_ = f32[64,512]{1,0:T(8,128)S(1)} collective-permute-done((f32[64,512]{1,0:T(8,128)S(1)}, f32[64,512]{1,0:T(8,128)S(1)}, u32[]{:S(2)}, u32[]{:S(2)}) %collective-permute-start.14) | collective-permute-done | bytes 131104 | tf_op jit(solution)/shard_map/ppermute | solution.py:189
  35.1 0.1 pad_add_fusion.place_ref
  35.1 0.1 collective-permute-done.7.refs_3_
  35.2 1.0 %unpack.1 = (bf16[3,256,256]{2,1,0:T(8,128)(2,1)S(1)}, bf16[3,256,256]{2,1,0:T(8,128)(2,1)S(1)}, f32[128,512]{1,0:T(8,128)S(1)}) custom-call(s32[4]{0:T(128)S(1)} %pad_add_fusion.place_ref, f32[64,512]{1,0:T(8,128)S(1)} %pad_maximum_fusion.refs_0_, f32[64,512]{1,0:T(8,128)S(1)} %collective-permute-done.5.refs_1_, ...), custom_call_target="tpu_custom_call" | custom-call | tf_op jit(solution)/shard_map/unpack/pallas_call | solution.py:276
  36.2 0.2 collective-permute-done.16.refs_3_
  36.4 6.0 %finish.1 = (f32[450,256]{1,0:T(8,128)}, bf16[256,1024]{1,0:T(8,128)(2,1)}) custom-call(s32[4]{0:T(128)S(1)} %pad_add_fusion.place_ref, bf16[512,1024]{1,0:T(8,128)(2,1)S(1)} %get-tuple-element.9.padded_ref.data_ref, bf16[3,256,256]{2,1,0:T(8,128)(2,1)S(1)} %get-tuple-element.11.high_ref, bf16[3,256,256]{2,1,0:T(8,128)(2,1)S(1)} %get-tuple-element.12.low_ref, ...), custom_call_target="tpu_custom_call" | custom-call | tf_op jit(solution)/shard_map/finish/pallas_call | solution.py:287
  (24 shorter events, 0.3 us)
Async XLA Ops:
  2.4 1.7 %collective-permute-start.8 = (f32[128,512]{1,0:T(8,128)S(1)}, f32[128,512]{1,0:T(8,128)S(1)}, u32[]{:S(2)}, u32[]{:S(2)}) collective-permute-start(f32[128,512]{1,0:T(8,128)S(1)} %constant_dynamic-slice_fusion.2), channel_id=1, source_target_pairs={{0,1},{1,0},{2,3},{3,2},{4,5},{5,4},{6,7},{7,6},{8,9},{9,8},{10,11... | collective-permute-start | bytes 786440 | tf_op jit(solution)/shard_map/ppermute | solution.py:189
  3.7 3.4 %collective-permute-start = (f32[128,512]{1,0:T(8,128)S(1)}, f32[128,512]{1,0:T(8,128)S(1)}, u32[]{:S(2)}, u32[]{:S(2)}) collective-permute-start(f32[128,512]{1,0:T(8,128)S(1)} %constant_dynamic-slice_fusion.5), channel_id=1, source_target_pairs={{0,1},{1,0},{2,3},{3,2},{4,5},{5,4},{6,7},{7,6},{8,9},{9,8},{10,11... | collective-permute-start | bytes 786440 | tf_op jit(solution)/shard_map/ppermute | solution.py:189
  4.2 6.7 %collective-permute-start.9 = (f32[64,512]{1,0:T(8,128)S(1)}, f32[64,512]{1,0:T(8,128)S(1)}, u32[]{:S(2)}, u32[]{:S(2)}) collective-permute-start(f32[64,512]{1,0:T(8,128)S(1)} %constant_dynamic-slice_fusion.1), channel_id=1, source_target_pairs={{0,16},{1,17},{2,18},{3,19},{4,20},{5,21},{6,22},{7,23},{8,24},{9,... | collective-permute-start | bytes 393224 | tf_op jit(solution)/shard_map/ppermute | solution.py:189
  7.2 5.6 %collective-permute-start.1 = (f32[64,512]{1,0:T(8,128)S(1)}, f32[64,512]{1,0:T(8,128)S(1)}, u32[]{:S(2)}, u32[]{:S(2)}) collective-permute-start(f32[64,512]{1,0:T(8,128)S(1)} %constant_dynamic-slice_fusion.4), channel_id=1, source_target_pairs={{0,2},{1,3},{2,0},{3,1},{4,6},{5,7},{6,4},{7,5},{8,10},{9,11},{10,... | collective-permute-start | bytes 393224 | tf_op jit(solution)/shard_map/ppermute | solution.py:189
  10.9 4.3 %collective-permute-start.10 = (f32[32,512]{1,0:T(8,128)S(1)}, f32[32,512]{1,0:T(8,128)S(1)}, u32[]{:S(2)}, u32[]{:S(2)}) collective-permute-start(f32[32,512]{1,0:T(8,128)S(1)} %constant_dynamic-slice_fusion), channel_id=1, source_target_pairs={{0,2},{1,3},{2,0},{3,1},{4,6},{5,7},{6,4},{7,5},{8,10},{9,11},{10,... | collective-permute-start | bytes 196616 | tf_op jit(solution)/shard_map/ppermute | solution.py:189
  12.8 5.0 %collective-permute-start.2 = (f32[32,512]{1,0:T(8,128)S(1)}, f32[32,512]{1,0:T(8,128)S(1)}, u32[]{:S(2)}, u32[]{:S(2)}) collective-permute-start(f32[32,512]{1,0:T(8,128)S(1)} %constant_dynamic-slice_fusion.3), channel_id=1, source_target_pairs={{0,4},{1,5},{2,6},{3,7},{4,0},{5,1},{6,2},{7,3},{8,12},{9,13},{10,... | collective-permute-start | bytes 196616 | tf_op jit(solution)/shard_map/ppermute | solution.py:189
  15.3 5.1 %collective-permute-start.11 = (f32[32,512]{1,0:T(8,128)S(1)}, f32[32,512]{1,0:T(8,128)S(1)}, u32[]{:S(2)}, u32[]{:S(2)}) collective-permute-start(f32[32,512]{1,0:T(8,128)S(1)} %dynamic-slice_add_fusion.4), channel_id=1, source_target_pairs={{0,4},{1,5},{2,6},{3,7},{4,0},{5,1},{6,2},{7,3},{8,12},{9,13},{10,... | collective-permute-start | bytes 196616 | tf_op jit(solution)/shard_map/ppermute | solution.py:189
  17.8 6.6 %collective-permute-start.3 = (f32[32,512]{1,0:T(8,128)S(1)}, f32[32,512]{1,0:T(8,128)S(1)}, u32[]{:S(2)}, u32[]{:S(2)}) collective-permute-start(f32[32,512]{1,0:T(8,128)S(1)} %dynamic-slice_add_fusion.5), channel_id=1, source_target_pairs={{0,8},{1,9},{2,10},{3,11},{4,12},{5,13},{6,14},{7,15},{8,0},{9,1},... | collective-permute-start | bytes 196616 | tf_op jit(solution)/shard_map/ppermute | solution.py:189
  20.4 5.2 %collective-permute-start.12 = (f32[32,512]{1,0:T(8,128)S(1)}, f32[32,512]{1,0:T(8,128)S(1)}, u32[]{:S(2)}, u32[]{:S(2)}) collective-permute-start(f32[32,512]{1,0:T(8,128)S(1)} %add.80), channel_id=1, source_target_pairs={{0,8},{1,9},{2,10},{3,11},{4,12},{5,13},{6,14},{7,15},{8,0},{9,1},... | collective-permute-start | bytes 196616 | tf_op jit(solution)/shard_map/ppermute | solution.py:189
  24.5 4.3 %collective-permute-start.4 = (f32[32,512]{1,0:T(8,128)S(1)}, f32[32,512]{1,0:T(8,128)S(1)}, u32[]{:S(2)}, u32[]{:S(2)}) collective-permute-start(f32[32,512]{1,0:T(8,128)S(1)} %add.72), channel_id=1, source_target_pairs={{0,4},{1,5},{2,6},{3,7},{4,0},{5,1},{6,2},{7,3},{8,12},{9,13},{10,... | collective-permute-start | bytes 196616 | tf_op jit(solution)/shard_map/ppermute | solution.py:189
  25.7 4.3 %collective-permute-start.13 = (f32[32,512]{1,0:T(8,128)S(1)}, f32[32,512]{1,0:T(8,128)S(1)}, u32[]{:S(2)}, u32[]{:S(2)}) collective-permute-start(f32[32,512]{1,0:T(8,128)S(1)} %add.81), channel_id=1, source_target_pairs={{0,2},{1,3},{2,0},{3,1},{4,6},{5,7},{6,4},{7,5},{8,10},{9,11},{10,... | collective-permute-start | bytes 196616 | tf_op jit(solution)/shard_map/ppermute | solution.py:189
  28.8 5.0 %collective-permute-start.5 = (f32[64,512]{1,0:T(8,128)S(1)}, f32[64,512]{1,0:T(8,128)S(1)}, u32[]{:S(2)}, u32[]{:S(2)}) collective-permute-start(f32[64,512]{1,0:T(8,128)S(1)} %pad_maximum_fusion.refs_0_), channel_id=1, source_target_pairs={{0,2},{1,3},{2,0},{3,1},{4,6},{5,7},{6,4},{7,5},{8,10},{9,11},{10,... | collective-permute-start | bytes 393224 | tf_op jit(solution)/shard_map/ppermute | solution.py:189
  30.0 5.0 %collective-permute-start.14 = (f32[64,512]{1,0:T(8,128)S(1)}, f32[64,512]{1,0:T(8,128)S(1)}, u32[]{:S(2)}, u32[]{:S(2)}) collective-permute-start(f32[64,512]{1,0:T(8,128)S(1)} %pad_maximum_fusion.1.refs_4_.refs_0_), channel_id=1, source_target_pairs={{0,16},{1,17},{2,18},{3,19},{4,20},{5,21},{6,22},{7,23},{8,24},{9,... | collective-permute-start | bytes 393224 | tf_op jit(solution)/shard_map/ppermute | solution.py:189
  31.7 3.5 %collective-permute-start.6 = (f32[64,512]{1,0:T(8,128)S(1)}, f32[64,512]{1,0:T(8,128)S(1)}, u32[]{:S(2)}, u32[]{:S(2)}) collective-permute-start(f32[64,512]{1,0:T(8,128)S(1)} %pad_maximum_fusion.refs_0_), channel_id=1, source_target_pairs={{0,1},{1,0},{2,3},{3,2},{4,5},{5,4},{6,7},{7,6},{8,9},{9,8},{10,11... | collective-permute-start | bytes 393224 | tf_op jit(solution)/shard_map/ppermute | solution.py:189
  33.9 1.3 %collective-permute-start.7 = (f32[64,512]{1,0:T(8,128)S(1)}, f32[64,512]{1,0:T(8,128)S(1)}, u32[]{:S(2)}, u32[]{:S(2)}) collective-permute-start(f32[64,512]{1,0:T(8,128)S(1)} %collective-permute-done.5.refs_1_), channel_id=1, source_target_pairs={{0,1},{1,0},{2,3},{3,2},{4,5},{5,4},{6,7},{7,6},{8,9},{9,8},{10,11... | collective-permute-start | bytes 393224 | tf_op jit(solution)/shard_map/ppermute | solution.py:189
  33.9 2.3 %collective-permute-start.15 = (f32[64,512]{1,0:T(8,128)S(1)}, f32[64,512]{1,0:T(8,128)S(1)}, u32[]{:S(2)}, u32[]{:S(2)}) collective-permute-start(f32[64,512]{1,0:T(8,128)S(1)} %pad_maximum_fusion.1.refs_4_.refs_0_), channel_id=1, source_target_pairs={{0,1},{1,0},{2,3},{3,2},{4,5},{5,4},{6,7},{7,6},{8,9},{9,8},{10,11... | collective-permute-start | bytes 393224 | tf_op jit(solution)/shard_map/ppermute | solution.py:189
  35.1 1.3 %collective-permute-start.16 = (f32[64,512]{1,0:T(8,128)S(1)}, f32[64,512]{1,0:T(8,128)S(1)}, u32[]{:S(2)}, u32[]{:S(2)}) collective-permute-start(f32[64,512]{1,0:T(8,128)S(1)} %collective-permute-done.14.refs_5_.refs_1_), channel_id=1, source_target_pairs={{0,1},{1,0},{2,3},{3,2},{4,5},{5,4},{6,7},{7,6},{8,9},{9,8},{10,11... | collective-permute-start | bytes 393224 | tf_op jit(solution)/shard_map/ppermute | solution.py:189

commit v7 on v5

--- a/solution.py
+++ b/solution.py
@@ -120,7 +120,7 @@
         inner = 1.6875 * diagonal - 0.5625 * t + 0.0625 * t2
         return 2.25 * diagonal - 2.4375 * t + dot3(t2, inner)
 
-    t = gram / scale
+    t = gram * (1.0 / scale)
     t2 = dot3(t, t)
     turn(0)
     first_two = two_steps(t, t2)
@@ -137,7 +137,7 @@
     answer = pltpu.make_async_copy(turned, response_ref, sems.at[0])
     answer.start()
     inverse = 1.5 * inverse - 0.5 * dot3(moved, cubed)
-    factor = inverse / jnp.sqrt(scale)
+    factor = inverse * (1.0 / jnp.sqrt(scale))
     fh, fl = split(factor)
     weights = dot(fh, signal) + dot(fl, signal)
     both = jnp.concatenate(split(weights), 0)

time: 42.5 us -> 42.5 us (level)
  no operation moved by 1% of the time
where the time goes in v7:
time: 42.5 us; the launch traced here: 42.4 us
  starting transfers between devices  20.1 us (47%)
  waiting for transfers between devices  12.8 us (30%)
  Pallas kernels  8.39 us (20%)
  between operations  0.75 us (2%)
    ppermute x17, starting transfers between devices, exchange(): return lax.ppermute(value, AXES, pairs)  20.1 us
    ppermute x17, waiting for transfers between devices, exchange(): return lax.ppermute(value, AXES, pairs)  12.8 us
    pallas_call x1, Pallas kernels, shards(): pl.pallas_call(functools.partial(finish_kernel, times, people, chunk), ou...  5.97 us
    pallas_call x1, Pallas kernels, shards(): pl.pallas_call(functools.partial(response_kernel, times), out_shape=[jax....  1.74 us
  transfers between devices with their start and end apart: 17, of which 11 were waited for; matrix products, arithmetic and copies ran while one was open for 1% of the time, Pallas kernels for 2%

profile of v7, /device:TPU:0, one launch (start us, length us, event | category | flops | bytes accessed | tf_op | source)
XLA Modules:
  0.0 42.4 jit_solution(8291039670712995181)
XLA Ops:
  0.6 1.7 %response_terms.1 = (f32[256,512]{1,0:T(8,128)S(1)}, bf16[512,1024]{1,0:T(8,128)(2,1)S(1)}) custom-call(bf16[450,1024]{1,0:T(8,128)(2,1)} %bitcast.7, bf16[256,1024]{1,0:T(8,128)(2,1)} %bitcast.8), custom_call_target="tpu_custom_call" | custom-call | tf_op jit(solution)/shard_map/response_terms/pallas_call | solution.py:184
  2.4 0.5 %collective-permute-start = (f32[128,512]{1,0:T(8,128)S(1)}, f32[128,512]{1,0:T(8,128)S(1)}, u32[]{:S(2)}, u32[]{:S(2)}) collective-permute-start(f32[128,512]{1,0:T(8,128)S(1)} %constant_dynamic-slice_fusion.5), channel_id=1, source_target_pairs={{0,1},{1,0},{2,3},{3,2},{4,5},{5,4},{6,7},{7,6},{8,9},{9,8},{10,11... | collective-permute-start | bytes 786440 | tf_op jit(solution)/shard_map/ppermute | solution.py:162
  2.9 0.7 %square_terms.1 = f32[256,512]{1,0:T(8,128)S(1)} custom-call(bf16[512,1024]{1,0:T(8,128)(2,1)S(1)} %get-tuple-element.6.padded_ref.data_ref), custom_call_target="tpu_custom_call" | custom-call | flops 402653184 | bytes 1048576 | tf_op jit(solution)/shard_map/square_terms/pallas_call | solution.py:200
  3.7 0.1 collective-permute-start.7
  3.8 0.3 collective-permute-done
  4.2 2.9 %collective-permute-start.1 = (f32[64,512]{1,0:T(8,128)S(1)}, f32[64,512]{1,0:T(8,128)S(1)}, u32[]{:S(2)}, u32[]{:S(2)}) collective-permute-start(f32[64,512]{1,0:T(8,128)S(1)} %constant_dynamic-slice_fusion.4), channel_id=1, source_target_pairs={{0,16},{1,17},{2,18},{3,19},{4,20},{5,21},{6,22},{7,23},{8,24},{9,... | collective-permute-start | bytes 393224 | tf_op jit(solution)/shard_map/ppermute | solution.py:162
  7.1 0.0 collective-permute-done.7
  7.2 1.6 %collective-permute-start.8 = (f32[64,512]{1,0:T(8,128)S(1)}, f32[64,512]{1,0:T(8,128)S(1)}, u32[]{:S(2)}, u32[]{:S(2)}) collective-permute-start(f32[64,512]{1,0:T(8,128)S(1)} %constant_dynamic-slice_fusion.1), channel_id=1, source_target_pairs={{0,2},{1,3},{2,0},{3,1},{4,6},{5,7},{6,4},{7,5},{8,10},{9,11},{10,... | collective-permute-start | bytes 393224 | tf_op jit(solution)/shard_map/ppermute | solution.py:162
  8.8 2.1 %collective-permute-done.1 = f32[64,512]{1,0:T(8,128)S(1)} collective-permute-done((f32[64,512]{1,0:T(8,128)S(1)}, f32[64,512]{1,0:T(8,128)S(1)}, u32[]{:S(2)}, u32[]{:S(2)}) %collective-permute-start.1) | collective-permute-done | bytes 131104 | tf_op jit(solution)/shard_map/ppermute | solution.py:162
  10.9 1.8 %collective-permute-start.2 = (f32[32,512]{1,0:T(8,128)S(1)}, f32[32,512]{1,0:T(8,128)S(1)}, u32[]{:S(2)}, u32[]{:S(2)}) collective-permute-start(f32[32,512]{1,0:T(8,128)S(1)} %constant_dynamic-slice_fusion.3), channel_id=1, source_target_pairs={{0,2},{1,3},{2,0},{3,1},{4,6},{5,7},{6,4},{7,5},{8,10},{9,11},{10,... | collective-permute-start | bytes 196616 | tf_op jit(solution)/shard_map/ppermute | solution.py:162
  12.8 0.0 collective-permute-done.8
  12.8 1.6 %collective-permute-start.9 = (f32[32,512]{1,0:T(8,128)S(1)}, f32[32,512]{1,0:T(8,128)S(1)}, u32[]{:S(2)}, u32[]{:S(2)}) collective-permute-start(f32[32,512]{1,0:T(8,128)S(1)} %constant_dynamic-slice_fusion), channel_id=1, source_target_pairs={{0,4},{1,5},{2,6},{3,7},{4,0},{5,1},{6,2},{7,3},{8,12},{9,13},{10,... | collective-permute-start | bytes 196616 | tf_op jit(solution)/shard_map/ppermute | solution.py:162
  14.5 0.8 %collective-permute-done.2 = f32[32,512]{1,0:T(8,128)S(1)} collective-permute-done((f32[32,512]{1,0:T(8,128)S(1)}, f32[32,512]{1,0:T(8,128)S(1)}, u32[]{:S(2)}, u32[]{:S(2)}) %collective-permute-start.2) | collective-permute-done | bytes 65568 | tf_op jit(solution)/shard_map/ppermute | solution.py:162
  15.3 1.9 %collective-permute-start.3 = (f32[32,512]{1,0:T(8,128)S(1)}, f32[32,512]{1,0:T(8,128)S(1)}, u32[]{:S(2)}, u32[]{:S(2)}) collective-permute-start(f32[32,512]{1,0:T(8,128)S(1)} %dynamic-slice_add_fusion.5), channel_id=1, source_target_pairs={{0,4},{1,5},{2,6},{3,7},{4,0},{5,1},{6,2},{7,3},{8,12},{9,13},{10,... | collective-permute-start | bytes 196616 | tf_op jit(solution)/shard_map/ppermute | solution.py:162
  17.2 0.7 %collective-permute-done.9 = f32[32,512]{1,0:T(8,128)S(1)} collective-permute-done((f32[32,512]{1,0:T(8,128)S(1)}, f32[32,512]{1,0:T(8,128)S(1)}, u32[]{:S(2)}, u32[]{:S(2)}) %collective-permute-start.9) | collective-permute-done | bytes 65568 | tf_op jit(solution)/shard_map/ppermute | solution.py:162
  17.8 2.6 %collective-permute-start.10 = (f32[32,512]{1,0:T(8,128)S(1)}, f32[32,512]{1,0:T(8,128)S(1)}, u32[]{:S(2)}, u32[]{:S(2)}) collective-permute-start(f32[32,512]{1,0:T(8,128)S(1)} %dynamic-slice_add_fusion.4), channel_id=1, source_target_pairs={{0,8},{1,9},{2,10},{3,11},{4,12},{5,13},{6,14},{7,15},{8,0},{9,1},... | collective-permute-start | bytes 196616 | tf_op jit(solution)/shard_map/ppermute | solution.py:162
  20.4 2.1 %collective-permute-start.4 = (f32[32,512]{1,0:T(8,128)S(1)}, f32[32,512]{1,0:T(8,128)S(1)}, u32[]{:S(2)}, u32[]{:S(2)}) collective-permute-start(f32[32,512]{1,0:T(8,128)S(1)} %add.72), channel_id=1, source_target_pairs={{0,8},{1,9},{2,10},{3,11},{4,12},{5,13},{6,14},{7,15},{8,0},{9,1},... | collective-permute-start | bytes 196616 | tf_op jit(solution)/shard_map/ppermute | solution.py:162
  22.5 1.9 %collective-permute-done.10 = f32[32,512]{1,0:T(8,128)S(1)} collective-permute-done((f32[32,512]{1,0:T(8,128)S(1)}, f32[32,512]{1,0:T(8,128)S(1)}, u32[]{:S(2)}, u32[]{:S(2)}) %collective-permute-start.10) | collective-permute-done | bytes 65568 | tf_op jit(solution)/shard_map/ppermute | solution.py:162
  24.5 0.4 %collective-permute-start.11 = (f32[32,512]{1,0:T(8,128)S(1)}, f32[32,512]{1,0:T(8,128)S(1)}, u32[]{:S(2)}, u32[]{:S(2)}) collective-permute-start(f32[32,512]{1,0:T(8,128)S(1)} %add.81), channel_id=1, source_target_pairs={{0,4},{1,5},{2,6},{3,7},{4,0},{5,1},{6,2},{7,3},{8,12},{9,13},{10,... | collective-permute-start | bytes 196616 | tf_op jit(solution)/shard_map/ppermute | solution.py:162
  24.9 0.8 %collective-permute-done.4 = f32[32,512]{1,0:T(8,128)S(1)} collective-permute-done((f32[32,512]{1,0:T(8,128)S(1)}, f32[32,512]{1,0:T(8,128)S(1)}, u32[]{:S(2)}, u32[]{:S(2)}) %collective-permute-start.4) | collective-permute-done | bytes 65568 | tf_op jit(solution)/shard_map/ppermute | solution.py:162
  25.7 1.2 %collective-permute-start.5 = (f32[32,512]{1,0:T(8,128)S(1)}, f32[32,512]{1,0:T(8,128)S(1)}, u32[]{:S(2)}, u32[]{:S(2)}) collective-permute-start(f32[32,512]{1,0:T(8,128)S(1)} %add.73), channel_id=1, source_target_pairs={{0,2},{1,3},{2,0},{3,1},{4,6},{5,7},{6,4},{7,5},{8,10},{9,11},{10,... | collective-permute-start | bytes 196616 | tf_op jit(solution)/shard_map/ppermute | solution.py:162
  26.9 1.9 %collective-permute-done.11 = f32[32,512]{1,0:T(8,128)S(1)} collective-permute-done((f32[32,512]{1,0:T(8,128)S(1)}, f32[32,512]{1,0:T(8,128)S(1)}, u32[]{:S(2)}, u32[]{:S(2)}) %collective-permute-start.11) | collective-permute-done | bytes 65568 | tf_op jit(solution)/shard_map/ppermute | solution.py:162
  28.8 1.2 %collective-permute-start.12 = (f32[64,512]{1,0:T(8,128)S(1)}, f32[64,512]{1,0:T(8,128)S(1)}, u32[]{:S(2)}, u32[]{:S(2)}) collective-permute-start(f32[64,512]{1,0:T(8,128)S(1)} %pad_maximum_fusion.1.refs_2_), channel_id=1, source_target_pairs={{0,2},{1,3},{2,0},{3,1},{4,6},{5,7},{6,4},{7,5},{8,10},{9,11},{10,... | collective-permute-start | bytes 393224 | tf_op jit(solution)/shard_map/ppermute | solution.py:162
  30.0 0.0 collective-permute-done.5
  30.0 1.6 %collective-permute-start.6 = (f32[64,512]{1,0:T(8,128)S(1)}, f32[64,512]{1,0:T(8,128)S(1)}, u32[]{:S(2)}, u32[]{:S(2)}) collective-permute-start(f32[64,512]{1,0:T(8,128)S(1)} %pad_maximum_fusion.refs_0_), channel_id=1, source_target_pairs={{0,16},{1,17},{2,18},{3,19},{4,20},{5,21},{6,22},{7,23},{8,24},{9,... | collective-permute-start | bytes 393224 | tf_op jit(solution)/shard_map/ppermute | solution.py:162
  31.7 0.5 %collective-permute-start.13 = (f32[64,512]{1,0:T(8,128)S(1)}, f32[64,512]{1,0:T(8,128)S(1)}, u32[]{:S(2)}, u32[]{:S(2)}) collective-permute-start(f32[64,512]{1,0:T(8,128)S(1)} %pad_maximum_fusion.refs_0_), channel_id=1, source_target_pairs={{0,1},{1,0},{2,3},{3,2},{4,5},{5,4},{6,7},{7,6},{8,9},{9,8},{10,11... | collective-permute-start | bytes 393224 | tf_op jit(solution)/shard_map/ppermute | solution.py:162
  32.2 1.7 %collective-permute-done.12.refs_3_ = f32[64,512]{1,0:T(8,128)S(1)} collective-permute-done((f32[64,512]{1,0:T(8,128)S(1)}, f32[64,512]{1,0:T(8,128)S(1)}, u32[]{:S(2)}, u32[]{:S(2)}) %collective-permute-start.12) | collective-permute-done | bytes 131104 | tf_op jit(solution)/shard_map/ppermute | solution.py:162
  33.9 1.2 %collective-permute-done.6.refs_1_ = f32[64,512]{1,0:T(8,128)S(1)} collective-permute-done((f32[64,512]{1,0:T(8,128)S(1)}, f32[64,512]{1,0:T(8,128)S(1)}, u32[]{:S(2)}, u32[]{:S(2)}) %collective-permute-start.6) | collective-permute-done | bytes 131104 | tf_op jit(solution)/shard_map/ppermute | solution.py:162
  35.1 0.1 pad_add_fusion.place_ref
  35.1 0.1 collective-permute-done.16.refs_7_
  35.2 1.2 %collective-permute-done.14.refs_5_ = f32[64,512]{1,0:T(8,128)S(1)} collective-permute-done((f32[64,512]{1,0:T(8,128)S(1)}, f32[64,512]{1,0:T(8,128)S(1)}, u32[]{:S(2)}, u32[]{:S(2)}) %collective-permute-start.14) | collective-permute-done | bytes 131104 | tf_op jit(solution)/shard_map/ppermute | solution.py:162
  36.4 6.0 %finish.1 = (f32[450,256]{1,0:T(8,128)}, bf16[256,1024]{1,0:T(8,128)(2,1)}) custom-call(s32[4]{0:T(128)S(1)} %pad_add_fusion.place_ref, bf16[512,1024]{1,0:T(8,128)(2,1)S(1)} %get-tuple-element.6.padded_ref.data_ref, f32[64,512]{1,0:T(8,128)S(1)} %pad_maximum_fusion.refs_0_, f32[64,512]{1,0:T(8,128)S(1)} %collective-permute-done.6.refs_1_, ...), custom_call_target="tpu_custom_call" | custom-call | tf_op jit(solution)/shard_map/finish/pallas_call | solution.py:249
  (23 shorter events, 0.3 us)
Async XLA Ops:
  2.4 1.7 %collective-permute-start = (f32[128,512]{1,0:T(8,128)S(1)}, f32[128,512]{1,0:T(8,128)S(1)}, u32[]{:S(2)}, u32[]{:S(2)}) collective-permute-start(f32[128,512]{1,0:T(8,128)S(1)} %constant_dynamic-slice_fusion.5), channel_id=1, source_target_pairs={{0,1},{1,0},{2,3},{3,2},{4,5},{5,4},{6,7},{7,6},{8,9},{9,8},{10,11... | collective-permute-start | bytes 786440 | tf_op jit(solution)/shard_map/ppermute | solution.py:162
  3.7 3.4 %collective-permute-start.7 = (f32[128,512]{1,0:T(8,128)S(1)}, f32[128,512]{1,0:T(8,128)S(1)}, u32[]{:S(2)}, u32[]{:S(2)}) collective-permute-start(f32[128,512]{1,0:T(8,128)S(1)} %constant_dynamic-slice_fusion.2), channel_id=1, source_target_pairs={{0,1},{1,0},{2,3},{3,2},{4,5},{5,4},{6,7},{7,6},{8,9},{9,8},{10,11... | collective-permute-start | bytes 786440 | tf_op jit(solution)/shard_map/ppermute | solution.py:162
  4.2 6.7 %collective-permute-start.1 = (f32[64,512]{1,0:T(8,128)S(1)}, f32[64,512]{1,0:T(8,128)S(1)}, u32[]{:S(2)}, u32[]{:S(2)}) collective-permute-start(f32[64,512]{1,0:T(8,128)S(1)} %constant_dynamic-slice_fusion.4), channel_id=1, source_target_pairs={{0,16},{1,17},{2,18},{3,19},{4,20},{5,21},{6,22},{7,23},{8,24},{9,... | collective-permute-start | bytes 393224 | tf_op jit(solution)/shard_map/ppermute | solution.py:162
  7.2 5.6 %collective-permute-start.8 = (f32[64,512]{1,0:T(8,128)S(1)}, f32[64,512]{1,0:T(8,128)S(1)}, u32[]{:S(2)}, u32[]{:S(2)}) collective-permute-start(f32[64,512]{1,0:T(8,128)S(1)} %constant_dynamic-slice_fusion.1), channel_id=1, source_target_pairs={{0,2},{1,3},{2,0},{3,1},{4,6},{5,7},{6,4},{7,5},{8,10},{9,11},{10,... | collective-permute-start | bytes 393224 | tf_op jit(solution)/shard_map/ppermute | solution.py:162
  10.9 4.3 %collective-permute-start.2 = (f32[32,512]{1,0:T(8,128)S(1)}, f32[32,512]{1,0:T(8,128)S(1)}, u32[]{:S(2)}, u32[]{:S(2)}) collective-permute-start(f32[32,512]{1,0:T(8,128)S(1)} %constant_dynamic-slice_fusion.3), channel_id=1, source_target_pairs={{0,2},{1,3},{2,0},{3,1},{4,6},{5,7},{6,4},{7,5},{8,10},{9,11},{10,... | collective-permute-start | bytes 196616 | tf_op jit(solution)/shard_map/ppermute | solution.py:162
  12.8 5.0 %collective-permute-start.9 = (f32[32,512]{1,0:T(8,128)S(1)}, f32[32,512]{1,0:T(8,128)S(1)}, u32[]{:S(2)}, u32[]{:S(2)}) collective-permute-start(f32[32,512]{1,0:T(8,128)S(1)} %constant_dynamic-slice_fusion), channel_id=1, source_target_pairs={{0,4},{1,5},{2,6},{3,7},{4,0},{5,1},{6,2},{7,3},{8,12},{9,13},{10,... | collective-permute-start | bytes 196616 | tf_op jit(solution)/shard_map/ppermute | solution.py:162
  15.3 5.1 %collective-permute-start.3 = (f32[32,512]{1,0:T(8,128)S(1)}, f32[32,512]{1,0:T(8,128)S(1)}, u32[]{:S(2)}, u32[]{:S(2)}) collective-permute-start(f32[32,512]{1,0:T(8,128)S(1)} %dynamic-slice_add_fusion.5), channel_id=1, source_target_pairs={{0,4},{1,5},{2,6},{3,7},{4,0},{5,1},{6,2},{7,3},{8,12},{9,13},{10,... | collective-permute-start | bytes 196616 | tf_op jit(solution)/shard_map/ppermute | solution.py:162
  17.8 6.6 %collective-permute-start.10 = (f32[32,512]{1,0:T(8,128)S(1)}, f32[32,512]{1,0:T(8,128)S(1)}, u32[]{:S(2)}, u32[]{:S(2)}) collective-permute-start(f32[32,512]{1,0:T(8,128)S(1)} %dynamic-slice_add_fusion.4), channel_id=1, source_target_pairs={{0,8},{1,9},{2,10},{3,11},{4,12},{5,13},{6,14},{7,15},{8,0},{9,1},... | collective-permute-start | bytes 196616 | tf_op jit(solution)/shard_map/ppermute | solution.py:162
  20.4 5.2 %collective-permute-start.4 = (f32[32,512]{1,0:T(8,128)S(1)}, f32[32,512]{1,0:T(8,128)S(1)}, u32[]{:S(2)}, u32[]{:S(2)}) collective-permute-start(f32[32,512]{1,0:T(8,128)S(1)} %add.72), channel_id=1, source_target_pairs={{0,8},{1,9},{2,10},{3,11},{4,12},{5,13},{6,14},{7,15},{8,0},{9,1},... | collective-permute-start | bytes 196616 | tf_op jit(solution)/shard_map/ppermute | solution.py:162
  24.5 4.3 %collective-permute-start.11 = (f32[32,512]{1,0:T(8,128)S(1)}, f32[32,512]{1,0:T(8,128)S(1)}, u32[]{:S(2)}, u32[]{:S(2)}) collective-permute-start(f32[32,512]{1,0:T(8,128)S(1)} %add.81), channel_id=1, source_target_pairs={{0,4},{1,5},{2,6},{3,7},{4,0},{5,1},{6,2},{7,3},{8,12},{9,13},{10,... | collective-permute-start | bytes 196616 | tf_op jit(solution)/shard_map/ppermute | solution.py:162
  25.7 4.3 %collective-permute-start.5 = (f32[32,512]{1,0:T(8,128)S(1)}, f32[32,512]{1,0:T(8,128)S(1)}, u32[]{:S(2)}, u32[]{:S(2)}) collective-permute-start(f32[32,512]{1,0:T(8,128)S(1)} %add.73), channel_id=1, source_target_pairs={{0,2},{1,3},{2,0},{3,1},{4,6},{5,7},{6,4},{7,5},{8,10},{9,11},{10,... | collective-permute-start | bytes 196616 | tf_op jit(solution)/shard_map/ppermute | solution.py:162
  28.8 5.0 %collective-permute-start.12 = (f32[64,512]{1,0:T(8,128)S(1)}, f32[64,512]{1,0:T(8,128)S(1)}, u32[]{:S(2)}, u32[]{:S(2)}) collective-permute-start(f32[64,512]{1,0:T(8,128)S(1)} %pad_maximum_fusion.1.refs_2_), channel_id=1, source_target_pairs={{0,2},{1,3},{2,0},{3,1},{4,6},{5,7},{6,4},{7,5},{8,10},{9,11},{10,... | collective-permute-start | bytes 393224 | tf_op jit(solution)/shard_map/ppermute | solution.py:162
  30.0 5.0 %collective-permute-start.6 = (f32[64,512]{1,0:T(8,128)S(1)}, f32[64,512]{1,0:T(8,128)S(1)}, u32[]{:S(2)}, u32[]{:S(2)}) collective-permute-start(f32[64,512]{1,0:T(8,128)S(1)} %pad_maximum_fusion.refs_0_), channel_id=1, source_target_pairs={{0,16},{1,17},{2,18},{3,19},{4,20},{5,21},{6,22},{7,23},{8,24},{9,... | collective-permute-start | bytes 393224 | tf_op jit(solution)/shard_map/ppermute | solution.py:162
  31.7 3.5 %collective-permute-start.15 = (f32[64,512]{1,0:T(8,128)S(1)}, f32[64,512]{1,0:T(8,128)S(1)}, u32[]{:S(2)}, u32[]{:S(2)}) collective-permute-start(f32[64,512]{1,0:T(8,128)S(1)} %pad_maximum_fusion.1.refs_2_), channel_id=1, source_target_pairs={{0,1},{1,0},{2,3},{3,2},{4,5},{5,4},{6,7},{7,6},{8,9},{9,8},{10,11... | collective-permute-start | bytes 393224 | tf_op jit(solution)/shard_map/ppermute | solution.py:162
  31.7 3.5 %collective-permute-start.13 = (f32[64,512]{1,0:T(8,128)S(1)}, f32[64,512]{1,0:T(8,128)S(1)}, u32[]{:S(2)}, u32[]{:S(2)}) collective-permute-start(f32[64,512]{1,0:T(8,128)S(1)} %pad_maximum_fusion.refs_0_), channel_id=1, source_target_pairs={{0,1},{1,0},{2,3},{3,2},{4,5},{5,4},{6,7},{7,6},{8,9},{9,8},{10,11... | collective-permute-start | bytes 393224 | tf_op jit(solution)/shard_map/ppermute | solution.py:162
  33.9 1.3 %collective-permute-start.16 = (f32[64,512]{1,0:T(8,128)S(1)}, f32[64,512]{1,0:T(8,128)S(1)}, u32[]{:S(2)}, u32[]{:S(2)}) collective-permute-start(f32[64,512]{1,0:T(8,128)S(1)} %collective-permute-done.12.refs_3_), channel_id=1, source_target_pairs={{0,1},{1,0},{2,3},{3,2},{4,5},{5,4},{6,7},{7,6},{8,9},{9,8},{10,11... | collective-permute-start | bytes 393224 | tf_op jit(solution)/shard_map/ppermute | solution.py:162
  35.1 1.3 %collective-permute-start.14 = (f32[64,512]{1,0:T(8,128)S(1)}, f32[64,512]{1,0:T(8,128)S(1)}, u32[]{:S(2)}, u32[]{:S(2)}) collective-permute-start(f32[64,512]{1,0:T(8,128)S(1)} %collective-permute-done.6.refs_1_), channel_id=1, source_target_pairs={{0,1},{1,0},{2,3},{3,2},{4,5},{5,4},{6,7},{7,6},{8,9},{9,8},{10,11... | collective-permute-start | bytes 393224 | tf_op jit(solution)/shard_map/ppermute | solution.py:162
